TPU v7x, 32 devices: a whole 2x2x4 slice. The times are simulated.
32 devices in a mesh: dp: 4 (over z), group: 8 (over y, x, core).
Axes of the slice: x: 2, y: 2, z: 4, core: 2. Of those that a mesh axis runs over, the one named last changes fastest.
Arguments:
- images: bfloat16 [64, 8, 8, 4096], P('dp', None, None, 'group'), may hold values from -6 to 6
- cotangent: bfloat16 [64, 8, 8, 4096], P('dp', None, None, 'group'), may hold values from -6 to 6
- conv_weight: bfloat16 [2, 576, 4096], P(None, 'dp', 'group'), may hold values from -0.25 to 0.25
- mix_weight: bfloat16 [2, 4096, 4096], P(None, 'group', 'dp'), may hold values from -0.09375 to 0.09375
Outputs:
- features_out: bfloat16 [64, 8, 8, 4096], P('dp', None, None, 'group')
- grad_images: bfloat16 [64, 8, 8, 4096], P('dp', None, None, 'group')
- grad_conv: float32 [2, 576, 4096], P(None, 'dp', 'group')
- grad_mix: float32 [2, 4096, 4096], P(None, 'group', 'dp')
All inputs are finite; a program needn't handle non-finite values.
Results may differ from a plain program's by a relative error of at most 0.022.
Values may be sent and summed in bfloat16 or wider, within the bound.
No kernel may reach another device: no remote copies, remote signals or barrier semaphores. Data moves between devices by JAX's collectives and lax.ppermute only.
A program may use at most 192 MiB of HBM per device.

v0:
```python
import math

import jax
import jax.numpy as jnp
from jax import lax
from jax.sharding import PartitionSpec as P

GW = 64


def make_patches(field):
    side_cells = field.shape[1]
    padded = jnp.pad(field, ((0, 0), (1, 1), (1, 1), (0, 0)))
    tap_list = [
        padded[:, row_shift : row_shift + side_cells, col_shift : col_shift + side_cells, :]
        for row_shift in range(3)
        for col_shift in range(3)
    ]
    return jnp.stack(tap_list, axis=3).reshape(-1, 9, field.shape[3])


def fold_patches(pieces, batch_size, side_cells):
    pieces = pieces.reshape(batch_size, side_cells, side_cells, 9, pieces.shape[2])
    summed = jnp.zeros((batch_size, side_cells + 2, side_cells + 2, pieces.shape[4]), jnp.float32)
    for tap_index in range(9):
        row_shift = tap_index // 3
        col_shift = tap_index % 3
        summed = summed + jnp.pad(
            pieces[:, :, :, tap_index, :],
            ((0, 0), (row_shift, 2 - row_shift), (col_shift, 2 - col_shift), (0, 0)),
        )
    return summed[:, 1 : side_cells + 1, 1 : side_cells + 1, :]


def silu_slope(value):
    sigmoid_v = jax.nn.sigmoid(value)
    return sigmoid_v * (1.0 + value * (1.0 - sigmoid_v))


def per_device(images, cotangent, conv_weight, mix_weight):
    batch_size, side_cells, _, local_width = images.shape
    local_groups = local_width // GW
    row_count = batch_size * side_cells * side_cells
    layer_count = conv_weight.shape[0]
    grad_scale = 1.0 / math.sqrt(row_count * lax.axis_size("dp"))
    fetched = [
        (
            lax.all_gather(conv_weight[layer], "dp", axis=0, tiled=True),
            lax.all_gather(mix_weight[layer], "dp", axis=1, tiled=True),
        )
        for layer in range(layer_count)
    ]
    current = images
    saved = []
    for layer in range(layer_count):
        conv_full, mix_full = fetched[layer]
        tap_weights = conv_full.reshape(9 * GW, local_groups, GW).transpose(1, 0, 2)
        flat = make_patches(current).reshape(row_count, 9, local_groups, GW)
        patches = flat.transpose(0, 2, 1, 3).reshape(row_count, local_groups, 9 * GW)
        pre_act = jnp.einsum(
            "pgk,gko->pgo", patches, tap_weights, preferred_element_type=jnp.float32
        ).reshape(row_count, local_width)
        hidden = jax.nn.silu(pre_act).astype(jnp.bfloat16)
        mixed = lax.psum_scatter(
            jnp.dot(hidden, mix_full, preferred_element_type=jnp.float32).astype(jnp.bfloat16),
            "group",
            scatter_dimension=1,
            tiled=True,
        ).astype(jnp.float32)
        saved.append((patches, pre_act, hidden, tap_weights, mix_full))
        current = (
            (current.reshape(row_count, local_width).astype(jnp.float32) + mixed)
            .astype(jnp.bfloat16)
            .reshape(images.shape)
        )
    gradient = cotangent
    conv_grads = []
    mix_grads = []
    for layer in reversed(range(layer_count)):
        patches, pre_act, hidden, tap_weights, mix_full = saved[layer]
        flat_grad = gradient.reshape(row_count, local_width)
        grad_wide = lax.all_gather(flat_grad, "group", axis=1, tiled=True)
        mix_term = lax.dot_general(
            hidden, grad_wide, (((0,), (0,)), ((), ())), preferred_element_type=jnp.float32
        )
        grad_hidden = lax.dot_general(
            grad_wide, mix_full, (((1,), (1,)), ((), ())), preferred_element_type=jnp.float32
        )
        grad_pre = (
            (grad_hidden * silu_slope(pre_act))
            .astype(jnp.bfloat16)
            .reshape(row_count, local_groups, GW)
        )
        conv_term = jnp.einsum(
            "pgk,pgo->gko", patches, grad_pre, preferred_element_type=jnp.float32
        )
        conv_term = conv_term.transpose(1, 0, 2).reshape(9 * GW, local_width)
        patch_grad = jnp.einsum(
            "pgo,gko->pgk", grad_pre, tap_weights, preferred_element_type=jnp.float32
        )
        patch_grad = (
            patch_grad.reshape(row_count, local_groups, 9, GW)
            .transpose(0, 2, 1, 3)
            .reshape(row_count, 9, local_width)
        )
        field_grad = fold_patches(patch_grad, batch_size, side_cells)
        conv_summed, mix_summed = (
            lax.psum_scatter(
                conv_term.astype(jnp.bfloat16), "dp", scatter_dimension=0, tiled=True
            ).astype(jnp.float32),
            lax.psum_scatter(
                mix_term.astype(jnp.bfloat16), "dp", scatter_dimension=1, tiled=True
            ).astype(jnp.float32),
        )
        conv_grads.insert(0, conv_summed * grad_scale)
        mix_grads.insert(0, mix_summed * grad_scale)
        gradient = (gradient.astype(jnp.float32) + field_grad).astype(jnp.bfloat16)
    return (current, gradient, jnp.stack(conv_grads), jnp.stack(mix_grads))


def solution(mesh):
    return jax.shard_map(
        per_device,
        mesh=mesh,
        in_specs=(
            P("dp", None, None, "group"),
            P("dp", None, None, "group"),
            P(None, "dp", "group"),
            P(None, "group", "dp"),
        ),
        out_specs=(
            P("dp", None, None, "group"),
            P("dp", None, None, "group"),
            P(None, "dp", "group"),
            P(None, "group", "dp"),
        ),
        check_vma=False,
    )
```

profile of v0, /device:TPU:0, one launch (start us, length us, event | category | flops | bytes accessed | tf_op | source)
XLA Modules:
  0.0 776.8 jit_solution(8822047516559328924)
XLA Ops:
  10.4 21.9 %all-gather = bf16[1,576,512]{2,1,0:T(8,128)(2,1)S(1)} all-gather(bf16[1,144,512]{2,1,0:T(8,128)(2,1)S(1)} %get-tuple-element.40), channel_id=2, replica_groups=mesh['dp'=4,'group'=8] {'dp'}, dimensions={1}, use_global_device_ids=true | all-gather | bytes 737280 | tf_op jit(solution)/shard_map/all_gather | solution.py:48
  41.6 3.9 stack.79
  45.5 3.9 stack.80
  49.4 3.9 stack.81
  53.3 3.9 stack.83
  57.2 3.9 stack.84
  61.1 3.9 stack.85
  67.0 3.2 constant_dynamic-update-slice_fusion.8
  87.3 20.5 %copy.24 = bf16[1024,8,9,64]{0,3,2,1:T(8,128)(2,1)} copy(bf16[1024,8,9,64]{3,1,0,2:T(8,128)(2,1)} %bitcast.1) | data formatting | bytes 18874368 | tf_op jit(solution)/shard_map/transpose | solution.py:59
  107.8 5.6 fusion.35
  114.0 9.3 %convolution_convert_fusion.1 = bf16[1024,4096]{1,0:T(8,128)(2,1)} fusion(bf16[1024,512]{0,1:T(8,128)(2,1)S(1)} %fusion.22, bf16[1,512,4096]{2,1,0:T(8,128)(2,1)} %all-gather.13.cloned.1.call-done), kind=kOutput, calls=%fused_computation.1 | convolution fusion | flops 4299161600 | bytes 13631488 | tf_op jit(solution)/shard_map/dot_general | solution.py:65
  124.7 16.4 %all-gather.2 = bf16[1,576,512]{2,1,0:T(8,128)(2,1)S(1)} all-gather(bf16[1,144,512]{2,1,0:T(8,128)(2,1)S(1)} %get-tuple-element.41), channel_id=4, replica_groups=mesh['dp'=4,'group'=8] {'dp'}, dimensions={1}, use_global_device_ids=true | all-gather | bytes 737280 | tf_op jit(solution)/shard_map/all_gather | solution.py:48
  142.2 52.9 %reduce-scatter.7.cloned.1.call-done = bf16[1024,512]{1,0:T(8,128)(2,1)} async-done(((bf16[1024,4096]{1,0:T(8,128)(2,1)}), bf16[1024,512]{1,0:T(8,128)(2,1)}) %reduce-scatter.7.cloned.1.call-update) | async-done | bytes 1048592 | tf_op jit(solution)/shard_map/reduce_scatter | solution.py:64
  198.2 3.5 copy.27
  201.7 3.6 pad_slice_fusion
  205.3 3.9 stack.96
  209.2 3.9 stack.89
  213.1 3.9 stack.90
  217.0 3.9 stack.91
  220.9 3.9 stack.93
  224.8 3.9 stack.94
  228.7 3.9 stack.95
  232.6 3.9 stack.88
  236.5 3.2 constant_dynamic-update-slice_fusion.17
  257.7 20.8 %copy.28 = bf16[1024,8,9,64]{0,3,2,1:T(8,128)(2,1)} copy(bf16[1024,8,9,64]{3,1,0,2:T(8,128)(2,1)} %bitcast.11) | data formatting | bytes 18874368 | tf_op jit(solution)/shard_map/transpose | solution.py:59
  278.5 7.1 fusion.36
  285.7 48.3 %all-gather.9.cloned.1.call-done = bf16[1024,4096]{1,0:T(8,128)(2,1)} async-done(((bf16[1024,512]{1,0:T(8,128)(2,1)}), bf16[1024,4096]{1,0:T(8,128)(2,1)}) %all-gather.9.cloned.1.call-update) | async-done | bytes 8388624 | tf_op jit(solution)/shard_map/all_gather | solution.py:82
  333.9 10.1 %fusion.18 = bf16[1024,512]{0,1:T(8,128)(2,1)S(1)} fusion(f32[8,1024,64]{1,2,0:T(8,128)} %fusion.36, bf16[1024,4096]{1,0:T(8,128)(2,1)} %all-gather.9.cloned.1.call-done, bf16[1,512,4096]{2,1,0:T(8,128)(2,1)} %all-gather.15.cloned.1.call-done), kind=kOutput, calls=%fused_computation.75 | convolution fusion | flops 4299685888 | bytes 15728640 | tf_op jit(solution)/shard_map/dot_general | solution.py:86
  344.1 7.8 %fusion.33 = f32[8,1024,576]{1,2,0:T(8,128)} fusion(bf16[1024,8,64]{0,2,1:T(8,128)(2,1)S(1)} %bitcast.225, bf16[8,576,64]{1,2,0:T(8,128)(2,1)S(1)} %bitcast.219), kind=kOutput, calls=%fused_computation.115 | convolution fusion | flops 603979776 | bytes 20512768 | tf_op jit(solution)/shard_map/pgo,gko->pgk/dot_general | solution.py:98
  351.9 26.0 %copy.30 = f32[1024,8,9,64]{3,1,0,2:T(8,128)} copy(f32[1024,8,9,64]{0,3,2,1:T(8,128)} %bitcast.209) | data formatting | bytes 37748736 | tf_op jit(solution)/shard_map/reshape | solution.py:102
  377.9 31.7 %reshape_reshape.8 = f32[16,8,8,9,512]{4,2,1,0,3:T(8,128)} reshape(f32[1024,9,8,64]{3,2,0,1:T(8,128)} %bitcast.206) | data formatting | bytes 37748736 | tf_op jit(solution)/shard_map/reshape;reshape | solution.py:23
  409.6 11.3 %slice_bitcast_fusion.17 = (f32[16,8,8,512]{3,2,1,0:T(8,128)S(1)}, f32[16,8,8,512]{3,2,1,0:T(8,128)S(1)}, f32[16,8,8,512]{3,2,1,0:T(8,128)}, f32[16,8,8,512]{3,2...) fusion(f32[16,8,8,9,512]{4,2,1,0,3:T(8,128)} %reshape_reshape.8), kind=kLoop, calls=%fused_computation.62 | loop fusion | bytes 37748736 | tf_op jit(solution)/shard_map/squeeze | solution.py:29
  422.5 7.1 fusion.9
  429.6 7.6 convolution_convert_fusion.4
  442.7 10.2 %convolution_convert_fusion.2 = bf16[512,4096]{1,0:T(8,128)(2,1)} fusion(bf16[1024,512]{0,1:T(8,128)(2,1)} %fusion.14, bf16[1024,4096]{1,0:T(8,128)(2,1)} %all-gather.9.cloned.1.call-done), kind=kOutput, calls=%fused_computation.2 | convolution fusion | flops 4297064448 | bytes 13631488 | tf_op jit(solution)/shard_map/dot_general | solution.py:83
  453.3 10.3 %convolution_convert_fusion = bf16[1024,4096]{1,0:T(8,128)(2,1)} fusion(bf16[1024,512]{0,1:T(8,128)(2,1)} %fusion.14, bf16[1,512,4096]{2,1,0:T(8,128)(2,1)} %all-gather.15.cloned.1.call-done), kind=kOutput, calls=%fused_computation | convolution fusion | flops 4299161600 | bytes 13631488 | tf_op jit(solution)/shard_map/dot_general | solution.py:65
  463.7 22.0 %all-gather.11.cloned.1.call-done = bf16[1024,4096]{1,0:T(8,128)(2,1)} async-done(((bf16[1024,512]{1,0:T(8,128)(2,1)}), bf16[1024,4096]{1,0:T(8,128)(2,1)}) %all-gather.11.cloned.1.call-update) | async-done | bytes 8388624 | tf_op jit(solution)/shard_map/all_gather | solution.py:82
  485.7 9.4 %fusion.26 = bf16[1024,512]{0,1:T(8,128)(2,1)S(1)} fusion(f32[8,1024,64]{1,2,0:T(8,128)S(1)} %fusion.35, bf16[1024,4096]{1,0:T(8,128)(2,1)} %all-gather.11.cloned.1.call-done, bf16[1,512,4096]{2,1,0:T(8,128)(2,1)} %all-gather.13.cloned.1.call-done), kind=kOutput, calls=%fused_computation.86 | convolution fusion | flops 4299685888 | bytes 15728640 | tf_op jit(solution)/shard_map/dot_general | solution.py:86
  495.1 7.0 convolution_convert_fusion.5
  503.5 9.5 %convolution_convert_fusion.3 = bf16[512,4096]{1,0:T(8,128)(2,1)} fusion(bf16[1024,512]{0,1:T(8,128)(2,1)S(1)} %copy-done.22, bf16[1024,4096]{1,0:T(8,128)(2,1)} %all-gather.11.cloned.1.call-done), kind=kOutput, calls=%fused_computation.3 | convolution fusion | flops 4297064448 | bytes 13631488 | tf_op jit(solution)/shard_map/dot_general | solution.py:83
  514.0 74.7 %reduce-scatter.17.cloned.1.call-done = bf16[512,1024]{1,0:T(8,128)(2,1)} async-done(((bf16[512,4096]{1,0:T(8,128)(2,1)}), bf16[512,1024]{1,0:T(8,128)(2,1)}) %reduce-scatter.17.cloned.1.call-update) | async-done | bytes 1048592 | tf_op jit(solution)/shard_map/reduce_scatter | solution.py:111
  590.2 73.8 %reduce-scatter.9.cloned.1.call-done = bf16[1024,512]{1,0:T(8,128)(2,1)} async-done(((bf16[1024,4096]{1,0:T(8,128)(2,1)}), bf16[1024,512]{1,0:T(8,128)(2,1)}) %reduce-scatter.9.cloned.1.call-update) | async-done | bytes 1048592 | tf_op jit(solution)/shard_map/reduce_scatter | solution.py:64
  666.6 7.9 %fusion.34 = f32[8,1024,576]{1,2,0:T(8,128)} fusion(bf16[1024,8,64]{0,2,1:T(8,128)(2,1)S(1)} %bitcast.224, bf16[8,576,64]{1,2,0:T(8,128)(2,1)S(1)} %bitcast.217), kind=kOutput, calls=%fused_computation.116 | convolution fusion | flops 603979776 | bytes 20512768 | tf_op jit(solution)/shard_map/pgo,gko->pgk/dot_general | solution.py:98
  674.5 26.2 %copy.31 = f32[1024,8,9,64]{3,1,0,2:T(8,128)} copy(f32[1024,8,9,64]{0,3,2,1:T(8,128)} %bitcast.208) | data formatting | bytes 37748736 | tf_op jit(solution)/shard_map/reshape | solution.py:102
  700.7 31.8 %reshape_reshape.9 = f32[16,8,8,9,512]{4,2,1,0,3:T(8,128)} reshape(f32[1024,9,8,64]{3,2,0,1:T(8,128)} %bitcast.207) | data formatting | bytes 37748736 | tf_op jit(solution)/shard_map/reshape;reshape | solution.py:23
  732.4 11.3 %slice_bitcast_fusion.8 = (f32[16,8,8,512]{3,2,1,0:T(8,128)S(1)}, f32[16,8,8,512]{3,2,1,0:T(8,128)S(1)}, f32[16,8,8,512]{3,2,1,0:T(8,128)}, f32[16,8,8,512]{3,2,...) fusion(f32[16,8,8,9,512]{4,2,1,0,3:T(8,128)} %reshape_reshape.9), kind=kLoop, calls=%fused_computation.45 | loop fusion | bytes 37748736 | tf_op jit(solution)/shard_map/squeeze | solution.py:29
  745.3 7.1 fusion.7
  754.2 11.5 %reduce-scatter.15.cloned.1.call-done = bf16[512,1024]{1,0:T(8,128)(2,1)} async-done(((bf16[512,4096]{1,0:T(8,128)(2,1)}), bf16[512,1024]{1,0:T(8,128)(2,1)}) %reduce-scatter.15.cloned.1.call-update) | async-done | bytes 1048592 | tf_op jit(solution)/shard_map/reduce_scatter | solution.py:111
  (117 shorter events, 76.6 us)
Async XLA Ops:
  7.2 3.2 copy-start.26
  7.2 106.8 %all-gather.13.cloned.1.call-start = ((), (), s32[]{:S(2)}) async-start(), calls=%async_computation.14 | async-start | bytes 5242880 | tf_op jit(solution)/shard_map/all_gather | solution.py:49
  10.3 23.1 %copy-start = (bf16[16,8,8,512]{3,2,1,0:T(8,128)(2,1)S(1)}, bf16[16,8,8,512]{3,2,1,0:T(8,128)(2,1)}, u32[]{:S(2)}) copy-start(bf16[16,8,8,512]{3,2,1,0:T(8,128)(2,1)} %param.4) | copy-start | bytes 3145732
  10.4 184.7 %reduce-scatter.7.cloned.1.call-start = ((), (), s32[]{:S(2)}) async-start(), calls=%async_computation.6 | async-start | bytes 9437184 | tf_op jit(solution)/shard_map/reduce_scatter | solution.py:64
  67.0 3.2 copy-start.15
  70.3 2.4 copy-start.13
  72.6 2.4 copy-start.11
  75.0 2.4 copy-start.4
  77.3 2.3 copy-start.9
  79.7 2.3 copy-start.7
  82.0 2.3 copy-start.5
  87.3 20.5 %copy-start.17 = (bf16[1,576,512]{1,2,0:T(8,128)(2,1)S(1)}, bf16[1,576,512]{1,2,0:T(8,128)(2,1)}, u32[]{:S(2)}) copy-start(bf16[1,576,512]{1,2,0:T(8,128)(2,1)} %copy.25) | copy-start | bytes 1769476
  114.0 9.3 %copy-start.21 = (bf16[1024,512]{0,1:T(8,128)(2,1)}, bf16[1024,512]{0,1:T(8,128)(2,1)S(1)}, u32[]{:S(2)}) copy-start(bf16[1024,512]{0,1:T(8,128)(2,1)S(1)} %fusion.22) | copy-start | bytes 3145732
  123.3 162.4 %all-gather.15.cloned.1.call-start = ((), (), s32[]{:S(2)}) async-start(), calls=%async_computation.15 | async-start | bytes 5242880 | tf_op jit(solution)/shard_map/all_gather | solution.py:49
  124.0 209.9 %all-gather.9.cloned.1.call-start = ((), (), s32[]{:S(2)}) async-start(), calls=%async_computation.8 | async-start | bytes 9437184 | tf_op jit(solution)/shard_map/all_gather | solution.py:82
  124.6 361.1 %all-gather.11.cloned.1.call-start = ((), (), s32[]{:S(2)}) async-start(), calls=%async_computation.9 | async-start | bytes 9437184 | tf_op jit(solution)/shard_map/all_gather | solution.py:82
  236.5 3.2 copy-start.16
  239.7 2.4 copy-start.14
  242.1 2.3 copy-start.12
  244.4 2.4 copy-start.3
  246.8 2.3 copy-start.10
  249.1 2.4 copy-start.8
  251.5 2.4 copy-start.6
  253.9 2.3 copy-start.2
  333.9 10.1 %copy-start.19 = (bf16[1,576,512]{1,2,0:T(8,128)(2,1)S(1)}, bf16[1,576,512]{1,2,0:T(8,128)(2,1)}, u32[]{:S(2)}) copy-start(bf16[1,576,512]{1,2,0:T(8,128)(2,1)} %copy.29) | copy-start | bytes 1769476
  344.0 7.8 %copy-start.25 = (bf16[1024,512]{0,1:T(8,128)(2,1)}, bf16[1024,512]{0,1:T(8,128)(2,1)S(1)}, u32[]{:S(2)}) copy-start(bf16[1024,512]{0,1:T(8,128)(2,1)S(1)} %fusion.18) | copy-start | bytes 3145732
  420.9 1.6 copy-start.20
  429.6 83.5 %reduce-scatter.13.cloned.1.call-start = ((), (), s32[]{:S(2)}) async-start(), calls=%async_computation.11 | async-start | bytes 737280 | tf_op jit(solution)/shard_map/reduce_scatter | solution.py:108
  442.7 146.0 %reduce-scatter.17.cloned.1.call-start = ((), (), s32[]{:S(2)}) async-start(), calls=%async_computation.13 | async-start | bytes 5242880 | tf_op jit(solution)/shard_map/reduce_scatter | solution.py:111
  453.0 210.9 %reduce-scatter.9.cloned.1.call-start = ((), (), s32[]{:S(2)}) async-start(), calls=%async_computation.7 | async-start | bytes 9437184 | tf_op jit(solution)/shard_map/reduce_scatter | solution.py:64
  463.6 288.8 %reduce-scatter.11.cloned.1.call-start = ((), (), s32[]{:S(2)}) async-start(), calls=%async_computation.10 | async-start | bytes 737280 | tf_op jit(solution)/shard_map/reduce_scatter | solution.py:108
  495.1 7.0 copy-start.23
  495.1 8.4 %copy-start.22 = (bf16[1024,512]{0,1:T(8,128)(2,1)S(1)}, bf16[1024,512]{0,1:T(8,128)(2,1)}, u32[]{:S(2)}) copy-start(bf16[1024,512]{0,1:T(8,128)(2,1)} %copy-done.21) | copy-start | bytes 3145732
  503.2 262.5 %reduce-scatter.15.cloned.1.call-start = ((), (), s32[]{:S(2)}) async-start(), calls=%async_computation.12 | async-start | bytes 5242880 | tf_op jit(solution)/shard_map/reduce_scatter | solution.py:111
  664.0 2.6 copy-start.18
  664.0 2.6 copy-start.24
  743.7 1.6 copy-start.1
Sparse Core Ops, SparseCore 0:
  10.5 85.6 all-gather.12
  123.4 71.6 reduce-scatter.6
  196.7 80.7 all-gather.14
  279.4 54.4 all-gather.8
  429.7 55.9 all-gather.10
  488.5 21.9 reduce-scatter.12
  513.5 75.1 reduce-scatter.16
  592.1 71.7 reduce-scatter.8
  666.3 21.8 reduce-scatter.10
  690.5 75.1 reduce-scatter.14
where the time goes:
time: 791 us; the launch traced here: 777 us
  local copies, waits for them, and re-layouts  303 us (38%)
  waiting for transfers between devices  285 us (36%)
  matrix products  102 us (13%)
  blocking collectives  38.4 us (5%)
  other arithmetic  33.4 us (4%)
  between operations  14.9 us (2%)
    reduce_scatter x2, waiting for transfers between devices, per_device(): lax.psum_scatter(jnp.dot(hidden, mix_full, preferred_element_type=jnp.flo...  127 us
    reduce_scatter x2, waiting for transfers between devices, per_device(): lax.psum_scatter(mix_term.astype(jnp.bfloat16), 'dp', scatter_dimension=1...  86.2 us
    all_gather x2, waiting for transfers between devices, per_device(): grad_wide = lax.all_gather(flat_grad, 'group', axis=1, tiled=True)  70.3 us
    another operation x20, local copies, waits for them, and re-layouts, make_patches(): return jnp.stack(tap_list, axis=3).reshape(-1, 9, field.shape[3])  68 us
    another operation x2, local copies, waits for them, and re-layouts, fold_patches(): pieces.reshape(batch_size, side_cells, side_cells, 9, pieces.shape[2])  63.5 us
    reshape x2, local copies, waits for them, and re-layouts, per_device(): patch_grad.reshape(row_count, local_groups, 9, GW).transpose(0, 2, 1, 3)  52.2 us
    transpose x2, local copies, waits for them, and re-layouts, per_device(): flat.transpose(0, 2, 1, 3).reshape(row_count, local_groups, 9 * GW)  41.3 us
    unnamed x70, local copies, waits for them, and re-layouts  38.5 us
  transfers between devices with their start and end apart: 10, of which 6 were waited for; matrix products, arithmetic and copies ran while one was open for 41% of the time, Pallas kernels for 0%

commit v1 on v0

v1 whole, which is shorter than its diff:
```python
import functools
import math

import jax
import jax.numpy as jnp
from jax import lax
from jax.experimental import pallas as pl
from jax.experimental.pallas import tpu as pltpu
from jax.sharding import PartitionSpec as P

GW = 64
TAPS = 9
HALF = 256
BF = jnp.bfloat16
F32 = jnp.float32
VMEM_LIMIT = 40 * 1024 * 1024

UP = [(0, 1), (1, 2), (2, 3)]
DOWN = [(3, 2), (2, 1), (1, 0)]
ACROSS_CORE = [(i, i ^ 1) for i in range(8)]
ACROSS_X = [(i, i ^ 2) for i in range(8)]
ACROSS_Y = [(i, i ^ 4) for i in range(8)]


def dot(a, b):
    return jnp.dot(a, b, preferred_element_type=F32)


def dot_nt(a, b):
    return lax.dot_general(a, b, (((1,), (1,)), ((), ())), preferred_element_type=F32)


def call(kernel, out_shape, flops, nbytes, **kw):
    return pl.pallas_call(
        kernel,
        out_shape=out_shape,
        compiler_params=pltpu.CompilerParams(vmem_limit_bytes=VMEM_LIMIT),
        cost_estimate=pl.CostEstimate(flops=flops, bytes_accessed=nbytes, transcendentals=0),
        **kw,
    )


def block_mask():
    rows = lax.broadcasted_iota(jnp.int32, (HALF, HALF), 0) // GW
    cols = lax.broadcasted_iota(jnp.int32, (HALF, HALF), 1) // GW
    return rows == cols


def spread_taps(w_ref, wide_ref, by_rows):
    mask = block_mask()
    for tap in range(TAPS):
        slab = w_ref[tap * GW : (tap + 1) * GW, :]
        square = jnp.concatenate([slab] * (HALF // GW), axis=0)
        square = jnp.where(mask, square, jnp.zeros_like(square))
        if by_rows:
            wide_ref[tap * HALF : (tap + 1) * HALF, :] = square
        else:
            wide_ref[:, tap * HALF : (tap + 1) * HALF] = square


def pad_field(value, pad_ref):
    side = value.shape[0]
    pad_ref[...] = jnp.zeros_like(pad_ref)
    pad_ref[1 : side + 1, 1 : side + 1] = value


def conv_kernel(x_ref, w_ref, hidden_ref, hidden_t_ref, slope_ref, pad_ref, wide_ref):
    side, _, images, _ = x_ref.shape
    pad_field(x_ref[...], pad_ref)
    spread_taps(w_ref, wide_ref, True)
    step = 2
    rows = step * side * images
    for part in range(side // step):
        top = part * step
        patches = jnp.concatenate(
            [
                pad_ref[top + a : top + a + step, b : b + side].reshape(rows, HALF)
                for a in range(3)
                for b in range(3)
            ],
            axis=1,
        )
        pre = dot(patches, wide_ref[...])
        sig = jax.nn.sigmoid(pre)
        hidden = (pre * sig).astype(BF)
        here = slice(part * rows, (part + 1) * rows)
        hidden_ref[here, :] = hidden
        hidden_t_ref[:, here] = hidden.T
        slope_ref[here, :] = sig * (1.0 + pre * (1.0 - sig))


def conv_forward(x, w):
    side, _, images, _ = x.shape
    rows = side * side * images
    return call(
        conv_kernel,
        (
            jax.ShapeDtypeStruct((rows, HALF), BF),
            jax.ShapeDtypeStruct((HALF, rows), BF),
            jax.ShapeDtypeStruct((rows, HALF), F32),
        ),
        2 * rows * HALF * HALF * TAPS,
        rows * HALF * 10,
        scratch_shapes=[
            pltpu.VMEM((side + 2, side + 2, images, HALF), BF),
            pltpu.VMEM((TAPS * HALF, HALF), BF),
        ],
    )(x, w)


def field_kernel(gp_ref, w_ref, g_ref, out_ref, pad_ref, wide_ref):
    side, _, images, _ = gp_ref.shape
    pad_field(gp_ref[...], pad_ref)
    spread_taps(w_ref, wide_ref, False)
    step = 2
    rows = step * side * images
    for part in range(side // step):
        top = part * step
        patches = jnp.concatenate(
            [
                pad_ref[top + 2 - a : top + 2 - a + step, 2 - b : 2 - b + side].reshape(rows, HALF)
                for a in range(3)
                for b in range(3)
            ],
            axis=1,
        )
        field = dot_nt(patches, wide_ref[...])
        here = slice(part * rows, (part + 1) * rows)
        out_ref[here, :] = (g_ref[here, :].astype(F32) + field).astype(BF)


def conv_field(gp, w, g):
    side, _, images, _ = gp.shape
    rows = side * side * images
    return call(
        field_kernel,
        jax.ShapeDtypeStruct((rows, HALF), BF),
        2 * rows * HALF * HALF * TAPS,
        rows * HALF * 6,
        scratch_shapes=[
            pltpu.VMEM((side + 2, side + 2, images, HALF), BF),
            pltpu.VMEM((HALF, TAPS * HALF), BF),
        ],
    )(gp, w, g)


def conv_grad_kernel(x_ref, gp_ref, out_ref, pad_ref):
    side, _, images, _ = x_ref.shape
    rows = side * side * images
    pad_field(x_ref[...], pad_ref)
    turned = gp_ref[...].T
    mask = block_mask()
    for tap in range(TAPS):
        a, b = tap // 3, tap % 3
        square = dot(turned, pad_ref[a : a + side, b : b + side].reshape(rows, HALF)).T
        square = jnp.where(mask, square, 0.0)
        slab = square[:GW]
        for q in range(1, HALF // GW):
            slab = slab + square[q * GW : (q + 1) * GW]
        out_ref[tap * GW : (tap + 1) * GW, :] = slab.astype(BF)


def conv_grad(x, gp):
    side, _, images, _ = x.shape
    rows = side * side * images
    return call(
        conv_grad_kernel,
        jax.ShapeDtypeStruct((TAPS * GW, HALF), BF),
        2 * rows * HALF * HALF * TAPS,
        rows * HALF * 4,
        scratch_shapes=[pltpu.VMEM((side + 2, side + 2, images, HALF), BF)],
    )(x, gp)


def place_vector(z, chip, core):
    return jnp.stack([z, chip, core]).astype(jnp.int32)


def with_place(kernel, grid, in_specs, out_specs, out_shape, flops, nbytes, scratch=()):
    return call(
        kernel,
        out_shape,
        flops,
        nbytes,
        grid_spec=pltpu.PrefetchScalarGridSpec(
            num_scalar_prefetch=1,
            grid=grid,
            in_specs=in_specs,
            out_specs=out_specs,
            scratch_shapes=list(scratch),
        ),
    )


def slot_of(rel, p):
    return (p[0] + 4 - (p[1] ^ rel)) % 4


def mix_columns(place, hidden, weights, other):
    rows, depth = hidden.shape
    width = weights.shape[3]

    def kernel(p, h_ref, w_ref, o_ref):
        del p
        o_ref[0] = dot(h_ref[...], w_ref[0, 0]).astype(BF)

    flip = 1 if other else 0
    return with_place(
        kernel,
        (4,),
        [
            pl.BlockSpec((rows, depth), lambda r, p: (0, 0)),
            pl.BlockSpec((1, 1, depth, width), lambda r, p: (slot_of(r, p), p[2] ^ flip, 0, 0)),
        ],
        pl.BlockSpec((1, rows, width), lambda r, p: (r, 0, 0)),
        jax.ShapeDtypeStruct((4, rows, width), BF),
        8 * rows * depth * width,
        8 * rows * width + 8 * depth * width + 2 * rows * depth,
    )(place, hidden, weights)


def mix_rows(place, h0, h1, w0, w1, other):
    rows, depth = h0.shape
    width = w0.shape[3]

    def kernel(p, ha_ref, hb_ref, wa_ref, wb_ref, o_ref):
        del p
        o_ref[0] = (dot(ha_ref[...], wa_ref[0, 0]) + dot(hb_ref[...], wb_ref[0, 0])).astype(BF)

    flip = 1 if other else 0
    h_spec = pl.BlockSpec((rows, depth), lambda r, p: (0, 0))
    w_spec = pl.BlockSpec((1, 1, depth, width), lambda r, p: (slot_of(r, p), p[2] ^ flip, 0, 0))
    return with_place(
        kernel,
        (4,),
        [h_spec, h_spec, w_spec, w_spec],
        pl.BlockSpec((1, rows, width), lambda r, p: (r, 0, 0)),
        jax.ShapeDtypeStruct((4, rows, width), BF),
        16 * rows * depth * width,
        8 * rows * width + 16 * depth * width + 4 * rows * depth,
    )(place, h0, h1, w0, w1)


def grad_pre_rows(place, wide, weights, slope):
    _, _, rows, width = wide.shape
    depth = weights.shape[2]

    def kernel(p, g_ref, w_ref, s_ref, o_ref, acc):
        step = pl.program_id(0)
        part = dot_nt(g_ref[0, 0], w_ref[0, p[2]]) + dot_nt(g_ref[0, 1], w_ref[0, 1 - p[2]])

        @pl.when(step == 0)
        def _():
            acc[...] = part

        @pl.when(step > 0)
        def _():
            acc[...] += part

        @pl.when(step == 3)
        def _():
            o_ref[...] = (acc[...] * s_ref[...]).astype(BF)

    return with_place(
        kernel,
        (4,),
        [
            pl.BlockSpec((1, 2, rows, width), lambda r, p: (r, 0, 0, 0)),
            pl.BlockSpec((1, 2, depth, width), lambda r, p: (slot_of(r, p), 0, 0, 0)),
            pl.BlockSpec((rows, depth), lambda r, p: (0, 0)),
        ],
        pl.BlockSpec((rows, depth), lambda r, p: (0, 0)),
        jax.ShapeDtypeStruct((rows, depth), BF),
        16 * rows * depth * width,
        16 * (rows + depth) * width + 6 * rows * depth,
        [pltpu.VMEM((rows, depth), F32)],
    )(place, wide, weights, slope)


def grad_pre_columns(place, wide0, wide1, w0, w1, slope):
    _, _, rows, width = wide0.shape
    depth = w0.shape[2]

    def kernel(p, ga_ref, gb_ref, wa_ref, wb_ref, s_ref, o_ref, acc):
        step = pl.program_id(0)
        mine, rest = p[2], 1 - p[2]
        part = dot_nt(ga_ref[0, 0], wa_ref[0, mine]) + dot_nt(ga_ref[0, 1], wa_ref[0, rest])
        part += dot_nt(gb_ref[0, 0], wb_ref[0, mine]) + dot_nt(gb_ref[0, 1], wb_ref[0, rest])

        @pl.when(step == 0)
        def _():
            acc[...] = part

        @pl.when(step > 0)
        def _():
            acc[...] += part

        @pl.when(step == 3)
        def _():
            o_ref[...] = (acc[...] * s_ref[...]).astype(BF)

    g_spec = pl.BlockSpec((1, 2, rows, width), lambda r, p: (r, 0, 0, 0))
    w_spec = pl.BlockSpec((1, 2, depth, width), lambda r, p: (slot_of(r, p), 0, 0, 0))
    return with_place(
        kernel,
        (4,),
        [g_spec, g_spec, w_spec, w_spec, pl.BlockSpec((rows, depth), lambda r, p: (0, 0))],
        pl.BlockSpec((rows, depth), lambda r, p: (0, 0)),
        jax.ShapeDtypeStruct((rows, depth), BF),
        32 * rows * depth * width,
        32 * (rows + depth) * width + 6 * rows * depth,
        [pltpu.VMEM((rows, depth), F32)],
    )(place, wide0, wide1, w0, w1, slope)


def mix_grad(place, hidden_t, wide):
    depth, rows = hidden_t.shape
    width = wide.shape[3]

    def kernel(p, h_ref, g_ref, o_ref):
        o_ref[0, p[2]] = dot(h_ref[...], g_ref[0, 0]).astype(BF)
        o_ref[0, 1 - p[2]] = dot(h_ref[...], g_ref[0, 1]).astype(BF)

    return with_place(
        kernel,
        (4,),
        [
            pl.BlockSpec((depth, rows), lambda i, p: (0, 0)),
            pl.BlockSpec((1, 2, rows, width), lambda i, p: (p[1] ^ ((p[0] + i) % 4), 0, 0, 0)),
        ],
        pl.BlockSpec((1, 2, depth, width), lambda i, p: (i, 0, 0, 0)),
        jax.ShapeDtypeStruct((4, 2, depth, width), BF),
        16 * rows * depth * width,
        16 * (rows + depth) * width + 2 * rows * depth,
    )(place, hidden_t, wide)


def gather_dp(own, z):
    up, down = own, own
    ups, downs = [], []
    for step in range(3):
        up = lax.ppermute(up, "dp", UP[step:])
        down = lax.ppermute(down, "dp", DOWN[step:])
        ups.append(up)
        downs.append(down)
    slots = [own] + [jnp.where(z >= j, ups[j - 1], downs[3 - j]) for j in (1, 2, 3)]
    return jnp.stack(slots)


def scatter_dp(parts):
    up = lax.ppermute(parts[3], "dp", UP[:1])
    down = lax.ppermute(parts[1], "dp", DOWN[:1])
    for step in (2, 3):
        up_term = (parts[4 - step].astype(F32) + up.astype(F32)).astype(BF)
        down_term = (parts[step].astype(F32) + down.astype(F32)).astype(BF)
        up = lax.ppermute(up_term, "dp", UP[:step])
        down = lax.ppermute(down_term, "dp", DOWN[:step])
    return parts[0].astype(F32) + up.astype(F32) + down.astype(F32)


def gather_group(own):
    cut = own.shape[0] // 2
    first, second = own[:cut], own[cut:]
    first = jnp.stack([first, lax.ppermute(first, "group", ACROSS_X)])
    second = jnp.stack([second, lax.ppermute(second, "group", ACROSS_Y)])
    first_y = lax.ppermute(first, "group", ACROSS_Y)
    second_x = lax.ppermute(second, "group", ACROSS_X)
    firsts = jnp.stack([first[0], first[1], first_y[0], first_y[1]])
    seconds = jnp.stack([second[0], second_x[0], second[1], second_x[1]])
    mine = jnp.concatenate([firsts, seconds], axis=1)
    return jnp.stack([mine, lax.ppermute(mine, "group", ACROSS_CORE)], axis=1)


def scatter_group(keep, sent):
    cut = keep.shape[1] // 2
    both = keep.astype(F32) + lax.ppermute(sent, "group", ACROSS_CORE).astype(F32)
    first, second = both[:, :cut], both[:, cut:]
    first_x = lax.ppermute(jnp.stack([first[1], first[3]]).astype(BF), "group", ACROSS_X)
    second_y = lax.ppermute(jnp.stack([second[2], second[3]]).astype(BF), "group", ACROSS_Y)
    first_near = first[0] + first_x[0].astype(F32)
    first_far = first[2] + first_x[1].astype(F32)
    second_near = second[0] + second_y[0].astype(F32)
    second_far = second[1] + second_y[1].astype(F32)
    first_y = lax.ppermute(first_far.astype(BF), "group", ACROSS_Y)
    second_x = lax.ppermute(second_far.astype(BF), "group", ACROSS_X)
    return jnp.concatenate([first_near + first_y.astype(F32), second_near + second_x.astype(F32)])


def staged(images, cotangent, conv_weight, mix_weight):
    batch, side, _, width = images.shape
    rows = batch * side * side
    scale = 1.0 / math.sqrt(rows * lax.axis_size("dp"))
    z = lax.axis_index("dp")
    group = lax.axis_index("group")
    place = place_vector(z, group // 2, group % 2)

    def to_rows(field):
        return field.transpose(1, 2, 0, 3).reshape(rows, width)

    def from_rows(flat):
        return flat.reshape(side, side, batch, width).transpose(2, 0, 1, 3)

    def half(flat, h):
        return flat[:, h * HALF : (h + 1) * HALF]

    def grid_of(flat):
        return flat.reshape(side, side, batch, flat.shape[1])

    conv = [lax.all_gather(conv_weight[layer], "dp", axis=0, tiled=True) for layer in range(2)]
    w0 = mix_weight[0].reshape(width, 2, 2, HALF).transpose(2, 1, 0, 3)
    w1 = mix_weight[1].reshape(2, HALF, 2, width).transpose(0, 2, 1, 3)
    x0 = to_rows(images)
    g2 = to_rows(cotangent)
    w0 = [gather_dp(w0[h], z) for h in range(2)]
    wide2 = gather_group(g2)
    w1 = [gather_dp(w1[h], z) for h in range(2)]

    layer0 = [conv_forward(grid_of(half(x0, h)), half(conv[0], h)) for h in range(2)]
    hidden0 = jnp.concatenate([layer0[0][0], layer0[1][0]], axis=1)
    hidden0_t = jnp.concatenate([layer0[0][1], layer0[1][1]], axis=0)
    slope0 = jnp.concatenate([layer0[0][2], layer0[1][2]], axis=1)

    x1, layer1, mix1 = [], [], []
    for h in range(2):
        sent = mix_columns(place, hidden0, w0[h], True)
        keep = mix_columns(place, hidden0, w0[h], False)
        mixed = scatter_group(keep, sent)
        x1.append((half(x0, h).astype(F32) + mixed).astype(BF))
        layer1.append(conv_forward(grid_of(x1[h]), half(conv[1], h)))
        mix1.append(scatter_dp(mix_grad(place, layer1[h][1], wide2)))

    g1, wide1, mix0, gp1 = [], [], [], []
    for h in range(2):
        gp1.append(grid_of(grad_pre_rows(place, wide2, w1[h], layer1[h][2])))
        g1.append(conv_field(gp1[h], half(conv[1], h), half(g2, h)))
        wide1.append(gather_group(g1[h]))
        mix0.append(scatter_dp(mix_grad(place, hidden0_t, wide1[h])))

    gp0 = grad_pre_columns(place, wide1[0], wide1[1], w0[0], w0[1], slope0)
    conv_terms = [
        jnp.concatenate(
            [conv_grad(grid_of(half(x0, h)), half(gp0, h)) for h in range(2)], axis=1
        ),
        jnp.concatenate(
            [conv_grad(grid_of(x1[h]), gp1[h].reshape(rows, HALF)) for h in range(2)], axis=1
        ),
    ]
    conv_sums = [
        lax.psum_scatter(term, "dp", scatter_dimension=0, tiled=True).astype(F32) * scale
        for term in conv_terms
    ]
    g0 = jnp.concatenate(
        [conv_field(grid_of(half(gp0, h)), half(conv[0], h), half(g1[h], 0)) for h in range(2)],
        axis=1,
    )

    sent = mix_rows(place, layer1[0][0], layer1[1][0], w1[0], w1[1], True)
    keep = mix_rows(place, layer1[0][0], layer1[1][0], w1[0], w1[1], False)
    mixed = scatter_group(keep, sent)
    x2 = (jnp.concatenate(x1, axis=1).astype(F32) + mixed).astype(BF)

    grad_mix0 = jnp.stack(mix0).transpose(2, 1, 0, 3).reshape(width, 2 * width) * scale
    grad_mix1 = jnp.stack(mix1).transpose(0, 2, 1, 3).reshape(width, 2 * width) * scale
    return (
        from_rows(x2),
        from_rows(g0),
        jnp.stack(conv_sums),
        jnp.stack([grad_mix0, grad_mix1]),
    )


def make_patches(field):
    side_cells = field.shape[1]
    padded = jnp.pad(field, ((0, 0), (1, 1), (1, 1), (0, 0)))
    tap_list = [
        padded[:, row_shift : row_shift + side_cells, col_shift : col_shift + side_cells, :]
        for row_shift in range(3)
        for col_shift in range(3)
    ]
    return jnp.stack(tap_list, axis=3).reshape(-1, 9, field.shape[3])


def fold_patches(pieces, batch_size, side_cells):
    pieces = pieces.reshape(batch_size, side_cells, side_cells, 9, pieces.shape[2])
    summed = jnp.zeros((batch_size, side_cells + 2, side_cells + 2, pieces.shape[4]), F32)
    for tap_index in range(9):
        row_shift = tap_index // 3
        col_shift = tap_index % 3
        summed = summed + jnp.pad(
            pieces[:, :, :, tap_index, :],
            ((0, 0), (row_shift, 2 - row_shift), (col_shift, 2 - col_shift), (0, 0)),
        )
    return summed[:, 1 : side_cells + 1, 1 : side_cells + 1, :]


def silu_slope(value):
    sigmoid_v = jax.nn.sigmoid(value)
    return sigmoid_v * (1.0 + value * (1.0 - sigmoid_v))


def general(images, cotangent, conv_weight, mix_weight):
    batch_size, side_cells, _, local_width = images.shape
    local_groups = local_width // GW
    row_count = batch_size * side_cells * side_cells
    layer_count = conv_weight.shape[0]
    grad_scale = 1.0 / math.sqrt(row_count * lax.axis_size("dp"))
    fetched = [
        (
            lax.all_gather(conv_weight[layer], "dp", axis=0, tiled=True),
            lax.all_gather(mix_weight[layer], "dp", axis=1, tiled=True),
        )
        for layer in range(layer_count)
    ]
    current = images
    saved = []
    for layer in range(layer_count):
        conv_full, mix_full = fetched[layer]
        tap_weights = conv_full.reshape(9 * GW, local_groups, GW).transpose(1, 0, 2)
        flat = make_patches(current).reshape(row_count, 9, local_groups, GW)
        patches = flat.transpose(0, 2, 1, 3).reshape(row_count, local_groups, 9 * GW)
        pre_act = jnp.einsum(
            "pgk,gko->pgo", patches, tap_weights, preferred_element_type=F32
        ).reshape(row_count, local_width)
        hidden = jax.nn.silu(pre_act).astype(BF)
        mixed = lax.psum_scatter(
            jnp.dot(hidden, mix_full, preferred_element_type=F32).astype(BF),
            "group",
            scatter_dimension=1,
            tiled=True,
        ).astype(F32)
        saved.append((patches, pre_act, hidden, tap_weights, mix_full))
        current = (
            (current.reshape(row_count, local_width).astype(F32) + mixed)
            .astype(BF)
            .reshape(images.shape)
        )
    gradient = cotangent
    conv_grads = []
    mix_grads = []
    for layer in reversed(range(layer_count)):
        patches, pre_act, hidden, tap_weights, mix_full = saved[layer]
        flat_grad = gradient.reshape(row_count, local_width)
        grad_wide = lax.all_gather(flat_grad, "group", axis=1, tiled=True)
        mix_term = lax.dot_general(
            hidden, grad_wide, (((0,), (0,)), ((), ())), preferred_element_type=F32
        )
        grad_hidden = dot_nt(grad_wide, mix_full)
        grad_pre = (
            (grad_hidden * silu_slope(pre_act)).astype(BF).reshape(row_count, local_groups, GW)
        )
        conv_term = jnp.einsum("pgk,pgo->gko", patches, grad_pre, preferred_element_type=F32)
        conv_term = conv_term.transpose(1, 0, 2).reshape(9 * GW, local_width)
        patch_grad = jnp.einsum("pgo,gko->pgk", grad_pre, tap_weights, preferred_element_type=F32)
        patch_grad = (
            patch_grad.reshape(row_count, local_groups, 9, GW)
            .transpose(0, 2, 1, 3)
            .reshape(row_count, 9, local_width)
        )
        field_grad = fold_patches(patch_grad, batch_size, side_cells)
        conv_summed, mix_summed = (
            lax.psum_scatter(
                conv_term.astype(BF), "dp", scatter_dimension=0, tiled=True
            ).astype(F32),
            lax.psum_scatter(
                mix_term.astype(BF), "dp", scatter_dimension=1, tiled=True
            ).astype(F32),
        )
        conv_grads.insert(0, conv_summed * grad_scale)
        mix_grads.insert(0, mix_summed * grad_scale)
        gradient = (gradient.astype(F32) + field_grad).astype(BF)
    return (current, gradient, jnp.stack(conv_grads), jnp.stack(mix_grads))


def solution(mesh):
    fits = mesh.shape["dp"] == 4 and mesh.shape["group"] == 8
    return jax.shard_map(
        staged if fits else general,
        mesh=mesh,
        in_specs=(
            P("dp", None, None, "group"),
            P("dp", None, None, "group"),
            P(None, "dp", "group"),
            P(None, "group", "dp"),
        ),
        out_specs=(
            P("dp", None, None, "group"),
            P("dp", None, None, "group"),
            P(None, "dp", "group"),
            P(None, "group", "dp"),
        ),
        check_vma=False,
    )
```

time: 791 us -> 555 us (0.70)
  local copies, waits for them, and re-layouts: 303 us -> 63.4 us
  waiting for transfers between devices: 285 us -> 120 us
  starting transfers between devices: 0.87 us -> 141 us
  matrix products: 102 us -> 0 us
  Pallas kernels: 0 us -> 66.2 us
  other arithmetic: 33.4 us -> 88.8 us
  blocking collectives: 38.4 us -> 48.1 us
    reduce_scatter x6 -> x2, waiting for transfers between devices: 213 us -> 0.02 us  [staged(): lax.psum_scatter(term, 'dp', scatter_dimension=0, tiled=True).astype(F32)]
    ppermute x0 -> x78, starting transfers between devices: none -> 141 us  [the longest x8 44.3 us: scatter_dp(): up = lax.ppermute(up_term, 'dp', UP[:step])]
    another operation x22 -> x8, local copies, waits for them, and re-layouts: 131 us -> 4.53 us  [the longest x2 1.9 us: gather_group(): first = jnp.stack([first, lax.ppermute(first, 'group', ACROSS_X)])]
    ppermute x0 -> x78, waiting for transfers between devices: none -> 120 us  [the longest x12 56.8 us: gather_dp(): down = lax.ppermute(down, 'dp', DOWN[step:])]
    dot_general x12 -> x0, matrix products: 102 us -> none  [the longest x2 19.7 us: per_device(): lax.dot_general(hidden, grad_wide, (((0,), (0,)), ((), ())), preferred_el...]
    all_gather x4 -> x0, waiting for transfers between devices: 70.3 us -> none  [the longest x2 70.3 us: per_device(): grad_wide = lax.all_gather(flat_grad, 'group', axis=1, tiled=True)]
    pallas_call x0 -> x25, Pallas kernels: none -> 66.2 us  [the longest x4 14 us: mix_grad(): with_place(kernel, (4,), [pl.BlockSpec((depth, rows), lambda i, p: (0, 0)...]
    another operation x6 -> x43, other arithmetic: 8.02 us -> 59.7 us  [the longest x6 20.2 us: gather_group(): return jnp.stack([mine, lax.ppermute(mine, 'group', ACROSS_CORE)], axis=1)]
  transfers between devices with their start and end apart: 10 -> 80, of which waited for: 6 -> 24; matrix products, arithmetic and copies ran while one was open for 41% -> 20% of each run, Pallas kernels for 0% -> 11%
where the time goes in v1:
time: 555 us; the launch traced here: 544 us
  starting transfers between devices  141 us (25%)
  waiting for transfers between devices  120 us (22%)
  other arithmetic  88.8 us (16%)
  Pallas kernels  66.2 us (12%)
  local copies, waits for them, and re-layouts  63.4 us (11%)
  blocking collectives  48.1 us (9%)
  between operations  16.3 us (3%)
    ppermute x12, waiting for transfers between devices, gather_dp(): down = lax.ppermute(down, 'dp', DOWN[step:])  56.8 us
    all_gather x2, blocking collectives, staged(): lax.all_gather(conv_weight[layer], 'dp', axis=0, tiled=True)  48.1 us
    ppermute x8, starting transfers between devices, scatter_dp(): up = lax.ppermute(up_term, 'dp', UP[:step])  44.3 us
    ppermute x12, starting transfers between devices, gather_dp(): up = lax.ppermute(up, 'dp', UP[step:])  28.8 us
    unnamed x135, local copies, waits for them, and re-layouts  27.7 us
    another operation x6, other arithmetic, gather_group(): return jnp.stack([mine, lax.ppermute(mine, 'group', ACROSS_CORE)], axis=1)  20.2 us
    ppermute x8, waiting for transfers between devices, scatter_dp(): up = lax.ppermute(up_term, 'dp', UP[:step])  18.2 us
    ppermute x4, waiting for transfers between devices, scatter_dp(): up = lax.ppermute(parts[3], 'dp', UP[:1])  16.7 us
  transfers between devices with their start and end apart: 80, of which 24 were waited for; matrix products, arithmetic and copies ran while one was open for 20% of the time, Pallas kernels for 11%

profile of v1, /device:TPU:0, one launch (start us, length us, event | category | flops | bytes accessed | tf_op | source)
XLA Modules:
  0.0 543.8 jit_solution(15742753986798737134)
XLA Ops:
  11.4 5.7 %collective-permute-start.11 = (bf16[2,512,256]{2,1,0:T(8,128)(2,1)}, bf16[2,512,256]{2,1,0:T(8,128)(2,1)}, u32[]{:S(2)}, u32[]{:S(2)}) collective-permute-start(bf16[2,512,256]{2,1,0:T(8,128)(2,1)} %get-tuple-element.102), channel_id=1, source_target_pairs={{0,8},{8,16},{16,24},{1,9},{9,17},{17,25},{2,10},{10,18},{18,26},{... | collective-permute-start | bytes 1572872 | tf_op jit(solution)/shard_map/ppermute | solution.py:342
  18.4 5.4 collective-permute-start
  27.5 5.3 collective-permute-start.22
  34.5 29.8 %all-gather = bf16[1,576,512]{2,1,0:T(8,128)(2,1)S(1)} all-gather(bf16[1,144,512]{2,1,0:T(8,128)(2,1)S(1)} %get-tuple-element.123), channel_id=2, replica_groups=mesh['dp'=4,'group'=8] {'dp'}, dimensions={1}, use_global_device_ids=true | all-gather | bytes 737280 | tf_op jit(solution)/shard_map/all_gather | solution.py:409
  76.6 18.3 %all-gather.1 = bf16[1,576,512]{2,1,0:T(8,128)(2,1)} all-gather(bf16[1,144,512]{2,1,0:T(8,128)(2,1)} %get-tuple-element.122), channel_id=3, replica_groups=mesh['dp'=4,'group'=8] {'dp'}, dimensions={1}, use_global_device_ids=true | all-gather | bytes 737280 | tf_op jit(solution)/shard_map/all_gather | solution.py:409
  97.9 5.4 collective-permute-start.28
  118.7 9.0 %collective-permute-done.13 = bf16[2,512,256]{2,1,0:T(8,128)(2,1)S(1)} collective-permute-done((bf16[2,512,256]{2,1,0:T(8,128)(2,1)}, bf16[2,512,256]{2,1,0:T(8,128)(2,1)S(1)}, u32[]{:S(2)}, u32[]{:S(2)}) %collective-permute-start.13) | collective-permute-done | bytes 524320 | tf_op jit(solution)/shard_map/ppermute | solution.py:343
  129.0 9.9 %collective-permute-done.29 = bf16[2,256,512]{2,1,0:T(8,128)(2,1)S(1)} collective-permute-done((bf16[2,256,512]{2,1,0:T(8,128)(2,1)}, bf16[2,256,512]{2,1,0:T(8,128)(2,1)S(1)}, u32[]{:S(2)}, u32[]{:S(2)}) %collective-permute-start.29) | collective-permute-done | bytes 524320 | tf_op jit(solution)/shard_map/ppermute | solution.py:343
  140.1 10.0 %collective-permute-done.2 = bf16[2,512,256]{2,1,0:T(8,128)(2,1)S(1)} collective-permute-done((bf16[2,512,256]{2,1,0:T(8,128)(2,1)}, bf16[2,512,256]{2,1,0:T(8,128)(2,1)S(1)}, u32[]{:S(2)}, u32[]{:S(2)}) %collective-permute-start.2) | collective-permute-done | bytes 524320 | tf_op jit(solution)/shard_map/ppermute | solution.py:343
  152.1 9.3 %collective-permute-done.24 = bf16[2,256,512]{2,1,0:T(8,128)(2,1)S(1)} collective-permute-done((bf16[2,256,512]{2,1,0:T(8,128)(2,1)}, bf16[2,256,512]{2,1,0:T(8,128)(2,1)S(1)}, u32[]{:S(2)}, u32[]{:S(2)}) %collective-permute-start.24) | collective-permute-done | bytes 524320 | tf_op jit(solution)/shard_map/ppermute | solution.py:343
  163.6 9.0 %collective-permute-done.30 = bf16[2,256,512]{2,1,0:T(8,128)(2,1)S(1)} collective-permute-done((bf16[2,256,512]{2,1,0:T(8,128)(2,1)S(1)}, bf16[2,256,512]{2,1,0:T(8,128)(2,1)S(1)}, u32[]{:S(2)}, u32[]{:S(2)}) %collective-permute-start.30) | collective-permute-done | bytes 524320 | tf_op jit(solution)/shard_map/ppermute | solution.py:343
  176.5 7.2 %collective-permute-done.14 = bf16[2,512,256]{2,1,0:T(8,128)(2,1)S(1)} collective-permute-done((bf16[2,512,256]{2,1,0:T(8,128)(2,1)S(1)}, bf16[2,512,256]{2,1,0:T(8,128)(2,1)S(1)}, u32[]{:S(2)}, u32[]{:S(2)}) %collective-permute-start.14) | collective-permute-done | bytes 524320 | tf_op jit(solution)/shard_map/ppermute | solution.py:343
  196.2 3.3 maximum_maximum_fusion
  222.3 8.2 %collective-permute-done.18 = bf16[2,512,256]{2,1,0:T(8,128)(2,1)S(1)} collective-permute-done((bf16[2,512,256]{2,1,0:T(8,128)(2,1)S(1)}, bf16[2,512,256]{2,1,0:T(8,128)(2,1)S(1)}, u32[]{:S(2)}, u32[]{:S(2)}) %collective-permute-start.18) | collective-permute-done | bytes 524320 | tf_op jit(solution)/shard_map/ppermute | solution.py:378
  234.4 7.4 %collective-permute-done.7 = bf16[2,512,256]{2,1,0:T(8,128)(2,1)S(1)} collective-permute-done((bf16[2,512,256]{2,1,0:T(8,128)(2,1)S(1)}, bf16[2,512,256]{2,1,0:T(8,128)(2,1)S(1)}, u32[]{:S(2)}, u32[]{:S(2)}) %collective-permute-start.7) | collective-permute-done | bytes 524320 | tf_op jit(solution)/shard_map/ppermute | solution.py:378
  258.7 4.6 shard_map.84
  263.4 3.4 shard_map.83
  268.8 7.6 %pad_maximum_fusion.g_ref = bf16[4,2,1024,512]{3,2,1,0:T(8,128)(2,1)} fusion(bf16[4,1,1024,512]{3,2,1,0:T(8,128)(2,1)} %bitcast.53, bf16[4,1,1024,512]{3,2,1,0:T(8,128)(2,1)} %fusion.66), kind=kLoop, calls=%fused_computation | loop fusion | flops 4194304 | bytes 16777216 | tf_op jit(solution)/shard_map/stack | solution.py:371
  276.5 3.5 copy-done
  281.2 4.2 shard_map.85.gp_ref
  290.5 4.0 shard_map.87.gp_ref
  303.3 3.5 copy-done.1
  307.8 3.4 shard_map.99
  311.3 6.5 %collective-permute-start.72 = (bf16[2,256,512]{2,1,0:T(8,128)(2,1)S(1)}, bf16[2,256,512]{2,1,0:T(8,128)(2,1)S(1)}, u32[]{:S(2)}, u32[]{:S(2)}) collective-permute-start(bf16[2,256,512]{2,1,0:T(8,128)(2,1)S(1)} %get-tuple-element.78), channel_id=1, source_target_pairs={{0,8},{1,9},{2,10},{3,11},{4,12},{5,13},{6,14},{7,15}} | collective-permute-start | bytes 1572872 | tf_op jit(solution)/shard_map/ppermute | solution.py:351
  317.9 3.4 shard_map.98
  328.7 5.6 %collective-permute-done.72 = bf16[2,256,512]{2,1,0:T(8,128)(2,1)S(1)} collective-permute-done((bf16[2,256,512]{2,1,0:T(8,128)(2,1)S(1)}, bf16[2,256,512]{2,1,0:T(8,128)(2,1)S(1)}, u32[]{:S(2)}, u32[]{:S(2)}) %collective-permute-start.72) | collective-permute-done | bytes 524320 | tf_op jit(solution)/shard_map/ppermute | solution.py:351
  337.2 7.4 %collective-permute-done.66 = bf16[2,256,512]{2,1,0:T(8,128)(2,1)S(1)} collective-permute-done((bf16[2,256,512]{2,1,0:T(8,128)(2,1)S(1)}, bf16[2,256,512]{2,1,0:T(8,128)(2,1)S(1)}, u32[]{:S(2)}, u32[]{:S(2)}) %collective-permute-start.66) | collective-permute-done | bytes 524320 | tf_op jit(solution)/shard_map/ppermute | solution.py:351
  347.1 4.4 collective-permute-start.73
  357.6 4.4 collective-permute-start.67
  372.2 5.2 collective-permute-start.74
  383.2 10.1 %collective-permute-start.68 = (bf16[2,256,512]{2,1,0:T(8,128)(2,1)}, bf16[2,256,512]{2,1,0:T(8,128)(2,1)}, u32[]{:S(2)}, u32[]{:S(2)}) collective-permute-start(bf16[2,256,512]{2,1,0:T(8,128)(2,1)} %get-tuple-element.68), channel_id=1, source_target_pairs={{0,8},{8,16},{16,24},{1,9},{9,17},{17,25},{2,10},{10,18},{18,26},{... | collective-permute-start | bytes 1572872 | tf_op jit(solution)/shard_map/ppermute | solution.py:356
  402.7 4.3 copy.37
  407.0 3.9 reshape.140
  410.9 8.6 %fusion.47 = (bf16[4,1024,512]{2,1,0:T(8,128)(2,1)S(1)}, f32[4,1024,512]{2,1,0:T(8,128)}) fusion(bf16[4,1024,512]{2,1,0:T(8,128)(2,1)} %collective-permute-done.34, bf16[4,1024,512]{2,1,0:T(8,128)(2,1)} %copy-done.4), kind=kLoop, calls=%fused_computation.158 | loop fusion | flops 8388608 | bytes 20971520 | tf_op jit(solution)/shard_map/convert.12
  428.4 3.5 shard_map.97
  432.0 3.5 shard_map.96
  435.5 8.2 %shard_map.89 = bf16[1024,512]{1,0:T(8,128)(2,1)S(1)} custom-call(s32[3]{0:T(128)S(1)} %pad_add_fusion.p, bf16[4,2,1024,256]{3,2,1,0:T(8,128)(2,1)S(1)} %pad_maximum_fusion.1.ga_ref.g_ref, bf16[4,2,1024,256]{3,2,1,0:T(8,128)(2,1)} %copy-done.11, bf16[4,2,512,256]{3,2,1,0:T(8,128)(2,1)S(1)} %copy-done.3, ...), custom_call_target="tpu_custom_call" | custom-call | flops 4294967296 | bytes 15728640 | tf_op jit(solution)/shard_map/pallas_call | solution.py:304
  444.7 4.4 collective-permute-start.60
  464.6 4.1 collective-permute-start.61
  468.7 3.7 collective-permute-done.54
  474.4 4.9 collective-permute-start.55
  480.1 3.3 fusion.27
  483.4 7.5 %collective-permute-done.61 = bf16[2,512,256]{2,1,0:T(8,128)(2,1)S(1)} collective-permute-done((bf16[2,512,256]{2,1,0:T(8,128)(2,1)S(1)}, bf16[2,512,256]{2,1,0:T(8,128)(2,1)S(1)}, u32[]{:S(2)}, u32[]{:S(2)}) %collective-permute-start.61) | collective-permute-done | bytes 524320 | tf_op jit(solution)/shard_map/ppermute | solution.py:356
  495.0 4.0 collective-permute-done.55
  499.0 5.2 collective-permute-start.62
  508.6 5.9 %collective-permute-start.56 = (bf16[2,512,256]{2,1,0:T(8,128)(2,1)}, bf16[2,512,256]{2,1,0:T(8,128)(2,1)S(1)}, u32[]{:S(2)}, u32[]{:S(2)}) collective-permute-start(bf16[2,512,256]{2,1,0:T(8,128)(2,1)} %get-tuple-element.56), channel_id=1, source_target_pairs={{0,8},{8,16},{16,24},{1,9},{9,17},{17,25},{2,10},{10,18},{18,26},{... | collective-permute-start | bytes 1572872 | tf_op jit(solution)/shard_map/ppermute | solution.py:356
  526.5 4.7 pad_maximum_fusion.3
  531.2 5.3 copy.36
  (383 shorter events, 217.6 us)
Async XLA Ops:
  7.2 386.2 %reduce-scatter.5.cloned.1.call-start = ((), (), s32[]{:S(2)}) async-start(), calls=%async_computation.3 | async-start | bytes 737280 | tf_op jit(solution)/shard_map/reduce_scatter | solution.py:449
  11.4 83.5 %collective-permute-start.11 = (bf16[2,512,256]{2,1,0:T(8,128)(2,1)}, bf16[2,512,256]{2,1,0:T(8,128)(2,1)}, u32[]{:S(2)}, u32[]{:S(2)}) collective-permute-start(bf16[2,512,256]{2,1,0:T(8,128)(2,1)} %get-tuple-element.102), channel_id=1, source_target_pairs={{0,8},{8,16},{16,24},{1,9},{9,17},{17,25},{2,10},{10,18},{18,26},{... | collective-permute-start | bytes 1572872 | tf_op jit(solution)/shard_map/ppermute | solution.py:342
  17.1 80.8 %collective-permute-start.12 = (bf16[2,512,256]{2,1,0:T(8,128)(2,1)}, bf16[2,512,256]{2,1,0:T(8,128)(2,1)}, u32[]{:S(2)}, u32[]{:S(2)}) collective-permute-start(bf16[2,512,256]{2,1,0:T(8,128)(2,1)} %get-tuple-element.102), channel_id=1, source_target_pairs={{24,16},{16,8},{8,0},{25,17},{17,9},{9,1},{26,18},{18,10},{10,2},{... | collective-permute-start | bytes 1572872 | tf_op jit(solution)/shard_map/ppermute | solution.py:343
  18.4 84.8 %collective-permute-start = (bf16[2,512,256]{2,1,0:T(8,128)(2,1)}, bf16[2,512,256]{2,1,0:T(8,128)(2,1)}, u32[]{:S(2)}, u32[]{:S(2)}) collective-permute-start(bf16[2,512,256]{2,1,0:T(8,128)(2,1)} %get-tuple-element.101), channel_id=1, source_target_pairs={{0,8},{8,16},{16,24},{1,9},{9,17},{17,25},{2,10},{10,18},{18,26},{... | collective-permute-start | bytes 1572872 | tf_op jit(solution)/shard_map/ppermute | solution.py:342
  23.8 81.0 %collective-permute-start.1 = (bf16[2,512,256]{2,1,0:T(8,128)(2,1)}, bf16[2,512,256]{2,1,0:T(8,128)(2,1)}, u32[]{:S(2)}, u32[]{:S(2)}) collective-permute-start(bf16[2,512,256]{2,1,0:T(8,128)(2,1)} %get-tuple-element.101), channel_id=1, source_target_pairs={{24,16},{16,8},{8,0},{25,17},{17,9},{9,1},{26,18},{18,10},{10,2},{... | collective-permute-start | bytes 1572872 | tf_op jit(solution)/shard_map/ppermute | solution.py:343
  27.5 81.7 %collective-permute-start.22 = (bf16[2,256,512]{2,1,0:T(8,128)(2,1)}, bf16[2,256,512]{2,1,0:T(8,128)(2,1)}, u32[]{:S(2)}, u32[]{:S(2)}) collective-permute-start(bf16[2,256,512]{2,1,0:T(8,128)(2,1)} %get-tuple-element.95), channel_id=1, source_target_pairs={{0,8},{8,16},{16,24},{1,9},{9,17},{17,25},{2,10},{10,18},{18,26},{... | collective-permute-start | bytes 1572872 | tf_op jit(solution)/shard_map/ppermute | solution.py:342
  109.9 17.8 %collective-permute-start.13 = (bf16[2,512,256]{2,1,0:T(8,128)(2,1)}, bf16[2,512,256]{2,1,0:T(8,128)(2,1)S(1)}, u32[]{:S(2)}, u32[]{:S(2)}) collective-permute-start(bf16[2,512,256]{2,1,0:T(8,128)(2,1)} %collective-permute-done.12), channel_id=1, source_target_pairs={{16,8},{8,0},{17,9},{9,1},{18,10},{10,2},{19,11},{11,3},{20,12},{1... | collective-permute-start | bytes 1572872 | tf_op jit(solution)/shard_map/ppermute | solution.py:343
  112.3 26.6 %collective-permute-start.29 = (bf16[2,256,512]{2,1,0:T(8,128)(2,1)}, bf16[2,256,512]{2,1,0:T(8,128)(2,1)S(1)}, u32[]{:S(2)}, u32[]{:S(2)}) collective-permute-start(bf16[2,256,512]{2,1,0:T(8,128)(2,1)} %get-tuple-element.96), channel_id=1, source_target_pairs={{24,16},{16,8},{8,0},{25,17},{17,9},{9,1},{26,18},{18,10},{10,2},{... | collective-permute-start | bytes 1572872 | tf_op jit(solution)/shard_map/ppermute | solution.py:343
  113.6 25.8 %collective-permute-start.4 = (bf16[2,512,256]{2,1,0:T(8,128)(2,1)}, bf16[2,512,256]{2,1,0:T(8,128)(2,1)S(1)}, u32[]{:S(2)}, u32[]{:S(2)}) collective-permute-start(bf16[2,512,256]{2,1,0:T(8,128)(2,1)} %collective-permute-done), channel_id=1, source_target_pairs={{8,16},{16,24},{9,17},{17,25},{10,18},{18,26},{11,19},{19,27},{12,... | collective-permute-start | bytes 1572872 | tf_op jit(solution)/shard_map/ppermute | solution.py:342
  114.4 35.8 %collective-permute-start.2 = (bf16[2,512,256]{2,1,0:T(8,128)(2,1)}, bf16[2,512,256]{2,1,0:T(8,128)(2,1)S(1)}, u32[]{:S(2)}, u32[]{:S(2)}) collective-permute-start(bf16[2,512,256]{2,1,0:T(8,128)(2,1)} %collective-permute-done.1), channel_id=1, source_target_pairs={{16,8},{8,0},{17,9},{9,1},{18,10},{10,2},{19,11},{11,3},{20,12},{1... | collective-permute-start | bytes 1572872 | tf_op jit(solution)/shard_map/ppermute | solution.py:343
  118.0 33.5 %collective-permute-start.26 = (bf16[2,256,512]{2,1,0:T(8,128)(2,1)}, bf16[2,256,512]{2,1,0:T(8,128)(2,1)S(1)}, u32[]{:S(2)}, u32[]{:S(2)}) collective-permute-start(bf16[2,256,512]{2,1,0:T(8,128)(2,1)} %collective-permute-done.22), channel_id=1, source_target_pairs={{8,16},{16,24},{9,17},{17,25},{10,18},{18,26},{11,19},{19,27},{12,... | collective-permute-start | bytes 1572872 | tf_op jit(solution)/shard_map/ppermute | solution.py:342
  127.7 33.7 %collective-permute-start.24 = (bf16[2,256,512]{2,1,0:T(8,128)(2,1)}, bf16[2,256,512]{2,1,0:T(8,128)(2,1)S(1)}, u32[]{:S(2)}, u32[]{:S(2)}) collective-permute-start(bf16[2,256,512]{2,1,0:T(8,128)(2,1)} %collective-permute-done.23), channel_id=1, source_target_pairs={{16,8},{8,0},{17,9},{9,1},{18,10},{10,2},{19,11},{11,3},{20,12},{1... | collective-permute-start | bytes 1572872 | tf_op jit(solution)/shard_map/ppermute | solution.py:343
  138.9 53.9 %collective-permute-start.42 = (bf16[2,512,512]{2,1,0:T(8,128)(2,1)S(1)}, bf16[2,512,512]{2,1,0:T(8,128)(2,1)S(1)}, u32[]{:S(2)}, u32[]{:S(2)}) collective-permute-start(bf16[2,512,512]{2,1,0:T(8,128)(2,1)S(1)} %pad_maximum_fusion.12), channel_id=1, source_target_pairs={{0,2},{1,3},{2,0},{3,1},{4,6},{5,7},{6,4},{7,5},{8,10},{9,11},{10,... | collective-permute-start | bytes 3145736 | tf_op jit(solution)/shard_map/ppermute | solution.py:367
  139.4 22.7 %collective-permute-start.32 = (bf16[2,256,512]{2,1,0:T(8,128)(2,1)}, bf16[2,256,512]{2,1,0:T(8,128)(2,1)S(1)}, u32[]{:S(2)}, u32[]{:S(2)}) collective-permute-start(bf16[2,256,512]{2,1,0:T(8,128)(2,1)} %collective-permute-done.28), channel_id=1, source_target_pairs={{8,16},{16,24},{9,17},{17,25},{10,18},{18,26},{11,19},{19,27},{12,... | collective-permute-start | bytes 1572872 | tf_op jit(solution)/shard_map/ppermute | solution.py:342
  150.1 22.5 %collective-permute-start.30 = (bf16[2,256,512]{2,1,0:T(8,128)(2,1)S(1)}, bf16[2,256,512]{2,1,0:T(8,128)(2,1)S(1)}, u32[]{:S(2)}, u32[]{:S(2)}) collective-permute-start(bf16[2,256,512]{2,1,0:T(8,128)(2,1)S(1)} %collective-permute-done.29), channel_id=1, source_target_pairs={{16,8},{8,0},{17,9},{9,1},{18,10},{10,2},{19,11},{11,3},{20,12},{1... | collective-permute-start | bytes 1572872 | tf_op jit(solution)/shard_map/ppermute | solution.py:343
  151.5 42.9 %collective-permute-start.40 = (bf16[2,512,512]{2,1,0:T(8,128)(2,1)S(1)}, bf16[2,512,512]{2,1,0:T(8,128)(2,1)S(1)}, u32[]{:S(2)}, u32[]{:S(2)}) collective-permute-start(bf16[2,512,512]{2,1,0:T(8,128)(2,1)S(1)} %pad_maximum_fusion.11), channel_id=1, source_target_pairs={{0,4},{1,5},{2,6},{3,7},{4,0},{5,1},{6,2},{7,3},{8,12},{9,13},{10,... | collective-permute-start | bytes 3145736 | tf_op jit(solution)/shard_map/ppermute | solution.py:366
  162.1 21.6 %collective-permute-start.14 = (bf16[2,512,256]{2,1,0:T(8,128)(2,1)S(1)}, bf16[2,512,256]{2,1,0:T(8,128)(2,1)S(1)}, u32[]{:S(2)}, u32[]{:S(2)}) collective-permute-start(bf16[2,512,256]{2,1,0:T(8,128)(2,1)S(1)} %collective-permute-done.13), channel_id=1, source_target_pairs={{8,0},{9,1},{10,2},{11,3},{12,4},{13,5},{14,6},{15,7}} | collective-permute-start | bytes 1572872 | tf_op jit(solution)/shard_map/ppermute | solution.py:343
  172.6 17.7 %collective-permute-start.5 = (bf16[2,512,256]{2,1,0:T(8,128)(2,1)S(1)}, bf16[2,512,256]{2,1,0:T(8,128)(2,1)S(1)}, u32[]{:S(2)}, u32[]{:S(2)}) collective-permute-start(bf16[2,512,256]{2,1,0:T(8,128)(2,1)S(1)} %collective-permute-done.4), channel_id=1, source_target_pairs={{16,24},{17,25},{18,26},{19,27},{20,28},{21,29},{22,30},{23,31}} | collective-permute-start | bytes 1572872 | tf_op jit(solution)/shard_map/ppermute | solution.py:342
  174.1 25.3 %collective-permute-start.3 = (bf16[2,512,256]{2,1,0:T(8,128)(2,1)S(1)}, bf16[2,512,256]{2,1,0:T(8,128)(2,1)S(1)}, u32[]{:S(2)}, u32[]{:S(2)}) collective-permute-start(bf16[2,512,256]{2,1,0:T(8,128)(2,1)S(1)} %collective-permute-done.2), channel_id=1, source_target_pairs={{8,0},{9,1},{10,2},{11,3},{12,4},{13,5},{14,6},{15,7}} | collective-permute-start | bytes 1572872 | tf_op jit(solution)/shard_map/ppermute | solution.py:343
  183.7 18.5 %collective-permute-start.27 = (bf16[2,256,512]{2,1,0:T(8,128)(2,1)S(1)}, bf16[2,256,512]{2,1,0:T(8,128)(2,1)}, u32[]{:S(2)}, u32[]{:S(2)}) collective-permute-start(bf16[2,256,512]{2,1,0:T(8,128)(2,1)S(1)} %collective-permute-done.26), channel_id=1, source_target_pairs={{16,24},{17,25},{18,26},{19,27},{20,28},{21,29},{22,30},{23,31}} | collective-permute-start | bytes 1572872 | tf_op jit(solution)/shard_map/ppermute | solution.py:342
  203.9 64.9 %collective-permute-start.43 = (bf16[4,1024,512]{2,1,0:T(8,128)(2,1)}, bf16[4,1024,512]{2,1,0:T(8,128)(2,1)}, u32[]{:S(2)}, u32[]{:S(2)}) collective-permute-start(bf16[4,1024,512]{2,1,0:T(8,128)(2,1)} %maximum_maximum_fusion), channel_id=1, source_target_pairs={{0,1},{1,0},{2,3},{3,2},{4,5},{5,4},{6,7},{7,6},{8,9},{9,8},{10,11... | collective-permute-start | bytes 12582920 | tf_op jit(solution)/shard_map/ppermute | solution.py:371
  219.4 22.4 %collective-permute-start.7 = (bf16[2,512,256]{2,1,0:T(8,128)(2,1)S(1)}, bf16[2,512,256]{2,1,0:T(8,128)(2,1)S(1)}, u32[]{:S(2)}, u32[]{:S(2)}) collective-permute-start(bf16[2,512,256]{2,1,0:T(8,128)(2,1)S(1)} %pad_maximum_fusion.17), channel_id=1, source_target_pairs={{0,2},{1,3},{2,0},{3,1},{4,6},{5,7},{6,4},{7,5},{8,10},{9,11},{10,... | collective-permute-start | bytes 1572872 | tf_op jit(solution)/shard_map/ppermute | solution.py:378
  220.0 23.2 %collective-permute-start.9 = (bf16[2,512,256]{2,1,0:T(8,128)(2,1)S(1)}, bf16[2,512,256]{2,1,0:T(8,128)(2,1)S(1)}, u32[]{:S(2)}, u32[]{:S(2)}) collective-permute-start(bf16[2,512,256]{2,1,0:T(8,128)(2,1)S(1)} %stack.284), channel_id=1, source_target_pairs={{0,4},{1,5},{2,6},{3,7},{4,0},{5,1},{6,2},{7,3},{8,12},{9,13},{10,... | collective-permute-start | bytes 1572872 | tf_op jit(solution)/shard_map/ppermute | solution.py:379
  289.5 31.9 %collective-permute-start.46 = (bf16[512,256]{1,0:T(8,128)(2,1)}, bf16[512,256]{1,0:T(8,128)(2,1)}, u32[]{:S(2)}, u32[]{:S(2)}) collective-permute-start(bf16[512,256]{1,0:T(8,128)(2,1)} %get-tuple-element.118), channel_id=1, source_target_pairs={{0,4},{1,5},{2,6},{3,7},{4,0},{5,1},{6,2},{7,3},{8,12},{9,13},{10,... | collective-permute-start | bytes 786440 | tf_op jit(solution)/shard_map/ppermute | solution.py:365
  290.0 33.5 %collective-permute-start.44 = (bf16[512,256]{1,0:T(8,128)(2,1)}, bf16[512,256]{1,0:T(8,128)(2,1)}, u32[]{:S(2)}, u32[]{:S(2)}) collective-permute-start(bf16[512,256]{1,0:T(8,128)(2,1)} %get-tuple-element.119), channel_id=1, source_target_pairs={{0,2},{1,3},{2,0},{3,1},{4,6},{5,7},{6,4},{7,5},{8,10},{9,11},{10,... | collective-permute-start | bytes 786440 | tf_op jit(solution)/shard_map/ppermute | solution.py:364
  299.3 25.3 %collective-permute-start.51 = (bf16[512,256]{1,0:T(8,128)(2,1)}, bf16[512,256]{1,0:T(8,128)(2,1)}, u32[]{:S(2)}, u32[]{:S(2)}) collective-permute-start(bf16[512,256]{1,0:T(8,128)(2,1)} %get-tuple-element.112), channel_id=1, source_target_pairs={{0,4},{1,5},{2,6},{3,7},{4,0},{5,1},{6,2},{7,3},{8,12},{9,13},{10,... | collective-permute-start | bytes 786440 | tf_op jit(solution)/shard_map/ppermute | solution.py:365
  300.9 25.1 %collective-permute-start.49 = (bf16[512,256]{1,0:T(8,128)(2,1)}, bf16[512,256]{1,0:T(8,128)(2,1)}, u32[]{:S(2)}, u32[]{:S(2)}) collective-permute-start(bf16[512,256]{1,0:T(8,128)(2,1)} %get-tuple-element.113), channel_id=1, source_target_pairs={{0,2},{1,3},{2,0},{3,1},{4,6},{5,7},{6,4},{7,5},{8,10},{9,11},{10,... | collective-permute-start | bytes 786440 | tf_op jit(solution)/shard_map/ppermute | solution.py:364
  303.2 203.5 %reduce-scatter.3.cloned.1.call-start = ((), (), s32[]{:S(2)}) async-start(), calls=%async_computation.2 | async-start | bytes 737280 | tf_op jit(solution)/shard_map/reduce_scatter | solution.py:449
  311.3 22.9 %collective-permute-start.72 = (bf16[2,256,512]{2,1,0:T(8,128)(2,1)S(1)}, bf16[2,256,512]{2,1,0:T(8,128)(2,1)S(1)}, u32[]{:S(2)}, u32[]{:S(2)}) collective-permute-start(bf16[2,256,512]{2,1,0:T(8,128)(2,1)S(1)} %get-tuple-element.78), channel_id=1, source_target_pairs={{0,8},{1,9},{2,10},{3,11},{4,12},{5,13},{6,14},{7,15}} | collective-permute-start | bytes 1572872 | tf_op jit(solution)/shard_map/ppermute | solution.py:351
  323.5 87.4 %collective-permute-start.34 = (bf16[4,1024,512]{2,1,0:T(8,128)(2,1)}, bf16[4,1024,512]{2,1,0:T(8,128)(2,1)}, u32[]{:S(2)}, u32[]{:S(2)}) collective-permute-start(bf16[4,1024,512]{2,1,0:T(8,128)(2,1)} %shard_map.84), channel_id=1, source_target_pairs={{0,1},{1,0},{2,3},{3,2},{4,5},{5,4},{6,7},{7,6},{8,9},{9,8},{10,11... | collective-permute-start | bytes 12582920 | tf_op jit(solution)/shard_map/ppermute | solution.py:376
  324.6 20.0 %collective-permute-start.66 = (bf16[2,256,512]{2,1,0:T(8,128)(2,1)S(1)}, bf16[2,256,512]{2,1,0:T(8,128)(2,1)S(1)}, u32[]{:S(2)}, u32[]{:S(2)}) collective-permute-start(bf16[2,256,512]{2,1,0:T(8,128)(2,1)S(1)} %get-tuple-element.72), channel_id=1, source_target_pairs={{0,8},{1,9},{2,10},{3,11},{4,12},{5,13},{6,14},{7,15}} | collective-permute-start | bytes 1572872 | tf_op jit(solution)/shard_map/ppermute | solution.py:351
  325.9 20.1 %collective-permute-start.69 = (bf16[2,256,512]{2,1,0:T(8,128)(2,1)S(1)}, bf16[2,256,512]{2,1,0:T(8,128)(2,1)S(1)}, u32[]{:S(2)}, u32[]{:S(2)}) collective-permute-start(bf16[2,256,512]{2,1,0:T(8,128)(2,1)S(1)} %get-tuple-element.73), channel_id=1, source_target_pairs={{24,16},{25,17},{26,18},{27,19},{28,20},{29,21},{30,22},{31,23}} | collective-permute-start | bytes 1572872 | tf_op jit(solution)/shard_map/ppermute | solution.py:352
  347.1 18.3 %collective-permute-start.73 = (bf16[2,256,512]{2,1,0:T(8,128)(2,1)S(1)}, bf16[2,256,512]{2,1,0:T(8,128)(2,1)S(1)}, u32[]{:S(2)}, u32[]{:S(2)}) collective-permute-start(bf16[2,256,512]{2,1,0:T(8,128)(2,1)S(1)} %get-tuple-element.76), channel_id=1, source_target_pairs={{0,8},{8,16},{1,9},{9,17},{2,10},{10,18},{3,11},{11,19},{4,12},{12... | collective-permute-start | bytes 1572872 | tf_op jit(solution)/shard_map/ppermute | solution.py:356
  365.3 58.7 %collective-permute-start.48 = (bf16[4,1024,256]{2,1,0:T(8,128)(2,1)}, bf16[4,1024,256]{2,1,0:T(8,128)(2,1)}, u32[]{:S(2)}, u32[]{:S(2)}) collective-permute-start(bf16[4,1024,256]{2,1,0:T(8,128)(2,1)} %maximum_maximum_fusion.1), channel_id=1, source_target_pairs={{0,1},{1,0},{2,3},{3,2},{4,5},{5,4},{6,7},{7,6},{8,9},{9,8},{10,11... | collective-permute-start | bytes 6291464 | tf_op jit(solution)/shard_map/ppermute | solution.py:371
  366.5 16.7 %collective-permute-start.77 = (bf16[2,256,512]{2,1,0:T(8,128)(2,1)S(1)}, bf16[2,256,512]{2,1,0:T(8,128)(2,1)}, u32[]{:S(2)}, u32[]{:S(2)}) collective-permute-start(bf16[2,256,512]{2,1,0:T(8,128)(2,1)S(1)} %get-tuple-element.75), channel_id=1, source_target_pairs={{24,16},{16,8},{8,0},{25,17},{17,9},{9,1},{26,18},{18,10},{10,2},{... | collective-permute-start | bytes 1572872 | tf_op jit(solution)/shard_map/ppermute | solution.py:357
  372.2 22.8 %collective-permute-start.74 = (bf16[2,256,512]{2,1,0:T(8,128)(2,1)}, bf16[2,256,512]{2,1,0:T(8,128)(2,1)}, u32[]{:S(2)}, u32[]{:S(2)}) collective-permute-start(bf16[2,256,512]{2,1,0:T(8,128)(2,1)} %get-tuple-element.74), channel_id=1, source_target_pairs={{0,8},{8,16},{16,24},{1,9},{9,17},{17,25},{2,10},{10,18},{18,26},{... | collective-permute-start | bytes 1572872 | tf_op jit(solution)/shard_map/ppermute | solution.py:356
  378.7 17.9 %collective-permute-start.71 = (bf16[2,256,512]{2,1,0:T(8,128)(2,1)}, bf16[2,256,512]{2,1,0:T(8,128)(2,1)}, u32[]{:S(2)}, u32[]{:S(2)}) collective-permute-start(bf16[2,256,512]{2,1,0:T(8,128)(2,1)} %get-tuple-element.69), channel_id=1, source_target_pairs={{24,16},{16,8},{8,0},{25,17},{17,9},{9,1},{26,18},{18,10},{10,2},{... | collective-permute-start | bytes 1572872 | tf_op jit(solution)/shard_map/ppermute | solution.py:357
  395.0 31.2 %collective-permute-start.53 = (bf16[4,1024,256]{2,1,0:T(8,128)(2,1)}, bf16[4,1024,256]{2,1,0:T(8,128)(2,1)}, u32[]{:S(2)}, u32[]{:S(2)}) collective-permute-start(bf16[4,1024,256]{2,1,0:T(8,128)(2,1)} %maximum_maximum_fusion.2), channel_id=1, source_target_pairs={{0,1},{1,0},{2,3},{3,2},{4,5},{5,4},{6,7},{7,6},{8,9},{9,8},{10,11... | collective-permute-start | bytes 6291464 | tf_op jit(solution)/shard_map/ppermute | solution.py:371
  421.7 57.6 %collective-permute-start.35 = (bf16[2,512,512]{2,1,0:T(8,128)(2,1)}, bf16[2,512,512]{2,1,0:T(8,128)(2,1)}, u32[]{:S(2)}, u32[]{:S(2)}) collective-permute-start(bf16[2,512,512]{2,1,0:T(8,128)(2,1)} %pad_maximum_fusion.10), channel_id=1, source_target_pairs={{0,2},{1,3},{2,0},{3,1},{4,6},{5,7},{6,4},{7,5},{8,10},{9,11},{10,... | collective-permute-start | bytes 3145736 | tf_op jit(solution)/shard_map/ppermute | solution.py:378
  422.7 57.3 %collective-permute-start.37 = (bf16[2,512,512]{2,1,0:T(8,128)(2,1)}, bf16[2,512,512]{2,1,0:T(8,128)(2,1)}, u32[]{:S(2)}, u32[]{:S(2)}) collective-permute-start(bf16[2,512,512]{2,1,0:T(8,128)(2,1)} %stack.286), channel_id=1, source_target_pairs={{0,4},{1,5},{2,6},{3,7},{4,0},{5,1},{6,2},{7,3},{8,12},{9,13},{10,... | collective-permute-start | bytes 3145736 | tf_op jit(solution)/shard_map/ppermute | solution.py:379
  464.6 26.3 %collective-permute-start.61 = (bf16[2,512,256]{2,1,0:T(8,128)(2,1)S(1)}, bf16[2,512,256]{2,1,0:T(8,128)(2,1)S(1)}, u32[]{:S(2)}, u32[]{:S(2)}) collective-permute-start(bf16[2,512,256]{2,1,0:T(8,128)(2,1)S(1)} %get-tuple-element.64), channel_id=1, source_target_pairs={{0,8},{8,16},{1,9},{9,17},{2,10},{10,18},{3,11},{11,19},{4,12},{12... | collective-permute-start | bytes 1572872 | tf_op jit(solution)/shard_map/ppermute | solution.py:356
  472.4 19.9 %collective-permute-start.64 = (bf16[2,512,256]{2,1,0:T(8,128)(2,1)S(1)}, bf16[2,512,256]{2,1,0:T(8,128)(2,1)S(1)}, u32[]{:S(2)}, u32[]{:S(2)}) collective-permute-start(bf16[2,512,256]{2,1,0:T(8,128)(2,1)S(1)} %get-tuple-element.65), channel_id=1, source_target_pairs={{24,16},{16,8},{25,17},{17,9},{26,18},{18,10},{27,19},{19,11},{28,... | collective-permute-start | bytes 1572872 | tf_op jit(solution)/shard_map/ppermute | solution.py:357
  474.4 24.6 %collective-permute-start.55 = (bf16[2,512,256]{2,1,0:T(8,128)(2,1)S(1)}, bf16[2,512,256]{2,1,0:T(8,128)(2,1)S(1)}, u32[]{:S(2)}, u32[]{:S(2)}) collective-permute-start(bf16[2,512,256]{2,1,0:T(8,128)(2,1)S(1)} %get-tuple-element.58), channel_id=1, source_target_pairs={{0,8},{8,16},{1,9},{9,17},{2,10},{10,18},{3,11},{11,19},{4,12},{12... | collective-permute-start | bytes 1572872 | tf_op jit(solution)/shard_map/ppermute | solution.py:356
  479.3 24.8 %collective-permute-start.58 = (bf16[2,512,256]{2,1,0:T(8,128)(2,1)S(1)}, bf16[2,512,256]{2,1,0:T(8,128)(2,1)S(1)}, u32[]{:S(2)}, u32[]{:S(2)}) collective-permute-start(bf16[2,512,256]{2,1,0:T(8,128)(2,1)S(1)} %get-tuple-element.59), channel_id=1, source_target_pairs={{24,16},{16,8},{25,17},{17,9},{26,18},{18,10},{27,19},{19,11},{28,... | collective-permute-start | bytes 1572872 | tf_op jit(solution)/shard_map/ppermute | solution.py:357
  483.4 25.2 %collective-permute-start.36 = (bf16[512,512]{1,0:T(8,128)(2,1)}, bf16[512,512]{1,0:T(8,128)(2,1)S(1)}, u32[]{:S(2)}, u32[]{:S(2)}) collective-permute-start(bf16[512,512]{1,0:T(8,128)(2,1)} %get-tuple-element.38), channel_id=1, source_target_pairs={{0,4},{1,5},{2,6},{3,7},{4,0},{5,1},{6,2},{7,3},{8,12},{9,13},{10,... | collective-permute-start | bytes 1572872 | tf_op jit(solution)/shard_map/ppermute | solution.py:384
  490.9 23.6 %collective-permute-start.38 = (bf16[512,512]{1,0:T(8,128)(2,1)}, bf16[512,512]{1,0:T(8,128)(2,1)}, u32[]{:S(2)}, u32[]{:S(2)}) collective-permute-start(bf16[512,512]{1,0:T(8,128)(2,1)} %get-tuple-element.39), channel_id=1, source_target_pairs={{0,2},{1,3},{2,0},{3,1},{4,6},{5,7},{6,4},{7,5},{8,10},{9,11},{10,... | collective-permute-start | bytes 1572872 | tf_op jit(solution)/shard_map/ppermute | solution.py:385
  493.6 26.5 %collective-permute-start.65 = (bf16[2,512,256]{2,1,0:T(8,128)(2,1)}, bf16[2,512,256]{2,1,0:T(8,128)(2,1)S(1)}, u32[]{:S(2)}, u32[]{:S(2)}) collective-permute-start(bf16[2,512,256]{2,1,0:T(8,128)(2,1)} %get-tuple-element.63), channel_id=1, source_target_pairs={{24,16},{16,8},{8,0},{25,17},{17,9},{9,1},{26,18},{18,10},{10,2},{... | collective-permute-start | bytes 1572872 | tf_op jit(solution)/shard_map/ppermute | solution.py:357
  499.0 21.1 %collective-permute-start.62 = (bf16[2,512,256]{2,1,0:T(8,128)(2,1)}, bf16[2,512,256]{2,1,0:T(8,128)(2,1)}, u32[]{:S(2)}, u32[]{:S(2)}) collective-permute-start(bf16[2,512,256]{2,1,0:T(8,128)(2,1)} %get-tuple-element.62), channel_id=1, source_target_pairs={{0,8},{8,16},{16,24},{1,9},{9,17},{17,25},{2,10},{10,18},{18,26},{... | collective-permute-start | bytes 1572872 | tf_op jit(solution)/shard_map/ppermute | solution.py:356
  (97 other events, 1169.5 us)
Sparse Core Ops, SparseCore 0:
  303.4 29.0 reduce-scatter.4
  463.3 27.7 reduce-scatter.2

commit v2 on v0

v2 whole, which is shorter than its diff:
```python
import functools
import math

import jax
import jax.numpy as jnp
from jax import lax
from jax.experimental import pallas as pl
from jax.experimental.pallas import tpu as pltpu
from jax.sharding import PartitionSpec as P

GW = 64
TAPS = 9
HALF = 256
BF = jnp.bfloat16
F32 = jnp.float32
MIB = 1024 * 1024

OUTER_INNER = [(0, 1), (1, 0), (2, 3), (3, 2)]
INNER = [(1, 2), (2, 1)]
OUTWARD = [(1, 0), (2, 3)]
INWARD = [(0, 1), (3, 2)]
ACROSS_CORE = [(i, i ^ 1) for i in range(8)]
ACROSS_X = [(i, i ^ 2) for i in range(8)]
ACROSS_Y = [(i, i ^ 4) for i in range(8)]


def dot(a, b):
    return jnp.dot(a, b, preferred_element_type=F32)


def dot_nt(a, b):
    return lax.dot_general(a, b, (((1,), (1,)), ((), ())), preferred_element_type=F32)


def call(kernel, out_shape, flops, nbytes, vmem=24, **kw):
    return pl.pallas_call(
        kernel,
        out_shape=out_shape,
        compiler_params=pltpu.CompilerParams(vmem_limit_bytes=vmem * MIB),
        cost_estimate=pl.CostEstimate(flops=flops, bytes_accessed=nbytes, transcendentals=0),
        **kw,
    )


def block_mask():
    rows = lax.broadcasted_iota(jnp.int32, (HALF, HALF), 0) // GW
    cols = lax.broadcasted_iota(jnp.int32, (HALF, HALF), 1) // GW
    return rows == cols


def spread_taps(w_ref, wide_ref, by_rows):
    mask = block_mask()
    for tap in range(TAPS):
        slab = w_ref[tap * GW : (tap + 1) * GW, :]
        square = jnp.concatenate([slab] * (HALF // GW), axis=0)
        square = jnp.where(mask, square, jnp.zeros_like(square))
        if by_rows:
            wide_ref[tap * HALF : (tap + 1) * HALF, :] = square
        else:
            wide_ref[:, tap * HALF : (tap + 1) * HALF] = square


def pad_field(value, pad_ref):
    side = value.shape[0]
    pad_ref[...] = jnp.zeros_like(pad_ref)
    pad_ref[1 : side + 1, 1 : side + 1] = value


STRIP = 2


def strips(pad_ref, flipped):
    side, images = pad_ref.shape[0] - 2, pad_ref.shape[2]
    rows = STRIP * side * images
    for part in range(side // STRIP):
        top = part * STRIP
        taps = [(2 - a, 2 - b) if flipped else (a, b) for a in range(3) for b in range(3)]
        patches = jnp.concatenate(
            [
                pad_ref[top + a : top + a + STRIP, b : b + side].reshape(rows, HALF)
                for a, b in taps
            ],
            axis=1,
        )
        yield slice(part * rows, (part + 1) * rows), patches


def convolve(x, w_ref, pad_ref, wide_ref, put):
    pad_field(x, pad_ref)
    spread_taps(w_ref, wide_ref, True)
    for here, patches in strips(pad_ref, False):
        pre = dot(patches, wide_ref[...])
        sig = jax.nn.sigmoid(pre)
        put(here, (pre * sig).astype(BF), sig * (1.0 + pre * (1.0 - sig)))


def convolve_back(gp, w_ref, pad_ref, wide_ref, put):
    pad_field(gp, pad_ref)
    spread_taps(w_ref, wide_ref, False)
    for here, patches in strips(pad_ref, True):
        put(here, dot_nt(patches, wide_ref[...]))


def conv_scratch(side, images):
    return [
        pltpu.VMEM((side + 2, side + 2, images, HALF), BF),
        pltpu.VMEM((TAPS * HALF, HALF), BF),
    ]


def place_vector(z, chip, core):
    return jnp.stack([z, chip, core]).astype(jnp.int32)


def with_place(kernel, grid, in_specs, out_specs, out_shape, flops, nbytes, scratch=(), vmem=24):
    return call(
        kernel,
        out_shape,
        flops,
        nbytes,
        vmem,
        grid_spec=pltpu.PrefetchScalarGridSpec(
            num_scalar_prefetch=1,
            grid=grid,
            in_specs=in_specs,
            out_specs=out_specs,
            scratch_shapes=list(scratch),
        ),
    )


def whole(shape):
    return pl.BlockSpec(shape, lambda s, p: (0,) * len(shape))


def rel_chip(slot, p):
    return p[0] ^ p[1] ^ slot


def fill_slots(p, refs, put):
    own, a, b, c, d, e = refs
    inner = (p[0] == 1) | (p[0] == 2)
    put(0, own)
    put(1, a)

    @pl.when(inner)
    def _():
        put(2, c)
        put(3, b)

    @pl.when(jnp.logical_not(inner))
    def _():
        put(2, d)
        put(3, e)


def put_columns(p, refs, sel, start, depth):
    width = sel.shape[3]

    def put(j, ref):
        sel[0, j, start : start + depth] = ref[:depth, :width]
        sel[1, j, start : start + depth] = ref[:depth, width:]

    fill_slots(p, refs, put)


def put_kernels(p, refs, conv, depth, tall):
    width = conv.shape[1]
    shard = conv.shape[0] // 4

    def put(j, ref):
        start = pl.multiple_of((p[0] ^ j) * shard, 16)
        conv[pl.ds(start, tall), :] = ref[depth : depth + tall, :width]
        start = pl.multiple_of((p[0] ^ j) * shard + shard - tall, 16)
        conv[pl.ds(start, tall), :] = ref[depth : depth + tall, width:]

    fill_slots(p, refs, put)


def first_layer(place, x, piece, side):
    rows, width = x.shape
    images = rows // (side * side)

    def kernel(p, x_ref, *refs):
        sent, keep, hid_t, slope, conv, hid, sel, pad_ref, wide_ref = refs[6:]
        step = pl.program_id(0)

        @pl.when(step == 0)
        def _():
            put_kernels(p, refs[:6], conv, width, piece[0].shape[0] - width)
            put_columns(p, refs[:6], sel, 0, width)
            for h in range(width // HALF):
                lanes = slice(h * HALF, (h + 1) * HALF)

                def put(here, value, slant, lanes=lanes):
                    hid[here, lanes] = value
                    hid_t[lanes, here] = value.T
                    slope[here, lanes] = slant

                grid = x_ref[:, lanes].reshape(side, side, images, HALF)
                convolve(grid, conv.at[:, lanes], pad_ref, wide_ref, put)

        sent[0] = dot(hid[...], sel[1 - p[2], step]).astype(BF)
        keep[0] = dot(hid[...], sel[p[2], step]).astype(BF)

    mix_spec = pl.BlockSpec((1, rows, width), lambda s, p: (rel_chip(s, p), 0, 0))
    mix_shape = jax.ShapeDtypeStruct((4, rows, width), BF)
    return with_place(
        kernel,
        (4,),
        [whole((rows, width))] + [whole(piece[0].shape)] * 6,
        (mix_spec, mix_spec, whole((width, rows)), whole((rows, width)), whole((TAPS * GW, width))),
        (
            mix_shape,
            mix_shape,
            jax.ShapeDtypeStruct((width, rows), BF),
            jax.ShapeDtypeStruct((rows, width), F32),
            jax.ShapeDtypeStruct((TAPS * GW, width), BF),
        ),
        16 * rows * width * width + 2 * rows * HALF * width * TAPS,
        30 * rows * width,
        [pltpu.VMEM((rows, width), BF), pltpu.VMEM((2, 4, width, width), BF)]
        + conv_scratch(side, images),
        60,
    )(place, x, *piece)


def next_layer(place, base, keep, other, first_x, second_y, first_y, second_x, piece, start, wide, side):
    rows, width = base.shape
    images = rows // (side * side)
    cut = rows // 2

    def kernel(p, b_ref, k_ref, o_ref, fx, sy, fy, sx, *refs):
        g_ref = refs[6]
        x_ref, hid, slope, conv, term = refs[7:12]
        hid_t, pad_ref, wide_ref = refs[12:]
        step = pl.program_id(0)

        @pl.when(step == 0)
        def _():
            put_kernels(p, refs[:6], conv, 0, tall)
            near, far = slice(0, cut), slice(cut, rows)
            x_ref[near, :] = (
                add(b_ref[near, :]) + add(k_ref[0, near, :], o_ref[0, near, :], fx[0], fy[...])
            ).astype(BF)
            x_ref[far, :] = (
                add(b_ref[far, :]) + add(k_ref[0, far, :], o_ref[0, far, :], sy[0], sx[...])
            ).astype(BF)
            for h in range(width // HALF):
                lanes = slice(h * HALF, (h + 1) * HALF)

                def put(here, value, slant, lanes=lanes):
                    hid[here, lanes] = value
                    hid_t[lanes, here] = value.T
                    slope[here, lanes] = slant

                grid = x_ref[:, lanes].reshape(side, side, images, HALF)
                convolve(grid, conv.at[:, lanes], pad_ref, wide_ref, put)

        term[0, :, :width] = dot(hid_t[...], g_ref[0]).astype(BF)
        term[0, :, width:] = dot(hid_t[...], g_ref[1]).astype(BF)

    all_spec = whole((rows, width))
    part = whole((1, rows, width))
    tall = piece[0].shape[0] - start
    block = math.gcd(start, 128)
    return with_place(
        kernel,
        (4,),
        [
            all_spec,
            part,
            part,
            whole((1, cut, width)),
            whole((1, cut, width)),
            whole((cut, width)),
            whole((cut, width)),
        ]
        + [pl.BlockSpec((block, 2 * width), lambda s, p: (start // block, 0))] * 6
        + [pl.BlockSpec((2, rows, width), lambda c, p: (c, 0, 0))],
        (
            all_spec,
            all_spec,
            all_spec,
            whole((TAPS * GW, width)),
            pl.BlockSpec((1, width, 2 * width), lambda c, p: (c, 0, 0)),
        ),
        (
            jax.ShapeDtypeStruct((rows, width), BF),
            jax.ShapeDtypeStruct((rows, width), BF),
            jax.ShapeDtypeStruct((rows, width), F32),
            jax.ShapeDtypeStruct((TAPS * GW, width), BF),
            jax.ShapeDtypeStruct((4, width, 2 * width), BF),
        ),
        16 * rows * width * width + 2 * rows * HALF * width * TAPS,
        32 * rows * width,
        [pltpu.VMEM((width, rows), BF)] + conv_scratch(side, images),
        60,
    )(place, base, keep, other, first_x, second_y, first_y, second_x, *piece, wide)


def output_gradient(place, wide, pieces, slope, conv, gradient, side):
    _, rows, width = wide.shape
    images = rows // (side * side)
    count = len(pieces)
    depth = width // count

    def kernel(p, s_ref, g_ref, *refs):
        c_ref, b_ref, gp_ref, o_ref, acc, sel, pad_ref, wide_ref = refs[6 * count :]
        step = pl.program_id(0)

        @pl.when(step == 0)
        def _():
            for k in range(count):
                put_columns(p, refs[6 * k : 6 * k + 6], sel, k * depth, depth)

        part = dot_nt(g_ref[0], sel[0, step]) + dot_nt(g_ref[1], sel[1, step])

        @pl.when(step == 0)
        def _():
            acc[...] = part

        @pl.when((step > 0) & (step < 3))
        def _():
            acc[...] += part

        @pl.when(step == 3)
        def _():
            gp_ref[...] = ((acc[...] + part) * s_ref[...]).astype(BF)
            for h in range(width // HALF):
                lanes = slice(h * HALF, (h + 1) * HALF)

                def put(here, field, lanes=lanes):
                    o_ref[here, lanes] = (b_ref[here, lanes].astype(F32) + field).astype(BF)

                grid = gp_ref[:, lanes].reshape(side, side, images, HALF)
                convolve_back(grid, c_ref.at[:, lanes], pad_ref, wide_ref, put)

    all_spec = whole((rows, width))
    return with_place(
        kernel,
        (4,),
        [all_spec, pl.BlockSpec((2, rows, width), lambda s, p: (p[0] ^ s, 0, 0))]
        + [whole((depth, 2 * width))] * (6 * count)
        + [whole((TAPS * GW, width)), all_spec],
        (all_spec, all_spec),
        (jax.ShapeDtypeStruct((rows, width), BF), jax.ShapeDtypeStruct((rows, width), BF)),
        16 * rows * width * width + 2 * rows * HALF * width * TAPS,
        32 * rows * width,
        [
            pltpu.VMEM((rows, width), F32),
            pltpu.VMEM((2, 4, width, width), BF),
            pltpu.VMEM((side + 2, side + 2, images, HALF), BF),
            pltpu.VMEM((HALF, TAPS * HALF), BF),
        ],
        60,
    )(place, slope, wide, *[a for piece in pieces for a in piece], conv, gradient)


def mix_columns(place, hidden, pieces):
    rows, width = hidden.shape
    count = len(pieces)
    depth = width // count

    def kernel(p, h_ref, *refs):
        sent, keep, sel = refs[6 * count :]
        step = pl.program_id(0)

        @pl.when(step == 0)
        def _():
            for k in range(count):
                put_columns(p, refs[6 * k : 6 * k + 6], sel, k * depth, depth)

        sent[0] = dot(h_ref[...], sel[1 - p[2], step]).astype(BF)
        keep[0] = dot(h_ref[...], sel[p[2], step]).astype(BF)

    mix_spec = pl.BlockSpec((1, rows, width), lambda s, p: (rel_chip(s, p), 0, 0))
    mix_shape = jax.ShapeDtypeStruct((4, rows, width), BF)
    return with_place(
        kernel,
        (4,),
        [whole(hidden.shape)] + [whole((depth, 2 * width))] * (6 * count),
        (mix_spec, mix_spec),
        (mix_shape, mix_shape),
        16 * rows * width * width,
        32 * rows * width,
        [pltpu.VMEM((2, 4, width, width), BF)],
        48,
    )(place, hidden, *[a for piece in pieces for a in piece])


def grad_pre(place, wide, piece, slope):
    rows, width = slope.shape

    def kernel(p, s_ref, mine_ref, other_ref, *refs):
        o_ref, sel, acc = refs[6:]
        step = pl.program_id(0)

        @pl.when(step == 0)
        def _():
            put_columns(p, refs[:6], sel, 0, width)

        part = dot_nt(mine_ref[0], sel[p[2], step]) + dot_nt(other_ref[0], sel[1 - p[2], step])

        @pl.when(step == 0)
        def _():
            acc[...] = part

        @pl.when((step > 0) & (step < 3))
        def _():
            acc[...] += part

        @pl.when(step == 3)
        def _():
            o_ref[...] = ((acc[...] + part) * s_ref[...]).astype(BF)

    return with_place(
        kernel,
        (4,),
        [whole((rows, width))]
        + [pl.BlockSpec((1, rows, width), lambda s, p: (rel_chip(s, p), 0, 0))] * 2
        + [whole((width, 2 * width))] * 6,
        whole((rows, width)),
        jax.ShapeDtypeStruct((rows, width), BF),
        16 * rows * width * width,
        32 * rows * width,
        [pltpu.VMEM((2, 4, width, width), BF), pltpu.VMEM((rows, width), F32)],
        60,
    )(place, slope, *wide, *piece)


def mix_grad(place, hidden_t, wide, extra=None):
    depth, rows = hidden_t.shape
    width = wide[0].shape[2]
    below = 0 if extra is None else extra.shape[1]

    def kernel(p, h_ref, mine_ref, other_ref, *refs):
        term = refs[-1]
        here = pl.multiple_of(p[2] * width, width)
        there = pl.multiple_of((1 - p[2]) * width, width)
        term[0, :depth, pl.ds(here, width)] = dot(h_ref[...], mine_ref[0]).astype(BF)
        term[0, :depth, pl.ds(there, width)] = dot(h_ref[...], other_ref[0]).astype(BF)
        if below:
            term[0, depth:, :] = refs[0][0]

    g_spec = pl.BlockSpec((1, rows, width), lambda c, p: (p[1] ^ c, 0, 0))
    specs = [whole((depth, rows)), g_spec, g_spec]
    args = [hidden_t, *wide]
    if below:
        specs.append(pl.BlockSpec((1, below, 2 * width), lambda c, p: (c, 0, 0)))
        args.append(extra)
    return with_place(
        kernel,
        (4,),
        specs,
        pl.BlockSpec((1, depth + below, 2 * width), lambda c, p: (c, 0, 0)),
        jax.ShapeDtypeStruct((4, depth + below, 2 * width), BF),
        16 * rows * depth * width,
        16 * (rows + depth) * width + 2 * rows * depth,
        (),
        60,
    )(place, *args)


def conv_grad(place, x, gp, shard, side, relative):
    rows, width = x.shape
    images = rows // (side * side)

    def kernel(p, x_ref, gp_ref, o_ref, pad_ref, full_ref):
        mask = block_mask()
        for k in range(width // HALF):
            lanes = slice(k * HALF, (k + 1) * HALF)
            pad_field(x_ref[:, lanes].reshape(side, side, images, HALF), pad_ref)
            turned = gp_ref[:, lanes].T
            for tap in range(TAPS):
                a, b = tap // 3, tap % 3
                square = dot(turned, pad_ref[a : a + side, b : b + side].reshape(rows, HALF)).T
                square = jnp.where(mask, square, 0.0)
                slab = square[:GW]
                for q in range(1, HALF // GW):
                    slab = slab + square[q * GW : (q + 1) * GW]
                full_ref[tap * GW : (tap + 1) * GW, lanes] = slab.astype(BF)
        for plane in range(4):
            index = plane ^ p[0] if relative else plane
            o_ref[index] = full_ref[plane * shard : (plane + 1) * shard, :]

    return with_place(
        kernel,
        (1,),
        [whole((rows, width))] * 2,
        whole((4, shard, width)),
        jax.ShapeDtypeStruct((4, shard, width), BF),
        2 * rows * HALF * width * TAPS,
        rows * width * 4,
        [
            pltpu.VMEM((side + 2, side + 2, images, HALF), BF),
            pltpu.VMEM((4 * shard, width), BF),
        ],
    )(place, x, gp)


def conv_field(gp, w, gradient, side):
    rows, width = gp.shape
    images = rows // (side * side)

    def kernel(gp_ref, w_ref, g_ref, o_ref, pad_ref, wide_ref):
        def put(here, field):
            o_ref[here, :] = (g_ref[here, :].astype(F32) + field).astype(BF)

        grid = gp_ref[...].reshape(side, side, images, HALF)
        convolve_back(grid, w_ref, pad_ref, wide_ref, put)

    half_spec = pl.BlockSpec((rows, HALF), lambda h: (0, h))
    return call(
        kernel,
        jax.ShapeDtypeStruct((rows, width), BF),
        2 * rows * HALF * width * TAPS,
        rows * width * 6,
        grid=(width // HALF,),
        in_specs=[half_spec, pl.BlockSpec((TAPS * GW, HALF), lambda h: (0, h)), half_spec],
        out_specs=half_spec,
        scratch_shapes=[
            pltpu.VMEM((side + 2, side + 2, images, HALF), BF),
            pltpu.VMEM((HALF, TAPS * HALF), BF),
        ],
    )(gp, w, gradient)


def finish(place, scale, last, first, convs, mix_shape, conv_shape):
    layers, depth, width = mix_shape
    _, shard, channels = conv_shape

    def kernel(p, last_ref, first_ref, *refs):
        del p
        mix_ref, conv_ref = refs[-2:]
        mix_ref[1] = last_ref[0].astype(F32) * scale
        mix_ref[0] = first_ref[0, :depth].astype(F32) * scale
        conv_ref[1, : shard // 2] = first_ref[0, depth:, :channels].astype(F32) * scale
        conv_ref[1, shard // 2 :] = first_ref[0, depth:, channels:].astype(F32) * scale
        total = refs[0][0].astype(F32)
        for ref in refs[1:4]:
            total = total + ref[...].astype(F32)
        conv_ref[0] = total * scale

    return with_place(
        kernel,
        (1,),
        [whole((1, depth, width)), whole((1, depth + shard // 2, width)), whole((1, shard, channels))]
        + [whole((shard, channels))] * 3,
        (whole(mix_shape), whole(conv_shape)),
        (jax.ShapeDtypeStruct(mix_shape, F32), jax.ShapeDtypeStruct(conv_shape, F32)),
        0,
        12 * depth * width,
        (),
        32,
    )(place, last, first, *convs)


class Clock:
    def __init__(self, token):
        self.token = token

    def gate(self, value):
        return lax.optimization_barrier((value, self.token))[0]

    def close(self, *values):
        self.token, *values = lax.optimization_barrier((self.token, *values))
        return values


def permute_dp(value, pairs):
    return lax.ppermute(value, "dp", pairs)


def permute_group(value, pairs):
    return lax.ppermute(value, "group", pairs)


def add(*terms):
    total = terms[0].astype(F32)
    for term in terms[1:]:
        total = total + term.astype(F32)
    return total


def gather_outer(own):
    return permute_dp(own, OUTER_INNER)


def gather_inner(own):
    return permute_dp(own, INNER)


def gather_second(a, b):
    return permute_dp(a, INNER), permute_dp(b, OUTWARD)


def gather_third(c):
    return permute_dp(c, OUTWARD)


def scatter_direct(parts):
    return [permute_dp(parts[i], [(j, j ^ i) for j in range(4)]) for i in (1, 2, 3)]


def plane_first(own):
    cut = own.shape[0] // 2
    return permute_group(own[:cut], ACROSS_X), permute_group(own[cut:], ACROSS_Y)


def plane_second(own, first_x, second_y):
    cut = own.shape[0] // 2
    return (
        permute_group(jnp.stack([own[:cut], first_x]), ACROSS_Y),
        permute_group(jnp.stack([own[cut:], second_y]), ACROSS_X),
    )


def plane_join(own, first_x, second_y, first_y, second_x):
    return jnp.stack(
        [
            own,
            jnp.concatenate([first_x, second_x[0]]),
            jnp.concatenate([first_y[0], second_y]),
            jnp.concatenate([first_y[1], second_x[1]]),
        ]
    )


def across_cores(value):
    return permute_group(value, ACROSS_CORE)


def sum_last(base, keep, other, first_x, second_y, first_y, second_x):
    cut = base.shape[0] // 2
    return jnp.concatenate(
        [
            add(base[:cut]) + add(keep[0, :cut], other[0, :cut], first_x[0], first_y),
            add(base[cut:]) + add(keep[0, cut:], other[0, cut:], second_y[0], second_x),
        ]
    ).astype(BF)


def sum_first(keep, other):
    rows = keep.shape[1]
    cut = rows // 2
    first = [add(keep[c, :cut], other[c, :cut]).astype(BF) for c in (1, 3)]
    second = [add(keep[c, cut:], other[c, cut:]).astype(BF) for c in (2, 3)]
    return (
        permute_group(jnp.stack(first), ACROSS_X),
        permute_group(jnp.stack(second), ACROSS_Y),
    )


def sum_second(keep, other, first_x, second_y):
    cut = keep.shape[1] // 2
    return (
        permute_group(add(keep[2, :cut], other[2, :cut], first_x[1]).astype(BF), ACROSS_Y),
        permute_group(add(keep[1, cut:], other[1, cut:], second_y[1]).astype(BF), ACROSS_X),
    )


def staged(images, cotangent, conv_weight, mix_weight):
    batch, side, _, width = images.shape
    shard = conv_weight.shape[1]
    rows = batch * side * side
    scale = 1.0 / math.sqrt(rows * lax.axis_size("dp"))
    z = lax.axis_index("dp")
    group = lax.axis_index("group")
    place = place_vector(z, group // 2, group % 2)
    clock = Clock(z)
    gate, close = clock.gate, clock.close

    def to_rows(field):
        return field.transpose(1, 2, 0, 3).reshape(rows, width)

    def from_rows(flat):
        return flat.reshape(side, side, batch, width).transpose(2, 0, 1, 3)

    tall = (shard // 2 + 15) // 16 * 16

    def with_kernels(weights, layer):
        kernels = conv_weight[layer]
        below = jnp.concatenate([kernels[:tall], kernels[shard - tall :]], axis=1)
        return jnp.concatenate([weights, below])

    depth = width // 2
    own0 = with_kernels(mix_weight[0], 0)
    own1, own2 = with_kernels(mix_weight[1, :depth], 1), mix_weight[1, depth:]
    a0, b0 = gather_outer(own0), gather_inner(own0)
    x0 = to_rows(images)
    a0, b0, x0 = close(a0, b0, x0)

    g2 = to_rows(gate(cotangent))
    wide2 = lax.all_gather(g2, "group", axis=0)
    c0, d0 = gather_second(a0, b0)
    c0, d0 = close(c0, d0)

    e0 = gather_third(c0)
    b1, b2 = gather_inner(gate(own1)), gather_inner(gate(own2))
    e0, b1, b2 = close(e0, b1, b2)
    p0 = (own0, a0, b0, c0, d0, e0)

    a1 = gather_outer(gate(own1))
    sent, keep, hidden0_t, slope0, conv0 = first_layer(place, x0, p0, side)
    a1, sent, keep, hidden0_t, slope0, conv0 = close(a1, sent, keep, hidden0_t, slope0, conv0)

    a2 = gather_outer(gate(own2))
    other = across_cores(sent)
    a2, other = close(a2, other)

    c1, d1 = gather_second(a1, b1)
    c2, d2 = gather_second(a2, b2)
    sx, sy = sum_first(keep, other)
    c1, d1, c2, d2, sx, sy = close(c1, d1, c2, d2, sx, sy)

    e1 = gather_third(c1)
    ty, tx = sum_second(keep, other, sx, sy)
    ty, tx, e1 = close(ty, tx, e1)
    p1 = (own1, a1, b1, c1, d1, e1)

    e2 = gather_third(gate(c2))
    x1, hidden1, slope1, conv1, m1 = next_layer(
        place, x0, keep, other, sx, sy, ty, tx, p1, depth, wide2, side
    )
    x1, hidden1, slope1, conv1, m1, e2 = close(x1, hidden1, slope1, conv1, m1, e2)
    p2 = (own2, a2, b2, c2, d2, e2)
    last = lax.psum_scatter(m1, "dp", scatter_dimension=0, tiled=True)

    gp1, g1 = output_gradient(place, wide2, [p1, p2], slope1, conv1, g2, side)
    ax, ay = plane_first(g1)
    gp1, g1, ax, ay = close(gp1, g1, ax, ay)
    ayy, axx = plane_second(g1, ax, ay)
    mine = plane_join(g1, ax, ay, ayy, axx)
    terms1 = conv_grad(place, x1, gp1, shard, side, False)
    mine, terms1 = close(mine, terms1)
    wide1 = (mine, across_cores(mine))
    below = jnp.concatenate([terms1[:, : shard // 2], terms1[:, shard // 2 :]], axis=2)
    m0 = mix_grad(place, hidden0_t, wide1, below)
    m0, last = close(m0, last)
    first = lax.psum_scatter(m0, "dp", scatter_dimension=0, tiled=True)

    gp0 = grad_pre(place, wide1, p0, slope0)
    terms0 = conv_grad(place, x0, gp0, shard, side, True)
    gp0, terms0 = close(gp0, terms0)
    cs = scatter_direct(terms0)

    sent, keep = mix_columns(place, gate(hidden1), [p1, p2])
    other = across_cores(sent)
    keep, other = close(keep, other)
    sx, sy = sum_first(keep, other)
    g0 = conv_field(gp0, conv0, g1, side)
    sx, sy, g0, *cs = close(sx, sy, g0, *cs)
    ty, tx = sum_second(keep, other, sx, sy)
    features = from_rows(sum_last(x1, keep, other, sx, sy, ty, tx))
    grad_images = from_rows(g0)
    grad_mix, grad_conv = finish(
        place, scale, last, first, [terms0, *cs], mix_weight.shape, conv_weight.shape
    )
    return features, grad_images, grad_conv, grad_mix


def make_patches(field):
    side_cells = field.shape[1]
    padded = jnp.pad(field, ((0, 0), (1, 1), (1, 1), (0, 0)))
    tap_list = [
        padded[:, row_shift : row_shift + side_cells, col_shift : col_shift + side_cells, :]
        for row_shift in range(3)
        for col_shift in range(3)
    ]
    return jnp.stack(tap_list, axis=3).reshape(-1, 9, field.shape[3])


def fold_patches(pieces, batch_size, side_cells):
    pieces = pieces.reshape(batch_size, side_cells, side_cells, 9, pieces.shape[2])
    summed = jnp.zeros((batch_size, side_cells + 2, side_cells + 2, pieces.shape[4]), F32)
    for tap_index in range(9):
        row_shift = tap_index // 3
        col_shift = tap_index % 3
        summed = summed + jnp.pad(
            pieces[:, :, :, tap_index, :],
            ((0, 0), (row_shift, 2 - row_shift), (col_shift, 2 - col_shift), (0, 0)),
        )
    return summed[:, 1 : side_cells + 1, 1 : side_cells + 1, :]


def silu_slope(value):
    sigmoid_v = jax.nn.sigmoid(value)
    return sigmoid_v * (1.0 + value * (1.0 - sigmoid_v))


def general(images, cotangent, conv_weight, mix_weight):
    batch_size, side_cells, _, local_width = images.shape
    local_groups = local_width // GW
    row_count = batch_size * side_cells * side_cells
    layer_count = conv_weight.shape[0]
    grad_scale = 1.0 / math.sqrt(row_count * lax.axis_size("dp"))
    fetched = [
        (
            lax.all_gather(conv_weight[layer], "dp", axis=0, tiled=True),
            lax.all_gather(mix_weight[layer], "dp", axis=1, tiled=True),
        )
        for layer in range(layer_count)
    ]
    current = images
    saved = []
    for layer in range(layer_count):
        conv_full, mix_full = fetched[layer]
        tap_weights = conv_full.reshape(9 * GW, local_groups, GW).transpose(1, 0, 2)
        flat = make_patches(current).reshape(row_count, 9, local_groups, GW)
        patches = flat.transpose(0, 2, 1, 3).reshape(row_count, local_groups, 9 * GW)
        pre_act = jnp.einsum(
            "pgk,gko->pgo", patches, tap_weights, preferred_element_type=F32
        ).reshape(row_count, local_width)
        hidden = jax.nn.silu(pre_act).astype(BF)
        mixed = lax.psum_scatter(
            jnp.dot(hidden, mix_full, preferred_element_type=F32).astype(BF),
            "group",
            scatter_dimension=1,
            tiled=True,
        ).astype(F32)
        saved.append((patches, pre_act, hidden, tap_weights, mix_full))
        current = (
            (current.reshape(row_count, local_width).astype(F32) + mixed)
            .astype(BF)
            .reshape(images.shape)
        )
    gradient = cotangent
    conv_grads = []
    mix_grads = []
    for layer in reversed(range(layer_count)):
        patches, pre_act, hidden, tap_weights, mix_full = saved[layer]
        flat_grad = gradient.reshape(row_count, local_width)
        grad_wide = lax.all_gather(flat_grad, "group", axis=1, tiled=True)
        mix_term = lax.dot_general(
            hidden, grad_wide, (((0,), (0,)), ((), ())), preferred_element_type=F32
        )
        grad_hidden = dot_nt(grad_wide, mix_full)
        grad_pre = (
            (grad_hidden * silu_slope(pre_act)).astype(BF).reshape(row_count, local_groups, GW)
        )
        conv_term = jnp.einsum("pgk,pgo->gko", patches, grad_pre, preferred_element_type=F32)
        conv_term = conv_term.transpose(1, 0, 2).reshape(9 * GW, local_width)
        patch_grad = jnp.einsum("pgo,gko->pgk", grad_pre, tap_weights, preferred_element_type=F32)
        patch_grad = (
            patch_grad.reshape(row_count, local_groups, 9, GW)
            .transpose(0, 2, 1, 3)
            .reshape(row_count, 9, local_width)
        )
        field_grad = fold_patches(patch_grad, batch_size, side_cells)
        conv_summed, mix_summed = (
            lax.psum_scatter(
                conv_term.astype(BF), "dp", scatter_dimension=0, tiled=True
            ).astype(F32),
            lax.psum_scatter(
                mix_term.astype(BF), "dp", scatter_dimension=1, tiled=True
            ).astype(F32),
        )
        conv_grads.insert(0, conv_summed * grad_scale)
        mix_grads.insert(0, mix_summed * grad_scale)
        gradient = (gradient.astype(F32) + field_grad).astype(BF)
    return (current, gradient, jnp.stack(conv_grads), jnp.stack(mix_grads))


def solution(mesh):
    fits = mesh.shape["dp"] == 4 and mesh.shape["group"] == 8
    return jax.shard_map(
        staged if fits else general,
        mesh=mesh,
        in_specs=(
            P("dp", None, None, "group"),
            P("dp", None, None, "group"),
            P(None, "dp", "group"),
            P(None, "group", "dp"),
        ),
        out_specs=(
            P("dp", None, None, "group"),
            P("dp", None, None, "group"),
            P(None, "dp", "group"),
            P(None, "group", "dp"),
        ),
        check_vma=False,
    )
```

time: 791 us -> 400 us (0.51); the launches traced: 777 us -> 398 us
  local copies, waits for them, and re-layouts: 303 us -> 17.3 us
  matrix products: 102 us -> 0 us
  Pallas kernels: 0 us -> 89 us
  waiting for transfers between devices: 285 us -> 224 us
  starting transfers between devices: 0.87 us -> 41 us
  blocking collectives: 38.4 us -> 0 us
  other arithmetic: 33.4 us -> 11.7 us
    ppermute x0 -> x33, waiting for transfers between devices: none -> 208 us  [the longest x18 142 us: permute_dp(): return lax.ppermute(value, 'dp', pairs)]
    reduce_scatter x6 -> x2, waiting for transfers between devices: 213 us -> 16.2 us  [the longest x1 9.89 us: staged(): first = lax.psum_scatter(m0, 'dp', scatter_dimension=0, tiled=True)]
    another operation x22 -> x1, local copies, waits for them, and re-layouts: 131 us -> 0.07 us  [plane_second(): jnp.stack([own[:cut], first_x])]
    dot_general x12 -> x0, matrix products: 102 us -> none  [the longest x2 19.7 us: per_device(): lax.dot_general(hidden, grad_wide, (((0,), (0,)), ((), ())), preferred_el...]
    pallas_call x0 -> x10, Pallas kernels: none -> 89 us  [the longest x1 16 us: output_gradient(): with_place(kernel, (4,), [all_spec, pl.BlockSpec((2, rows, width), lambda...]
    all_gather x4 -> x1, waiting for transfers between devices: 70.3 us -> 0.02 us  [staged(): wide2 = lax.all_gather(g2, 'group', axis=0)]
    reshape x2 -> x0, local copies, waits for them, and re-layouts: 52.2 us -> none  [per_device(): patch_grad.reshape(row_count, local_groups, 9, GW).transpose(0, 2, 1, 3)]
    ppermute x0 -> x33, starting transfers between devices: none -> 40.9 us  [the longest x18 29.1 us: permute_dp(): return lax.ppermute(value, 'dp', pairs)]
  transfers between devices with their start and end apart: 10 -> 36, of which waited for: 6 -> 22; matrix products, arithmetic and copies ran while one was open for 41% -> 4% of each run, Pallas kernels for 0% -> 22%
where the time goes in v2:
time: 400 us; the launch traced here: 398 us
  waiting for transfers between devices  224 us (56%)
  Pallas kernels  89 us (22%)
  starting transfers between devices  41 us (10%)
  local copies, waits for them, and re-layouts  17.3 us (4%)
  between operations  14.4 us (4%)
  other arithmetic  11.7 us (3%)
    ppermute x18, waiting for transfers between devices, permute_dp(): return lax.ppermute(value, 'dp', pairs)  142 us
    ppermute x15, waiting for transfers between devices, permute_group(): return lax.ppermute(value, 'group', pairs)  65.3 us
    ppermute x18, starting transfers between devices, permute_dp(): return lax.ppermute(value, 'dp', pairs)  29.1 us
    pallas_call x1, Pallas kernels, output_gradient(): with_place(kernel, (4,), [all_spec, pl.BlockSpec((2, rows, width), lambda...  16 us
    pallas_call x1, Pallas kernels, next_layer(): with_place(kernel, (4,), [all_spec, part, part, whole((1, cut, width)), w...  14.9 us
    pallas_call x1, Pallas kernels, first_layer(): with_place(kernel, (4,), [whole((rows, width))] + [whole(piece[0].shape)]...  13.9 us
    pallas_call x1, Pallas kernels, grad_pre(): with_place(kernel, (4,), [whole((rows, width))] + [pl.BlockSpec((1, rows,...  12.7 us
    ppermute x15, starting transfers between devices, permute_group(): return lax.ppermute(value, 'group', pairs)  11.9 us
  transfers between devices with their start and end apart: 36, of which 22 were waited for; matrix products, arithmetic and copies ran while one was open for 4% of the time, Pallas kernels for 22%

profile of v2, /device:TPU:0, one launch (start us, length us, event | category | flops | bytes accessed | tf_op | source)
XLA Modules:
  0.0 397.5 jit_solution(18102205344163121542)
XLA Ops:
  9.7 1.8 collective-permute-start.1
  11.5 4.8 %collective-permute-start = (bf16[592,1024]{1,0:T(8,128)(2,1)S(1)}, bf16[592,1024]{1,0:T(8,128)(2,1)}, u32[]{:S(2)}, u32[]{:S(2)}) collective-permute-start(bf16[592,1024]{1,0:T(8,128)(2,1)S(1)} %maximum_maximum_fusion.refs_0_), channel_id=1, source_target_pairs={{0,8},{8,0},{16,24},{24,16},{1,9},{9,1},{17,25},{25,17},{2,10},{10... | collective-permute-start | bytes 3637256 | tf_op jit(solution)/shard_map/ppermute | solution.py:572
  16.3 1.5 copy.13
  17.9 24.9 %collective-permute-done.refs_1_ = bf16[592,1024]{1,0:T(8,128)(2,1)} collective-permute-done((bf16[592,1024]{1,0:T(8,128)(2,1)S(1)}, bf16[592,1024]{1,0:T(8,128)(2,1)}, u32[]{:S(2)}, u32[]{:S(2)}) %collective-permute-start) | collective-permute-done | bytes 1212448 | tf_op jit(solution)/shard_map/ppermute | solution.py:572
  42.8 2.8 copy.14
  45.7 1.7 collective-permute-start.2
  48.7 28.3 %collective-permute-done.3.refs_4_ = bf16[592,1024]{1,0:T(8,128)(2,1)S(1)} collective-permute-done((bf16[592,1024]{1,0:T(8,128)(2,1)}, bf16[592,1024]{1,0:T(8,128)(2,1)S(1)}, u32[]{:S(2)}, u32[]{:S(2)}) %collective-permute-start.3) | collective-permute-done | bytes 1212448 | tf_op jit(solution)/shard_map/ppermute | solution.py:572
  80.2 1.5 collective-permute-start.6
  81.7 25.1 %collective-permute-done.4.refs_5_ = bf16[592,1024]{1,0:T(8,128)(2,1)} collective-permute-done((bf16[592,1024]{1,0:T(8,128)(2,1)}, bf16[592,1024]{1,0:T(8,128)(2,1)}, u32[]{:S(2)}, u32[]{:S(2)}) %collective-permute-start.4) | collective-permute-done | bytes 1212448 | tf_op jit(solution)/shard_map/ppermute | solution.py:572
  106.9 4.8 %collective-permute-start.7 = (bf16[336,1024]{1,0:T(8,128)(2,1)S(1)}, bf16[336,1024]{1,0:T(8,128)(2,1)S(1)}, u32[]{:S(2)}, u32[]{:S(2)}) collective-permute-start(bf16[336,1024]{1,0:T(8,128)(2,1)S(1)} %maximum_maximum_fusion.1.refs_0_), channel_id=1, source_target_pairs={{0,8},{8,0},{16,24},{24,16},{1,9},{9,1},{17,25},{25,17},{2,10},{10... | collective-permute-start | bytes 2064392 | tf_op jit(solution)/shard_map/ppermute | solution.py:572
  112.3 13.9 %shard_map.75 = (bf16[4,1024,512]{2,1,0:T(8,128)(2,1)}, bf16[4,1024,512]{2,1,0:T(8,128)(2,1)}, bf16[512,1024]{1,0:T(8,128)(2,1)}, f32[1024,512]{1,0:T(8,128)}, bf16[576,512]{1,0:T(8,128)(2,1)}) custom-call(s32[3]{0:T(128)} %pad_add_fusion.p, bf16[1024,512]{1,0:T(8,128)(2,1)} %bitcast.76, bf16[592,1024]{1,0:T(8,128)(2,1)} %copy-done.32, ...), custom_call_target="tpu_custom_call" | custom-call | flops 6710886400 | bytes 15728640 | tf_op jit(solution)/shard_map/pallas_call | solution.py:208
  127.8 13.3 %collective-permute-done.8.refs_7_ = bf16[256,1024]{1,0:T(8,128)(2,1)S(1)} collective-permute-done((bf16[256,1024]{1,0:T(8,128)(2,1)S(1)}, bf16[256,1024]{1,0:T(8,128)(2,1)S(1)}, u32[]{:S(2)}, u32[]{:S(2)}) %collective-permute-start.8) | collective-permute-done | bytes 524320 | tf_op jit(solution)/shard_map/ppermute | solution.py:572
  141.1 3.7 add_convert_fusion.9
  144.9 1.7 collective-permute-start.14
  146.7 1.5 collective-permute-start.15
  150.2 2.2 collective-permute-done.13.refs_10_
  153.0 13.6 %collective-permute-done.11.refs_4_ = bf16[336,1024]{1,0:T(8,128)(2,1)S(1)} collective-permute-done((bf16[336,1024]{1,0:T(8,128)(2,1)S(1)}, bf16[336,1024]{1,0:T(8,128)(2,1)S(1)}, u32[]{:S(2)}, u32[]{:S(2)}) %collective-permute-start.11) | collective-permute-done | bytes 688160 | tf_op jit(solution)/shard_map/ppermute | solution.py:572
  166.6 2.6 collective-permute-done.14.fx
  169.2 1.5 collective-permute-done.15.sy
  172.0 1.6 fusion.5
  174.2 1.6 collective-permute-start.16
  175.8 9.8 %collective-permute-done.17.sx = bf16[512,512]{1,0:T(8,128)(2,1)S(1)} collective-permute-done((bf16[512,512]{1,0:T(8,128)(2,1)S(1)}, bf16[512,512]{1,0:T(8,128)(2,1)S(1)}, u32[]{:S(2)}, u32[]{:S(2)}) %collective-permute-start.17) | collective-permute-done | bytes 524320 | tf_op jit(solution)/shard_map/ppermute | solution.py:576
  185.7 9.5 %collective-permute-done.18.refs_5_ = bf16[336,1024]{1,0:T(8,128)(2,1)S(1)} collective-permute-done((bf16[336,1024]{1,0:T(8,128)(2,1)S(1)}, bf16[336,1024]{1,0:T(8,128)(2,1)S(1)}, u32[]{:S(2)}, u32[]{:S(2)}) %collective-permute-start.18) | collective-permute-done | bytes 688160 | tf_op jit(solution)/shard_map/ppermute | solution.py:572
  195.3 1.5 collective-permute-start.19
  196.8 14.9 %shard_map.76 = (bf16[1024,512]{1,0:T(8,128)(2,1)}, bf16[1024,512]{1,0:T(8,128)(2,1)}, f32[1024,512]{1,0:T(8,128)}, bf16[576,512]{1,0:T(8,128)(2,1)}, bf16[4,512,1024]{2,1,0:T(8,128)(2,1)}) custom-call(s32[3]{0:T(128)} %pad_add_fusion.p, bf16[1024,512]{1,0:T(8,128)(2,1)} %bitcast.77, bf16[4,1024,512]{2,1,0:T(8,128)(2,1)} %get-tuple-element.113.k_ref, ...), custom_call_target="tpu_custom_call" | custom-call | flops 6710886400 | bytes 16777216 | tf_op jit(solution)/shard_map/pallas_call | solution.py:267
  212.5 16.0 %shard_map.77 = (bf16[1024,512]{1,0:T(8,128)(2,1)}, bf16[1024,512]{1,0:T(8,128)(2,1)}) custom-call(s32[3]{0:T(128)} %pad_add_fusion.p, f32[1024,512]{1,0:T(8,128)} %get-tuple-element.134.s_ref, bf16[8,1024,512]{2,1,0:T(8,128)(2,1)} %all-gather.2.cloned.1.call-done.refs_6_.g_ref, bf16[336,1024]{1,0:T(8,128)(2,1)} %copy-done.2, bf16[336,1024]{1,0:T(8,128)(2,1)} %copy-done.12, ...), custom_call_target="tpu_custom_call" | custom-call | flops 6710886400 | bytes 16777216 | tf_op jit(solution)/shard_map/pallas_call | solution.py:340
  230.6 9.6 %collective-permute-done.21 = bf16[512,512]{1,0:T(8,128)(2,1)S(1)} collective-permute-done((bf16[512,512]{1,0:T(8,128)(2,1)S(1)}, bf16[512,512]{1,0:T(8,128)(2,1)S(1)}, u32[]{:S(2)}, u32[]{:S(2)}) %collective-permute-start.21) | collective-permute-done | bytes 524320 | tf_op jit(solution)/shard_map/ppermute | solution.py:576
  240.3 1.5 collective-permute-done.20
  242.2 1.9 collective-permute-start.23
  244.1 3.3 shard_map.78
  247.5 15.8 %collective-permute-done.22 = bf16[2,512,512]{2,1,0:T(8,128)(2,1)S(1)} collective-permute-done((bf16[2,512,512]{2,1,0:T(8,128)(2,1)S(1)}, bf16[2,512,512]{2,1,0:T(8,128)(2,1)S(1)}, u32[]{:S(2)}, u32[]{:S(2)}) %collective-permute-start.22) | collective-permute-done | bytes 1048608 | tf_op jit(solution)/shard_map/ppermute | solution.py:576
  264.4 1.9 copy-done.30
  267.2 4.5 %collective-permute-done.24.other_ref = bf16[4,1024,512]{2,1,0:T(8,128)(2,1)} collective-permute-done((bf16[4,1024,512]{2,1,0:T(8,128)(2,1)S(1)}, bf16[4,1024,512]{2,1,0:T(8,128)(2,1)}, u32[]{:S(2)}, u32[]{:S(2)}) %collective-permute-start.24) | collective-permute-done | bytes 4194336 | tf_op jit(solution)/shard_map/ppermute | solution.py:576
  271.7 9.9 %shard_map.79 = bf16[4,584,1024]{2,1,0:T(8,128)(2,1)} custom-call(s32[3]{0:T(128)} %pad_add_fusion.p, bf16[512,1024]{1,0:T(8,128)(2,1)} %get-tuple-element.146.h_ref, bf16[4,1024,512]{2,1,0:T(8,128)(2,1)} %copy-done.30, bf16[4,1024,512]{2,1,0:T(8,128)(2,1)} %collective-permute-done.24.other_ref, bf16[4,72,1024]{2,1,0:T(8,128)(2,1)} %pad_maximum_fusion.8.refs_0_), custom_call_target="tpu_custom_call" | custom-call | flops 4294967296 | bytes 13631488 | tf_op jit(solution)/shard_map/pallas_call | solution.py:452
  281.6 6.4 %reduce-scatter.3.cloned.1.call-done.last_ref = bf16[1,512,1024]{2,1,0:T(8,128)(2,1)} async-done(((bf16[4,512,1024]{2,1,0:T(8,128)(2,1)}), bf16[1,512,1024]{2,1,0:T(8,128)(2,1)}) %reduce-scatter.3.cloned.1.call-update) | async-done | bytes 1048592 | tf_op jit(solution)/shard_map/reduce_scatter | solution.py:728
  288.0 12.7 %shard_map.80.gp_ref = bf16[1024,512]{1,0:T(8,128)(2,1)} custom-call(s32[3]{0:T(128)} %pad_add_fusion.p, f32[1024,512]{1,0:T(8,128)} %get-tuple-element.151.s_ref, bf16[4,1024,512]{2,1,0:T(8,128)(2,1)} %copy-done.30, bf16[4,1024,512]{2,1,0:T(8,128)(2,1)} %collective-permute-done.24.other_ref, bf16[592,1024]{1,0:T(8,128)(2,1)} %copy-done.32, ...), custom_call_target="tpu_custom_call" | custom-call | flops 4294967296 | bytes 16777216 | tf_op jit(solution)/shard_map/pallas_call | solution.py:417
  302.0 3.4 shard_map.81.refs_0_
  305.5 8.7 %shard_map.82 = (bf16[4,1024,512]{2,1,0:T(8,128)(2,1)}, bf16[4,1024,512]{2,1,0:T(8,128)(2,1)}) custom-call(s32[3]{0:T(128)S(1)} %copy-done.19, bf16[1024,512]{1,0:T(8,128)(2,1)} %get-tuple-element.154.h_ref, bf16[336,1024]{1,0:T(8,128)(2,1)S(1)} %copy-done.3, bf16[336,1024]{1,0:T(8,128)(2,1)S(1)} %copy-done.13, bf16[336,1024]{1,0:T(8,128)(2,1)S(1)} %copy-done.11, ...), custom_call_target="tpu_custom_call" | custom-call | flops 4294967296 | bytes 16777216 | tf_op jit(solution)/shard_map/pallas_call | solution.py:379
  314.2 7.4 %collective-permute-done.25 = bf16[4,1024,512]{2,1,0:T(8,128)(2,1)S(1)} collective-permute-done((bf16[4,1024,512]{2,1,0:T(8,128)(2,1)}, bf16[4,1024,512]{2,1,0:T(8,128)(2,1)S(1)}, u32[]{:S(2)}, u32[]{:S(2)}) %collective-permute-start.25) | collective-permute-done | bytes 4194336 | tf_op jit(solution)/shard_map/ppermute | solution.py:576
  321.6 2.1 add_convert_fusion.3
  326.8 2.5 collective-permute-start.30
  331.3 3.1 shard_map.83
  334.4 4.3 %collective-permute-done.30.refs_3_ = bf16[144,512]{1,0:T(8,128)(2,1)S(1)} collective-permute-done((bf16[144,512]{1,0:T(8,128)(2,1)S(1)}, bf16[144,512]{1,0:T(8,128)(2,1)S(1)}, u32[]{:S(2)}, u32[]{:S(2)}) %collective-permute-start.30) | collective-permute-done | bytes 147488 | tf_op jit(solution)/shard_map/ppermute | solution.py:572
  338.8 21.0 %collective-permute-done.29.refs_2_ = bf16[144,512]{1,0:T(8,128)(2,1)S(1)} collective-permute-done((bf16[144,512]{1,0:T(8,128)(2,1)S(1)}, bf16[144,512]{1,0:T(8,128)(2,1)S(1)}, u32[]{:S(2)}, u32[]{:S(2)}) %collective-permute-start.29) | collective-permute-done | bytes 147488 | tf_op jit(solution)/shard_map/ppermute | solution.py:572
  360.9 12.5 %collective-permute-done.31 = bf16[512,512]{1,0:T(8,128)(2,1)S(1)} collective-permute-done((bf16[512,512]{1,0:T(8,128)(2,1)S(1)}, bf16[512,512]{1,0:T(8,128)(2,1)S(1)}, u32[]{:S(2)}, u32[]{:S(2)}) %collective-permute-start.31) | collective-permute-done | bytes 524320 | tf_op jit(solution)/shard_map/ppermute | solution.py:576
  374.3 2.5 copy_bitcast_fusion
  376.8 9.9 %reduce-scatter.5.cloned.1.call-done.first_ref = bf16[1,584,1024]{2,1,0:T(8,128)(2,1)} async-done(((bf16[4,584,1024]{2,1,0:T(8,128)(2,1)}), bf16[1,584,1024]{2,1,0:T(8,128)(2,1)}) %reduce-scatter.5.cloned.1.call-update) | async-done | bytes 1196048 | tf_op jit(solution)/shard_map/reduce_scatter | solution.py:741
  388.0 3.0 shard_map.84
  (155 shorter events, 29.0 us)
Async XLA Ops:
  7.2 189.6 %all-gather.2.cloned.1.call-start = ((), (), s32[]{:S(2)}) async-start(), calls=%async_computation.2 | async-start | bytes 9437184 | tf_op jit(solution)/shard_map/all_gather | solution.py:695
  9.7 35.9 %copy-start.32 = (bf16[592,1024]{1,0:T(8,128)(2,1)}, bf16[592,1024]{1,0:T(8,128)(2,1)S(1)}, u32[]{:S(2)}) copy-start(bf16[592,1024]{1,0:T(8,128)(2,1)S(1)} %maximum_maximum_fusion.refs_0_) | copy-start | bytes 3637252
  9.7 8.1 %collective-permute-start.1 = (bf16[592,1024]{1,0:T(8,128)(2,1)S(1)}, bf16[592,1024]{1,0:T(8,128)(2,1)}, u32[]{:S(2)}, u32[]{:S(2)}) collective-permute-start(bf16[592,1024]{1,0:T(8,128)(2,1)S(1)} %maximum_maximum_fusion.refs_0_), channel_id=1, source_target_pairs={{8,16},{16,8},{9,17},{17,9},{10,18},{18,10},{11,19},{19,11},{12,20... | collective-permute-start | bytes 3637256 | tf_op jit(solution)/shard_map/ppermute | solution.py:572
  11.5 31.3 %collective-permute-start = (bf16[592,1024]{1,0:T(8,128)(2,1)S(1)}, bf16[592,1024]{1,0:T(8,128)(2,1)}, u32[]{:S(2)}, u32[]{:S(2)}) collective-permute-start(bf16[592,1024]{1,0:T(8,128)(2,1)S(1)} %maximum_maximum_fusion.refs_0_), channel_id=1, source_target_pairs={{0,8},{8,0},{16,24},{24,16},{1,9},{9,1},{17,25},{25,17},{2,10},{10... | collective-permute-start | bytes 3637256 | tf_op jit(solution)/shard_map/ppermute | solution.py:572
  17.9 61.5 %copy-start.36 = (bf16[2,512,1024]{2,1,0:T(8,128)(2,1)S(1)}, bf16[2,512,1024]{2,1,0:T(8,128)(2,1)}, u32[]{:S(2)}) copy-start(bf16[2,512,1024]{2,1,0:T(8,128)(2,1)} %param.7) | copy-start | bytes 6291460
  45.7 242.3 %reduce-scatter.3.cloned.1.call-start = ((), (), s32[]{:S(2)}) async-start(), calls=%async_computation.3 | async-start | bytes 5242880 | tf_op jit(solution)/shard_map/reduce_scatter | solution.py:728
  45.7 3.0 collective-permute-start.2
  47.4 29.6 %collective-permute-start.3 = (bf16[592,1024]{1,0:T(8,128)(2,1)}, bf16[592,1024]{1,0:T(8,128)(2,1)S(1)}, u32[]{:S(2)}, u32[]{:S(2)}) collective-permute-start(bf16[592,1024]{1,0:T(8,128)(2,1)} %collective-permute-done.1.refs_2_), channel_id=1, source_target_pairs={{8,0},{16,24},{9,1},{17,25},{10,2},{18,26},{11,3},{19,27},{12,4},{... | collective-permute-start | bytes 3637256 | tf_op jit(solution)/shard_map/ppermute | solution.py:572
  78.1 28.8 %collective-permute-start.4 = (bf16[592,1024]{1,0:T(8,128)(2,1)}, bf16[592,1024]{1,0:T(8,128)(2,1)}, u32[]{:S(2)}, u32[]{:S(2)}) collective-permute-start(bf16[592,1024]{1,0:T(8,128)(2,1)} %collective-permute-done.2.refs_3_), channel_id=1, source_target_pairs={{8,0},{16,24},{9,1},{17,25},{10,2},{18,26},{11,3},{19,27},{12,4},{... | collective-permute-start | bytes 3637256 | tf_op jit(solution)/shard_map/ppermute | solution.py:572
  79.4 46.9 %copy-start.16 = (bf16[256,1024]{1,0:T(8,128)(2,1)}, bf16[256,1024]{1,0:T(8,128)(2,1)S(1)}, u32[]{:S(2)}) copy-start(bf16[256,1024]{1,0:T(8,128)(2,1)S(1)} %get-tuple-element.106.refs_6_) | copy-start | bytes 1572868
  79.5 46.7 %copy-start.2 = (bf16[336,1024]{1,0:T(8,128)(2,1)}, bf16[336,1024]{1,0:T(8,128)(2,1)S(1)}, u32[]{:S(2)}) copy-start(bf16[336,1024]{1,0:T(8,128)(2,1)S(1)} %maximum_maximum_fusion.1.refs_0_) | copy-start | bytes 2064388
  79.5 2.2 collective-permute-start.5
  80.2 1.5 collective-permute-start.6
  81.7 66.4 %copy-start.10 = (bf16[336,1024]{1,0:T(8,128)(2,1)}, bf16[336,1024]{1,0:T(8,128)(2,1)S(1)}, u32[]{:S(2)}) copy-start(bf16[336,1024]{1,0:T(8,128)(2,1)S(1)} %collective-permute-done.5.refs_2_) | copy-start | bytes 2064388
  106.9 19.3 %collective-permute-start.7 = (bf16[336,1024]{1,0:T(8,128)(2,1)S(1)}, bf16[336,1024]{1,0:T(8,128)(2,1)S(1)}, u32[]{:S(2)}, u32[]{:S(2)}) collective-permute-start(bf16[336,1024]{1,0:T(8,128)(2,1)S(1)} %maximum_maximum_fusion.1.refs_0_), channel_id=1, source_target_pairs={{0,8},{8,0},{16,24},{24,16},{1,9},{9,1},{17,25},{25,17},{2,10},{10... | collective-permute-start | bytes 2064392 | tf_op jit(solution)/shard_map/ppermute | solution.py:572
  126.2 23.2 %copy-start.12 = (bf16[336,1024]{1,0:T(8,128)(2,1)}, bf16[336,1024]{1,0:T(8,128)(2,1)S(1)}, u32[]{:S(2)}) copy-start(bf16[336,1024]{1,0:T(8,128)(2,1)S(1)} %collective-permute-done.7.refs_1_) | copy-start | bytes 2064388
  126.2 14.9 %collective-permute-start.9 = (bf16[4,1024,512]{2,1,0:T(8,128)(2,1)}, bf16[4,1024,512]{2,1,0:T(8,128)(2,1)S(1)}, u32[]{:S(2)}, u32[]{:S(2)}) collective-permute-start(bf16[4,1024,512]{2,1,0:T(8,128)(2,1)} %get-tuple-element.107), channel_id=1, source_target_pairs={{0,1},{1,0},{2,3},{3,2},{4,5},{5,4},{6,7},{7,6},{8,9},{9,8},{10,11... | collective-permute-start | bytes 12582920 | tf_op jit(solution)/shard_map/ppermute | solution.py:576
  126.3 14.8 %collective-permute-start.8 = (bf16[256,1024]{1,0:T(8,128)(2,1)S(1)}, bf16[256,1024]{1,0:T(8,128)(2,1)S(1)}, u32[]{:S(2)}, u32[]{:S(2)}) collective-permute-start(bf16[256,1024]{1,0:T(8,128)(2,1)S(1)} %get-tuple-element.106.refs_6_), channel_id=1, source_target_pairs={{0,8},{8,0},{16,24},{24,16},{1,9},{9,1},{17,25},{25,17},{2,10},{10... | collective-permute-start | bytes 1572872 | tf_op jit(solution)/shard_map/ppermute | solution.py:572
  126.5 25.9 %collective-permute-start.13 = (bf16[256,1024]{1,0:T(8,128)(2,1)}, bf16[256,1024]{1,0:T(8,128)(2,1)S(1)}, u32[]{:S(2)}, u32[]{:S(2)}) collective-permute-start(bf16[256,1024]{1,0:T(8,128)(2,1)} %collective-permute-done.6.refs_8_), channel_id=1, source_target_pairs={{8,0},{16,24},{9,1},{17,25},{10,2},{18,26},{11,3},{19,27},{12,4},{... | collective-permute-start | bytes 1572872 | tf_op jit(solution)/shard_map/ppermute | solution.py:572
  141.1 30.9 %copy-start.31 = (bf16[4,1024,512]{2,1,0:T(8,128)(2,1)}, bf16[4,1024,512]{2,1,0:T(8,128)(2,1)S(1)}, u32[]{:S(2)}) copy-start(bf16[4,1024,512]{2,1,0:T(8,128)(2,1)S(1)} %collective-permute-done.9.o_ref) | copy-start | bytes 12582916
  144.9 24.3 %collective-permute-start.14 = (bf16[2,512,512]{2,1,0:T(8,128)(2,1)S(1)}, bf16[2,512,512]{2,1,0:T(8,128)(2,1)S(1)}, u32[]{:S(2)}, u32[]{:S(2)}) collective-permute-start(bf16[2,512,512]{2,1,0:T(8,128)(2,1)S(1)} %pad_maximum_fusion.1), channel_id=1, source_target_pairs={{0,2},{1,3},{2,0},{3,1},{4,6},{5,7},{6,4},{7,5},{8,10},{9,11},{10,... | collective-permute-start | bytes 3145736 | tf_op jit(solution)/shard_map/ppermute | solution.py:576
  146.7 24.0 %collective-permute-start.15 = (bf16[2,512,512]{2,1,0:T(8,128)(2,1)S(1)}, bf16[2,512,512]{2,1,0:T(8,128)(2,1)S(1)}, u32[]{:S(2)}, u32[]{:S(2)}) collective-permute-start(bf16[2,512,512]{2,1,0:T(8,128)(2,1)S(1)} %pad_maximum_fusion.2), channel_id=1, source_target_pairs={{0,4},{1,5},{2,6},{3,7},{4,0},{5,1},{6,2},{7,3},{8,12},{9,13},{10,... | collective-permute-start | bytes 3145736 | tf_op jit(solution)/shard_map/ppermute | solution.py:576
  148.2 18.5 %collective-permute-start.11 = (bf16[336,1024]{1,0:T(8,128)(2,1)S(1)}, bf16[336,1024]{1,0:T(8,128)(2,1)S(1)}, u32[]{:S(2)}, u32[]{:S(2)}) collective-permute-start(bf16[336,1024]{1,0:T(8,128)(2,1)S(1)} %collective-permute-done.5.refs_2_), channel_id=1, source_target_pairs={{8,0},{16,24},{9,1},{17,25},{10,2},{18,26},{11,3},{19,27},{12,4},{... | collective-permute-start | bytes 2064392 | tf_op jit(solution)/shard_map/ppermute | solution.py:572
  149.5 17.2 %collective-permute-start.10 = (bf16[336,1024]{1,0:T(8,128)(2,1)S(1)}, bf16[336,1024]{1,0:T(8,128)(2,1)S(1)}, u32[]{:S(2)}, u32[]{:S(2)}) collective-permute-start(bf16[336,1024]{1,0:T(8,128)(2,1)S(1)} %collective-permute-done.7.refs_1_), channel_id=1, source_target_pairs={{8,16},{16,8},{9,17},{17,9},{10,18},{18,10},{11,19},{19,11},{12,20... | collective-permute-start | bytes 2064392 | tf_op jit(solution)/shard_map/ppermute | solution.py:572
  152.3 21.3 %copy-start.22 = (bf16[256,1024]{1,0:T(8,128)(2,1)}, bf16[256,1024]{1,0:T(8,128)(2,1)S(1)}, u32[]{:S(2)}) copy-start(bf16[256,1024]{1,0:T(8,128)(2,1)S(1)} %collective-permute-done.13.refs_10_) | copy-start | bytes 1572868
  152.3 14.3 %collective-permute-start.12 = (bf16[256,1024]{1,0:T(8,128)(2,1)S(1)}, bf16[256,1024]{1,0:T(8,128)(2,1)S(1)}, u32[]{:S(2)}, u32[]{:S(2)}) collective-permute-start(bf16[256,1024]{1,0:T(8,128)(2,1)S(1)} %collective-permute-done.8.refs_7_), channel_id=1, source_target_pairs={{8,16},{16,8},{9,17},{17,9},{10,18},{18,10},{11,19},{19,11},{12,20... | collective-permute-start | bytes 1572872 | tf_op jit(solution)/shard_map/ppermute | solution.py:572
  166.6 30.2 %copy-start.39 = (bf16[336,1024]{1,0:T(8,128)(2,1)}, bf16[336,1024]{1,0:T(8,128)(2,1)S(1)}, u32[]{:S(2)}) copy-start(bf16[336,1024]{1,0:T(8,128)(2,1)S(1)} %collective-permute-done.11.refs_4_) | copy-start | bytes 2064388
  166.6 28.7 %copy-start.24 = (bf16[256,1024]{1,0:T(8,128)(2,1)}, bf16[256,1024]{1,0:T(8,128)(2,1)S(1)}, u32[]{:S(2)}) copy-start(bf16[256,1024]{1,0:T(8,128)(2,1)S(1)} %collective-permute-done.12.refs_9_) | copy-start | bytes 1572868
  170.7 24.6 %collective-permute-start.18 = (bf16[336,1024]{1,0:T(8,128)(2,1)S(1)}, bf16[336,1024]{1,0:T(8,128)(2,1)S(1)}, u32[]{:S(2)}, u32[]{:S(2)}) collective-permute-start(bf16[336,1024]{1,0:T(8,128)(2,1)S(1)} %collective-permute-done.10.refs_3_), channel_id=1, source_target_pairs={{8,0},{16,24},{9,1},{17,25},{10,2},{18,26},{11,3},{19,27},{12,4},{... | collective-permute-start | bytes 2064392 | tf_op jit(solution)/shard_map/ppermute | solution.py:572
  173.7 11.9 %collective-permute-start.17 = (bf16[512,512]{1,0:T(8,128)(2,1)S(1)}, bf16[512,512]{1,0:T(8,128)(2,1)S(1)}, u32[]{:S(2)}, u32[]{:S(2)}) collective-permute-start(bf16[512,512]{1,0:T(8,128)(2,1)S(1)} %get-tuple-element.180), channel_id=1, source_target_pairs={{0,2},{1,3},{2,0},{3,1},{4,6},{5,7},{6,4},{7,5},{8,10},{9,11},{10,... | collective-permute-start | bytes 1572872 | tf_op jit(solution)/shard_map/ppermute | solution.py:576
  174.2 11.5 %collective-permute-start.16 = (bf16[512,512]{1,0:T(8,128)(2,1)S(1)}, bf16[512,512]{1,0:T(8,128)(2,1)S(1)}, u32[]{:S(2)}, u32[]{:S(2)}) collective-permute-start(bf16[512,512]{1,0:T(8,128)(2,1)S(1)} %get-tuple-element.181), channel_id=1, source_target_pairs={{0,4},{1,5},{2,6},{3,7},{4,0},{5,1},{6,2},{7,3},{8,12},{9,13},{10,... | collective-permute-start | bytes 1572872 | tf_op jit(solution)/shard_map/ppermute | solution.py:576
  195.3 16.4 %collective-permute-start.19 = (bf16[256,1024]{1,0:T(8,128)(2,1)S(1)}, bf16[256,1024]{1,0:T(8,128)(2,1)S(1)}, u32[]{:S(2)}, u32[]{:S(2)}) collective-permute-start(bf16[256,1024]{1,0:T(8,128)(2,1)S(1)} %collective-permute-done.12.refs_9_), channel_id=1, source_target_pairs={{8,0},{16,24},{9,1},{17,25},{10,2},{18,26},{11,3},{19,27},{12,4},{... | collective-permute-start | bytes 1572872 | tf_op jit(solution)/shard_map/ppermute | solution.py:572
  212.5 174.2 %reduce-scatter.5.cloned.1.call-start = ((), (), s32[]{:S(2)}) async-start(), calls=%async_computation.4 | async-start | bytes 5980160 | tf_op jit(solution)/shard_map/reduce_scatter | solution.py:741
  229.9 10.4 %collective-permute-start.21 = (bf16[512,512]{1,0:T(8,128)(2,1)S(1)}, bf16[512,512]{1,0:T(8,128)(2,1)S(1)}, u32[]{:S(2)}, u32[]{:S(2)}) collective-permute-start(bf16[512,512]{1,0:T(8,128)(2,1)S(1)} %get-tuple-element.194), channel_id=1, source_target_pairs={{0,4},{1,5},{2,6},{3,7},{4,0},{5,1},{6,2},{7,3},{8,12},{9,13},{10,... | collective-permute-start | bytes 1572872 | tf_op jit(solution)/shard_map/ppermute | solution.py:576
  229.9 11.8 %collective-permute-start.20 = (bf16[512,512]{1,0:T(8,128)(2,1)S(1)}, bf16[512,512]{1,0:T(8,128)(2,1)S(1)}, u32[]{:S(2)}, u32[]{:S(2)}) collective-permute-start(bf16[512,512]{1,0:T(8,128)(2,1)S(1)} %get-tuple-element.195), channel_id=1, source_target_pairs={{0,2},{1,3},{2,0},{3,1},{4,6},{5,7},{6,4},{7,5},{8,10},{9,11},{10,... | collective-permute-start | bytes 1572872 | tf_op jit(solution)/shard_map/ppermute | solution.py:576
  241.9 21.4 %collective-permute-start.22 = (bf16[2,512,512]{2,1,0:T(8,128)(2,1)S(1)}, bf16[2,512,512]{2,1,0:T(8,128)(2,1)S(1)}, u32[]{:S(2)}, u32[]{:S(2)}) collective-permute-start(bf16[2,512,512]{2,1,0:T(8,128)(2,1)S(1)} %pad_maximum_fusion.3), channel_id=1, source_target_pairs={{0,2},{1,3},{2,0},{3,1},{4,6},{5,7},{6,4},{7,5},{8,10},{9,11},{10,... | collective-permute-start | bytes 3145736 | tf_op jit(solution)/shard_map/ppermute | solution.py:576
  242.2 21.3 %collective-permute-start.23 = (bf16[2,512,512]{2,1,0:T(8,128)(2,1)S(1)}, bf16[2,512,512]{2,1,0:T(8,128)(2,1)S(1)}, u32[]{:S(2)}, u32[]{:S(2)}) collective-permute-start(bf16[2,512,512]{2,1,0:T(8,128)(2,1)S(1)} %pad_maximum_fusion.4), channel_id=1, source_target_pairs={{0,4},{1,5},{2,6},{3,7},{4,0},{5,1},{6,2},{7,3},{8,12},{9,13},{10,... | collective-permute-start | bytes 3145736 | tf_op jit(solution)/shard_map/ppermute | solution.py:576
  264.3 7.4 %collective-permute-start.24 = (bf16[4,1024,512]{2,1,0:T(8,128)(2,1)S(1)}, bf16[4,1024,512]{2,1,0:T(8,128)(2,1)}, u32[]{:S(2)}, u32[]{:S(2)}) collective-permute-start(bf16[4,1024,512]{2,1,0:T(8,128)(2,1)S(1)} %pad_maximum_fusion.mine_ref), channel_id=1, source_target_pairs={{0,1},{1,0},{2,3},{3,2},{4,5},{5,4},{6,7},{7,6},{8,9},{9,8},{10,11... | collective-permute-start | bytes 12582920 | tf_op jit(solution)/shard_map/ppermute | solution.py:576
  314.2 7.4 %collective-permute-start.25 = (bf16[4,1024,512]{2,1,0:T(8,128)(2,1)}, bf16[4,1024,512]{2,1,0:T(8,128)(2,1)S(1)}, u32[]{:S(2)}, u32[]{:S(2)}) collective-permute-start(bf16[4,1024,512]{2,1,0:T(8,128)(2,1)} %get-tuple-element.156), channel_id=1, source_target_pairs={{0,1},{1,0},{2,3},{3,2},{4,5},{5,4},{6,7},{7,6},{8,9},{9,8},{10,11... | collective-permute-start | bytes 12582920 | tf_op jit(solution)/shard_map/ppermute | solution.py:576
  323.8 35.9 %collective-permute-start.26 = (bf16[2,512,512]{2,1,0:T(8,128)(2,1)S(1)}, bf16[2,512,512]{2,1,0:T(8,128)(2,1)S(1)}, u32[]{:S(2)}, u32[]{:S(2)}) collective-permute-start(bf16[2,512,512]{2,1,0:T(8,128)(2,1)S(1)} %pad_maximum_fusion.5), channel_id=1, source_target_pairs={{0,2},{1,3},{2,0},{3,1},{4,6},{5,7},{6,4},{7,5},{8,10},{9,11},{10,... | collective-permute-start | bytes 3145736 | tf_op jit(solution)/shard_map/ppermute | solution.py:576
  325.3 34.4 %collective-permute-start.27 = (bf16[2,512,512]{2,1,0:T(8,128)(2,1)S(1)}, bf16[2,512,512]{2,1,0:T(8,128)(2,1)S(1)}, u32[]{:S(2)}, u32[]{:S(2)}) collective-permute-start(bf16[2,512,512]{2,1,0:T(8,128)(2,1)S(1)} %pad_maximum_fusion.6), channel_id=1, source_target_pairs={{0,4},{1,5},{2,6},{3,7},{4,0},{5,1},{6,2},{7,3},{8,12},{9,13},{10,... | collective-permute-start | bytes 3145736 | tf_op jit(solution)/shard_map/ppermute | solution.py:576
  326.8 11.9 %collective-permute-start.30 = (bf16[144,512]{1,0:T(8,128)(2,1)S(1)}, bf16[144,512]{1,0:T(8,128)(2,1)S(1)}, u32[]{:S(2)}, u32[]{:S(2)}) collective-permute-start(bf16[144,512]{1,0:T(8,128)(2,1)S(1)} %get-tuple-element.196), channel_id=1, source_target_pairs={{0,24},{8,16},{16,8},{24,0},{1,25},{9,17},{17,9},{25,1},{2,26},{10... | collective-permute-start | bytes 442376 | tf_op jit(solution)/shard_map/ppermute | solution.py:572
  329.3 30.5 %collective-permute-start.29 = (bf16[144,512]{1,0:T(8,128)(2,1)S(1)}, bf16[144,512]{1,0:T(8,128)(2,1)S(1)}, u32[]{:S(2)}, u32[]{:S(2)}) collective-permute-start(bf16[144,512]{1,0:T(8,128)(2,1)S(1)} %get-tuple-element.197), channel_id=1, source_target_pairs={{0,16},{8,24},{16,0},{24,8},{1,17},{9,25},{17,1},{25,9},{2,18},{10... | collective-permute-start | bytes 442376 | tf_op jit(solution)/shard_map/ppermute | solution.py:572
  330.1 29.6 %copy-start.33 = (bf16[4,1024,512]{2,1,0:T(8,128)(2,1)S(1)}, bf16[4,1024,512]{2,1,0:T(8,128)(2,1)}, u32[]{:S(2)}) copy-start(bf16[4,1024,512]{2,1,0:T(8,128)(2,1)} %get-tuple-element.157) | copy-start | bytes 12582916
  330.2 29.6 %collective-permute-start.28 = (bf16[144,512]{1,0:T(8,128)(2,1)S(1)}, bf16[144,512]{1,0:T(8,128)(2,1)S(1)}, u32[]{:S(2)}, u32[]{:S(2)}) collective-permute-start(bf16[144,512]{1,0:T(8,128)(2,1)S(1)} %get-tuple-element.198), channel_id=1, source_target_pairs={{0,8},{8,0},{16,24},{24,16},{1,9},{9,1},{17,25},{25,17},{2,10},{10... | collective-permute-start | bytes 442376 | tf_op jit(solution)/shard_map/ppermute | solution.py:572
  334.4 39.1 %copy-start.7 = (bf16[1024,512]{1,0:T(8,128)(2,1)S(1)}, bf16[1024,512]{1,0:T(8,128)(2,1)}, u32[]{:S(2)}) copy-start(bf16[1024,512]{1,0:T(8,128)(2,1)} %get-tuple-element.132.x_ref) | copy-start | bytes 3145732
  360.2 13.2 %collective-permute-start.31 = (bf16[512,512]{1,0:T(8,128)(2,1)S(1)}, bf16[512,512]{1,0:T(8,128)(2,1)S(1)}, u32[]{:S(2)}, u32[]{:S(2)}) collective-permute-start(bf16[512,512]{1,0:T(8,128)(2,1)S(1)} %get-tuple-element.174), channel_id=1, source_target_pairs={{0,4},{1,5},{2,6},{3,7},{4,0},{5,1},{6,2},{7,3},{8,12},{9,13},{10,... | collective-permute-start | bytes 1572872 | tf_op jit(solution)/shard_map/ppermute | solution.py:576
  360.9 12.6 %collective-permute-start.32 = (bf16[512,512]{1,0:T(8,128)(2,1)S(1)}, bf16[512,512]{1,0:T(8,128)(2,1)S(1)}, u32[]{:S(2)}, u32[]{:S(2)}) collective-permute-start(bf16[512,512]{1,0:T(8,128)(2,1)S(1)} %get-tuple-element.175), channel_id=1, source_target_pairs={{0,2},{1,3},{2,0},{3,1},{4,6},{5,7},{6,4},{7,5},{8,10},{9,11},{10,... | collective-permute-start | bytes 1572872 | tf_op jit(solution)/shard_map/ppermute | solution.py:576
  (31 other events, 167.1 us)
Sparse Core Ops, SparseCore 0:
  45.8 54.2 all-gather.1
  211.9 75.9 reduce-scatter.2
  290.4 96.2 reduce-scatter.4

commit v3 on v2

--- a/solution.py
+++ b/solution.py
@@ -169,26 +169,52 @@
     shard = conv.shape[0] // 4
 
     def put(j, ref):
-        start = pl.multiple_of((p[0] ^ j) * shard, 16)
-        conv[pl.ds(start, tall), :] = ref[depth : depth + tall, :width]
-        start = pl.multiple_of((p[0] ^ j) * shard + shard - tall, 16)
-        conv[pl.ds(start, tall), :] = ref[depth : depth + tall, width:]
+        put_shard(p, j, conv, ref[depth : depth + tall, :width], 0)
+        put_shard(p, j, conv, ref[depth : depth + tall, width:], shard - tall)
 
     fill_slots(p, refs, put)
 
 
-def first_layer(place, x, piece, side):
+def put_shard(p, slot, conv, value, offset):
+    shard = conv.shape[0] // 4
+    start = pl.multiple_of((p[0] ^ slot) * shard + offset, 16)
+    conv[pl.ds(start, value.shape[0]), :] = value
+
+
+def first_layer(place, x, piece, far, side):
     rows, width = x.shape
     images = rows // (side * side)
-
-    def kernel(p, x_ref, *refs):
-        sent, keep, hid_t, slope, conv, hid, sel, pad_ref, wide_ref = refs[6:]
+    tall = piece[0].shape[0] - width
+
+    def kernel(p, x_ref, own, a, b, c, d, far_ref, *refs):
+        sent, keep, hid, hid_t, slope, conv, sel, pad_ref, wide_ref = refs
         step = pl.program_id(0)
+        inner = (p[0] == 1) | (p[0] == 2)
 
         @pl.when(step == 0)
         def _():
-            put_kernels(p, refs[:6], conv, width, piece[0].shape[0] - width)
-            put_columns(p, refs[:6], sel, 0, width)
+            shard = conv.shape[0] // 4
+
+            def put_slot(j, ref):
+                if j < 3:
+                    sel[0, j] = ref[:width, :width]
+                    sel[1, j] = ref[:width, width:]
+                put_shard(p, j, conv, ref[width:, :width], 0)
+                put_shard(p, j, conv, ref[width:, width:], shard - tall)
+
+            put_slot(0, own)
+            put_slot(1, a)
+
+            @pl.when(inner)
+            def _():
+                put_slot(2, c)
+                put_slot(3, b)
+
+            @pl.when(jnp.logical_not(inner))
+            def _():
+                put_slot(2, d)
+                put_shard(p, 3, conv, far_ref[...], 0)
+
             for h in range(width // HALF):
                 lanes = slice(h * HALF, (h + 1) * HALF)
 
@@ -203,34 +229,127 @@
         sent[0] = dot(hid[...], sel[1 - p[2], step]).astype(BF)
         keep[0] = dot(hid[...], sel[p[2], step]).astype(BF)
 
-    mix_spec = pl.BlockSpec((1, rows, width), lambda s, p: (rel_chip(s, p), 0, 0))
-    mix_shape = jax.ShapeDtypeStruct((4, rows, width), BF)
+    mix_spec = pl.BlockSpec((1, rows, width), lambda s, p: (s, 0, 0))
+    mix_shape = jax.ShapeDtypeStruct((3, rows, width), BF)
     return with_place(
         kernel,
-        (4,),
-        [whole((rows, width))] + [whole(piece[0].shape)] * 6,
-        (mix_spec, mix_spec, whole((width, rows)), whole((rows, width)), whole((TAPS * GW, width))),
+        (3,),
+        [whole((rows, width))] + [whole(piece[0].shape)] * 5 + [whole(far.shape)],
+        (mix_spec, mix_spec)
+        + (whole((rows, width)), whole((width, rows)), whole((rows, width)))
+        + (whole((TAPS * GW, width)),),
         (
             mix_shape,
             mix_shape,
+            jax.ShapeDtypeStruct((rows, width), BF),
             jax.ShapeDtypeStruct((width, rows), BF),
             jax.ShapeDtypeStruct((rows, width), F32),
             jax.ShapeDtypeStruct((TAPS * GW, width), BF),
         ),
-        16 * rows * width * width + 2 * rows * HALF * width * TAPS,
+        12 * rows * width * width + 2 * rows * HALF * width * TAPS,
         30 * rows * width,
-        [pltpu.VMEM((rows, width), BF), pltpu.VMEM((2, 4, width, width), BF)]
-        + conv_scratch(side, images),
+        [pltpu.VMEM((2, 3, width, width), BF)] + conv_scratch(side, images),
         60,
-    )(place, x, *piece)
-
-
-def next_layer(place, base, keep, other, first_x, second_y, first_y, second_x, piece, start, wide, side):
+    )(place, x, *piece, far)
+
+
+def last_slot(place, hidden, inner_piece, outer_piece):
+    rows, width = hidden.shape
+
+    def kernel(p, h_ref, b_ref, e_ref, sent, keep):
+        inner = (p[0] == 1) | (p[0] == 2)
+        for core in range(2):
+            lanes = slice(core * width, (core + 1) * width)
+            weights = jnp.where(inner, b_ref[:, lanes], e_ref[:, lanes])
+            value = dot(h_ref[...], weights).astype(BF)
+
+            @pl.when(p[2] == core)
+            def _(value=value):
+                keep[0] = value
+
+            @pl.when(p[2] != core)
+            def _(value=value):
+                sent[0] = value
+
+    shape = (1, rows, width)
+    return with_place(
+        kernel,
+        (1,),
+        [whole((rows, width))] + [whole((width, 2 * width))] * 2,
+        (whole(shape), whole(shape)),
+        (jax.ShapeDtypeStruct(shape, BF), jax.ShapeDtypeStruct(shape, BF)),
+        4 * rows * width * width,
+        12 * rows * width,
+        (),
+        24,
+    )(place, hidden, inner_piece, outer_piece)
+
+
+def sum_cores(place, keep, keep_last, other, other_last):
+    _, rows, width = keep.shape
+    cut = rows // 2
+
+    def kernel(p, k_ref, kl_ref, o_ref, ol_ref, to_x, to_y, near, first_far, second_far):
+        rel = pl.program_id(0)
+        slot = rel_chip(rel, p)
+
+        def both(here):
+            early = add(k_ref[0, here, :], o_ref[0, here, :])
+            late = add(kl_ref[0, here, :], ol_ref[0, here, :])
+            return jnp.where(slot == 3, late, early)
+
+        first, second = slice(0, cut), slice(cut, rows)
+
+        @pl.when(rel == 0)
+        def _():
+            near[first, :] = both(first)
+            near[second, :] = both(second)
+
+        @pl.when(rel == 1)
+        def _():
+            to_x[0] = both(first).astype(BF)
+            second_far[...] = both(second)
+
+        @pl.when(rel == 2)
+        def _():
+            first_far[...] = both(first)
+            to_y[0] = both(second).astype(BF)
+
+        @pl.when(rel == 3)
+        def _():
+            to_x[1] = both(first).astype(BF)
+            to_y[1] = both(second).astype(BF)
+
+    early = pl.BlockSpec(
+        (1, rows, width), lambda r, p: (jnp.minimum(rel_chip(r, p), 2), 0, 0)
+    )
+    last = whole((1, rows, width))
+    pair, single = (2, cut, width), (cut, width)
+    return with_place(
+        kernel,
+        (4,),
+        [early, last, early, last],
+        (whole(pair), whole(pair), whole((rows, width)), whole(single), whole(single)),
+        (
+            jax.ShapeDtypeStruct(pair, BF),
+            jax.ShapeDtypeStruct(pair, BF),
+            jax.ShapeDtypeStruct((rows, width), F32),
+            jax.ShapeDtypeStruct(single, F32),
+            jax.ShapeDtypeStruct(single, F32),
+        ),
+        0,
+        24 * rows * width,
+        (),
+        32,
+    )(place, keep, keep_last, other, other_last)
+
+
+def next_layer(place, base, near_sum, first_x, second_y, first_y, second_x, piece, start, wide, side):
     rows, width = base.shape
     images = rows // (side * side)
     cut = rows // 2
 
-    def kernel(p, b_ref, k_ref, o_ref, fx, sy, fy, sx, *refs):
+    def kernel(p, b_ref, n_ref, fx, sy, fy, sx, *refs):
         g_ref = refs[6]
         x_ref, hid, slope, conv, term = refs[7:12]
         hid_t, pad_ref, wide_ref = refs[12:]
@@ -241,10 +360,10 @@
             put_kernels(p, refs[:6], conv, 0, tall)
             near, far = slice(0, cut), slice(cut, rows)
             x_ref[near, :] = (
-                add(b_ref[near, :]) + add(k_ref[0, near, :], o_ref[0, near, :], fx[0], fy[...])
+                add(b_ref[near, :]) + add(n_ref[near, :], fx[0], fy[...])
             ).astype(BF)
             x_ref[far, :] = (
-                add(b_ref[far, :]) + add(k_ref[0, far, :], o_ref[0, far, :], sy[0], sx[...])
+                add(b_ref[far, :]) + add(n_ref[far, :], sy[0], sx[...])
             ).astype(BF)
             for h in range(width // HALF):
                 lanes = slice(h * HALF, (h + 1) * HALF)
@@ -261,7 +380,6 @@
         term[0, :, width:] = dot(hid_t[...], g_ref[1]).astype(BF)
 
     all_spec = whole((rows, width))
-    part = whole((1, rows, width))
     tall = piece[0].shape[0] - start
     block = math.gcd(start, 128)
     return with_place(
@@ -269,8 +387,7 @@
         (4,),
         [
             all_spec,
-            part,
-            part,
+            all_spec,
             whole((1, cut, width)),
             whole((1, cut, width)),
             whole((cut, width)),
@@ -296,7 +413,7 @@
         32 * rows * width,
         [pltpu.VMEM((width, rows), BF)] + conv_scratch(side, images),
         60,
-    )(place, base, keep, other, first_x, second_y, first_y, second_x, *piece, wide)
+    )(place, base, near_sum, first_x, second_y, first_y, second_x, *piece, wide)
 
 
 def output_gradient(place, wide, pieces, slope, conv, gradient, side):
@@ -688,44 +805,52 @@
     own0 = with_kernels(mix_weight[0], 0)
     own1, own2 = with_kernels(mix_weight[1, :depth], 1), mix_weight[1, depth:]
     a0, b0 = gather_outer(own0), gather_inner(own0)
+    far0 = permute_dp(conv_weight[0], [(0, 3), (3, 0)])
     x0 = to_rows(images)
-    a0, b0, x0 = close(a0, b0, x0)
-
-    g2 = to_rows(gate(cotangent))
-    wide2 = lax.all_gather(g2, "group", axis=0)
+    g2 = to_rows(cotangent)
+    a0, b0, far0, x0, g2 = close(a0, b0, far0, x0, g2)
+
+    wide2 = lax.all_gather(gate(g2), "group", axis=0)
     c0, d0 = gather_second(a0, b0)
     c0, d0 = close(c0, d0)
 
-    e0 = gather_third(c0)
+    e0 = gather_third(c0[:width])
     b1, b2 = gather_inner(gate(own1)), gather_inner(gate(own2))
-    e0, b1, b2 = close(e0, b1, b2)
+    sent, keep, hidden0, hidden0_t, slope0, conv0 = first_layer(
+        place, x0, (own0, a0, b0, c0, d0), far0, side
+    )
+    e0, b1, b2, sent, keep, hidden0, hidden0_t, slope0, conv0 = close(
+        e0, b1, b2, sent, keep, hidden0, hidden0_t, slope0, conv0
+    )
     p0 = (own0, a0, b0, c0, d0, e0)
 
     a1 = gather_outer(gate(own1))
-    sent, keep, hidden0_t, slope0, conv0 = first_layer(place, x0, p0, side)
-    a1, sent, keep, hidden0_t, slope0, conv0 = close(a1, sent, keep, hidden0_t, slope0, conv0)
-
+    other = across_cores(sent)
+    sent_last, keep_last = last_slot(place, hidden0, b0, e0)
+    other_last = across_cores(sent_last)
+    a1, other, keep_last, other_last = close(a1, other, keep_last, other_last)
+
+    c1, d1 = gather_second(a1, b1)
     a2 = gather_outer(gate(own2))
-    other = across_cores(sent)
-    a2, other = close(a2, other)
-
-    c1, d1 = gather_second(a1, b1)
-    c2, d2 = gather_second(a2, b2)
-    sx, sy = sum_first(keep, other)
-    c1, d1, c2, d2, sx, sy = close(c1, d1, c2, d2, sx, sy)
+    to_x, to_y, near, first_far, second_far = sum_cores(place, keep, keep_last, other, other_last)
+    sx, sy = permute_group(to_x, ACROSS_X), permute_group(to_y, ACROSS_Y)
+    c1, d1, a2, sx, sy = close(c1, d1, a2, sx, sy)
 
     e1 = gather_third(c1)
-    ty, tx = sum_second(keep, other, sx, sy)
-    ty, tx, e1 = close(ty, tx, e1)
+    c2 = gather_inner(a2)
+    ty = permute_group(add(first_far, sx[1]).astype(BF), ACROSS_Y)
+    tx = permute_group(add(second_far, sy[1]).astype(BF), ACROSS_X)
+    ty, tx, e1, c2 = close(ty, tx, e1, c2)
     p1 = (own1, a1, b1, c1, d1, e1)
 
-    e2 = gather_third(gate(c2))
+    d2 = gather_third(gate(b2))
+    e2 = gather_third(c2)
     x1, hidden1, slope1, conv1, m1 = next_layer(
-        place, x0, keep, other, sx, sy, ty, tx, p1, depth, wide2, side
-    )
-    x1, hidden1, slope1, conv1, m1, e2 = close(x1, hidden1, slope1, conv1, m1, e2)
+        place, x0, near, sx, sy, ty, tx, p1, depth, wide2, side
+    )
+    last = lax.psum_scatter(m1, "dp", scatter_dimension=0, tiled=True)
+    x1, hidden1, slope1, conv1, d2, e2 = close(x1, hidden1, slope1, conv1, d2, e2)
     p2 = (own2, a2, b2, c2, d2, e2)
-    last = lax.psum_scatter(m1, "dp", scatter_dimension=0, tiled=True)
 
     gp1, g1 = output_gradient(place, wide2, [p1, p2], slope1, conv1, g2, side)
     ax, ay = plane_first(g1)

time: 400 us -> 399 us (level)
  waiting for transfers between devices: 224 us -> 207 us
  starting transfers between devices: 41 us -> 52.8 us
  other arithmetic: 11.7 us -> 6.48 us
  local copies, waits for them, and re-layouts: 17.3 us -> 22.2 us
    ppermute x18 -> x19, waiting for transfers between devices: 142 us -> 125 us  [permute_dp(): return lax.ppermute(value, 'dp', pairs)]
    ppermute x18 -> x19, starting transfers between devices: 29.1 us -> 39.6 us  [permute_dp(): return lax.ppermute(value, 'dp', pairs)]
    reduce_scatter x1, waiting for transfers between devices: 9.89 us -> 18.2 us  [staged(): first = lax.psum_scatter(m0, 'dp', scatter_dimension=0, tiled=True)]
    ppermute x15 -> x16, waiting for transfers between devices: 65.3 us -> 58.1 us  [permute_group(): return lax.ppermute(value, 'group', pairs)]
    pallas_call x2 -> x4, Pallas kernels: 28.8 us -> 32 us  [the longest x1 14.7 us: next_layer(): with_place(kernel, (4,), [all_spec, all_spec, whole((1, cut, width)), who...]
    ppermute x15 -> x16, starting transfers between devices: 11.9 us -> 13.2 us  [permute_group(): return lax.ppermute(value, 'group', pairs)]
  transfers between devices with their start and end apart: 36 -> 38, of which waited for: 22 -> 21; matrix products, arithmetic and copies ran while one was open for 4% -> 5% of each run, Pallas kernels for 22% -> 23%
where the time goes in v3:
time: 399 us; the launch traced here: 396 us
  waiting for transfers between devices  207 us (52%)
  Pallas kernels  92.6 us (23%)
  starting transfers between devices  52.8 us (13%)
  local copies, waits for them, and re-layouts  22.2 us (6%)
  between operations  14.6 us (4%)
  other arithmetic  6.48 us (2%)
    ppermute x19, waiting for transfers between devices, permute_dp(): return lax.ppermute(value, 'dp', pairs)  125 us
    ppermute x16, waiting for transfers between devices, permute_group(): return lax.ppermute(value, 'group', pairs)  58.1 us
    ppermute x19, starting transfers between devices, permute_dp(): return lax.ppermute(value, 'dp', pairs)  39.6 us
    reduce_scatter x1, waiting for transfers between devices, staged(): first = lax.psum_scatter(m0, 'dp', scatter_dimension=0, tiled=True)  18.2 us
    pallas_call x1, Pallas kernels, output_gradient(): with_place(kernel, (4,), [all_spec, pl.BlockSpec((2, rows, width), lambda...  16.2 us
    pallas_call x1, Pallas kernels, next_layer(): with_place(kernel, (4,), [all_spec, all_spec, whole((1, cut, width)), who...  14.7 us
    ppermute x16, starting transfers between devices, permute_group(): return lax.ppermute(value, 'group', pairs)  13.2 us
    pallas_call x1, Pallas kernels, grad_pre(): with_place(kernel, (4,), [whole((rows, width))] + [pl.BlockSpec((1, rows,...  12.7 us
  transfers between devices with their start and end apart: 38, of which 21 were waited for; matrix products, arithmetic and copies ran while one was open for 5% of the time, Pallas kernels for 23%

profile of v3, /device:TPU:0, one launch (start us, length us, event | category | flops | bytes accessed | tf_op | source)
XLA Modules:
  0.0 396.2 jit_solution(16007320546623143282)
XLA Ops:
  9.7 3.1 collective-permute-start
  13.6 4.4 %collective-permute-start.2 = (bf16[144,512]{1,0:T(8,128)(2,1)S(1)}, bf16[144,512]{1,0:T(8,128)(2,1)S(1)}, u32[]{:S(2)}, u32[]{:S(2)}) collective-permute-start(bf16[144,512]{1,0:T(8,128)(2,1)S(1)} %slice_bitcast_fusion.12), channel_id=1, source_target_pairs={{0,24},{24,0},{1,25},{25,1},{2,26},{26,2},{3,27},{27,3},{4,28},{28... | collective-permute-start | bytes 442376 | tf_op jit(solution)/shard_map/ppermute | solution.py:689
  18.0 2.8 copy.8
  20.7 2.8 copy.9
  23.5 21.4 %collective-permute-done.2.far_ref = bf16[144,512]{1,0:T(8,128)(2,1)S(1)} collective-permute-done((bf16[144,512]{1,0:T(8,128)(2,1)S(1)}, bf16[144,512]{1,0:T(8,128)(2,1)S(1)}, u32[]{:S(2)}, u32[]{:S(2)}) %collective-permute-start.2) | collective-permute-done | bytes 147488 | tf_op jit(solution)/shard_map/ppermute | solution.py:689
  47.1 30.6 %collective-permute-done.4.d.refs_4_ = bf16[592,1024]{1,0:T(8,128)(2,1)} collective-permute-done((bf16[592,1024]{1,0:T(8,128)(2,1)S(1)}, bf16[592,1024]{1,0:T(8,128)(2,1)}, u32[]{:S(2)}, u32[]{:S(2)}) %collective-permute-start.4) | collective-permute-done | bytes 1212448 | tf_op jit(solution)/shard_map/ppermute | solution.py:689
  83.6 1.6 collective-permute-start.7
  85.2 12.6 %shard_map.75 = (bf16[3,1024,512]{2,1,0:T(8,128)(2,1)}, bf16[3,1024,512]{2,1,0:T(8,128)(2,1)}, bf16[1024,512]{1,0:T(8,128)(2,1)}, bf16[512,1024]{1,0:T(8,128)(2,...) custom-call(s32[3]{0:T(128)} %pad_add_fusion.p, bf16[1024,512]{1,0:T(8,128)(2,1)} %bitcast.80, ...), custom_call_target="tpu_custom_call" | custom-call | flops 5637144576 | bytes 15728640 | tf_op jit(solution)/shard_map/pallas_call | solution.py:234
  97.8 5.8 %collective-permute-done.5.e_ref.refs_5_ = bf16[512,1024]{1,0:T(8,128)(2,1)S(1)} collective-permute-done((bf16[512,1024]{1,0:T(8,128)(2,1)}, bf16[512,1024]{1,0:T(8,128)(2,1)S(1)}, u32[]{:S(2)}, u32[]{:S(2)}) %collective-permute-start.5) | collective-permute-done | bytes 1048608 | tf_op jit(solution)/shard_map/ppermute | solution.py:689
  103.6 1.6 copy-done.32
  105.2 2.2 shard_map.76
  107.6 8.6 %collective-permute-start.8 = (bf16[336,1024]{1,0:T(8,128)(2,1)S(1)}, bf16[336,1024]{1,0:T(8,128)(2,1)S(1)}, u32[]{:S(2)}, u32[]{:S(2)}) collective-permute-start(bf16[336,1024]{1,0:T(8,128)(2,1)S(1)} %maximum_maximum_fusion.1.refs_0_), channel_id=1, source_target_pairs={{0,8},{8,0},{16,24},{24,16},{1,9},{9,1},{17,25},{25,17},{2,10},{10... | collective-permute-start | bytes 2064392 | tf_op jit(solution)/shard_map/ppermute | solution.py:689
  116.2 15.9 %collective-permute-done.8.refs_1_ = bf16[336,1024]{1,0:T(8,128)(2,1)S(1)} collective-permute-done((bf16[336,1024]{1,0:T(8,128)(2,1)S(1)}, bf16[336,1024]{1,0:T(8,128)(2,1)S(1)}, u32[]{:S(2)}, u32[]{:S(2)}) %collective-permute-start.8) | collective-permute-done | bytes 688160 | tf_op jit(solution)/shard_map/ppermute | solution.py:689
  132.1 2.6 shard_map.77
  139.9 4.9 %collective-permute-start.13 = (bf16[256,1024]{1,0:T(8,128)(2,1)S(1)}, bf16[256,1024]{1,0:T(8,128)(2,1)S(1)}, u32[]{:S(2)}, u32[]{:S(2)}) collective-permute-start(bf16[256,1024]{1,0:T(8,128)(2,1)S(1)} %get-tuple-element.125.refs_6_), channel_id=1, source_target_pairs={{0,8},{8,0},{16,24},{24,16},{1,9},{9,1},{17,25},{25,17},{2,10},{10... | collective-permute-start | bytes 1572872 | tf_op jit(solution)/shard_map/ppermute | solution.py:689
  144.8 13.5 %collective-permute-done.12.refs_4_ = bf16[336,1024]{1,0:T(8,128)(2,1)S(1)} collective-permute-done((bf16[336,1024]{1,0:T(8,128)(2,1)}, bf16[336,1024]{1,0:T(8,128)(2,1)S(1)}, u32[]{:S(2)}, u32[]{:S(2)}) %collective-permute-start.12) | collective-permute-done | bytes 688160 | tf_op jit(solution)/shard_map/ppermute | solution.py:689
  158.3 9.5 %collective-permute-done.13.refs_7_ = bf16[256,1024]{1,0:T(8,128)(2,1)S(1)} collective-permute-done((bf16[256,1024]{1,0:T(8,128)(2,1)S(1)}, bf16[256,1024]{1,0:T(8,128)(2,1)S(1)}, u32[]{:S(2)}, u32[]{:S(2)}) %collective-permute-start.13) | collective-permute-done | bytes 524320 | tf_op jit(solution)/shard_map/ppermute | solution.py:689
  171.4 8.9 %collective-permute-done.16.fy = bf16[512,512]{1,0:T(8,128)(2,1)S(1)} collective-permute-done((bf16[512,512]{1,0:T(8,128)(2,1)S(1)}, bf16[512,512]{1,0:T(8,128)(2,1)S(1)}, u32[]{:S(2)}, u32[]{:S(2)}) %collective-permute-start.16) | collective-permute-done | bytes 524320 | tf_op jit(solution)/shard_map/ppermute | solution.py:693
  180.2 1.8 collective-permute-done.17.sx
  182.0 3.8 collective-permute-done.18.refs_5_
  189.6 14.7 %shard_map.78 = (bf16[1024,512]{1,0:T(8,128)(2,1)}, bf16[1024,512]{1,0:T(8,128)(2,1)}, f32[1024,512]{1,0:T(8,128)}, bf16[576,512]{1,0:T(8,128)(2,1)}, bf16[4,512,1024]{2,1,0:T(8,128)(2,1)}) custom-call(s32[3]{0:T(128)} %pad_add_fusion.p, bf16[1024,512]{1,0:T(8,128)(2,1)} %bitcast.81, f32[1024,512]{1,0:T(8,128)} %copy-done.19, ...), custom_call_target="tpu_custom_call" | custom-call | flops 6710886400 | bytes 16777216 | tf_op jit(solution)/shard_map/pallas_call | solution.py:385
  204.2 6.8 %collective-permute-done.21.refs_11_ = bf16[256,1024]{1,0:T(8,128)(2,1)S(1)} collective-permute-done((bf16[256,1024]{1,0:T(8,128)(2,1)S(1)}, bf16[256,1024]{1,0:T(8,128)(2,1)S(1)}, u32[]{:S(2)}, u32[]{:S(2)}) %collective-permute-start.21) | collective-permute-done | bytes 524320 | tf_op jit(solution)/shard_map/ppermute | solution.py:689
  211.8 16.2 %shard_map.79 = (bf16[1024,512]{1,0:T(8,128)(2,1)}, bf16[1024,512]{1,0:T(8,128)(2,1)}) custom-call(s32[3]{0:T(128)} %pad_add_fusion.p, f32[1024,512]{1,0:T(8,128)} %get-tuple-element.156.s_ref, bf16[8,1024,512]{2,1,0:T(8,128)(2,1)} %bitcast.92, bf16[336,1024]{1,0:T(8,128)(2,1)} %copy-done.12, bf16[336,1024]{1,0:T(8,128)(2,1)} %copy-done.20, ...), custom_call_target="tpu_custom_call" | custom-call | flops 6710886400 | bytes 16777216 | tf_op jit(solution)/shard_map/pallas_call | solution.py:457
  229.4 1.6 collective-permute-start.23
  231.0 8.1 %collective-permute-done.22 = bf16[512,512]{1,0:T(8,128)(2,1)S(1)} collective-permute-done((bf16[512,512]{1,0:T(8,128)(2,1)S(1)}, bf16[512,512]{1,0:T(8,128)(2,1)S(1)}, u32[]{:S(2)}, u32[]{:S(2)}) %collective-permute-start.22) | collective-permute-done | bytes 524320 | tf_op jit(solution)/shard_map/ppermute | solution.py:693
  239.1 2.1 collective-permute-done.23
  241.4 1.6 collective-permute-start.25
  243.1 1.9 collective-permute-start.24
  244.9 3.3 shard_map.80
  248.3 13.7 %collective-permute-done.25 = bf16[2,512,512]{2,1,0:T(8,128)(2,1)S(1)} collective-permute-done((bf16[2,512,512]{2,1,0:T(8,128)(2,1)S(1)}, bf16[2,512,512]{2,1,0:T(8,128)(2,1)S(1)}, u32[]{:S(2)}, u32[]{:S(2)}) %collective-permute-start.25) | collective-permute-done | bytes 1048608 | tf_op jit(solution)/shard_map/ppermute | solution.py:693
  263.1 1.9 copy-done.35
  265.9 4.4 %collective-permute-done.26.other_ref = bf16[4,1024,512]{2,1,0:T(8,128)(2,1)} collective-permute-done((bf16[4,1024,512]{2,1,0:T(8,128)(2,1)S(1)}, bf16[4,1024,512]{2,1,0:T(8,128)(2,1)}, u32[]{:S(2)}, u32[]{:S(2)}) %collective-permute-start.26) | collective-permute-done | bytes 4194336 | tf_op jit(solution)/shard_map/ppermute | solution.py:693
  270.3 9.9 %shard_map.81 = bf16[4,584,1024]{2,1,0:T(8,128)(2,1)} custom-call(s32[3]{0:T(128)} %pad_add_fusion.p, bf16[512,1024]{1,0:T(8,128)(2,1)} %get-tuple-element.168.h_ref, bf16[4,1024,512]{2,1,0:T(8,128)(2,1)} %copy-done.35, bf16[4,1024,512]{2,1,0:T(8,128)(2,1)} %collective-permute-done.26.other_ref, bf16[4,72,1024]{2,1,0:T(8,128)(2,1)} %pad_maximum_fusion.6.refs_0_), custom_call_target="tpu_custom_call" | custom-call | flops 4294967296 | bytes 13631488 | tf_op jit(solution)/shard_map/pallas_call | solution.py:569
  280.2 6.3 %reduce-scatter.3.cloned.1.call-done.last_ref = bf16[1,512,1024]{2,1,0:T(8,128)(2,1)} async-done(((bf16[4,512,1024]{2,1,0:T(8,128)(2,1)}), bf16[1,512,1024]{2,1,0:T(8,128)(2,1)}) %reduce-scatter.3.cloned.1.call-update) | async-done | bytes 1048592 | tf_op jit(solution)/shard_map/reduce_scatter | solution.py:851
  286.6 12.7 %shard_map.82.gp_ref = bf16[1024,512]{1,0:T(8,128)(2,1)} custom-call(s32[3]{0:T(128)} %pad_add_fusion.p, f32[1024,512]{1,0:T(8,128)} %get-tuple-element.173.s_ref, bf16[4,1024,512]{2,1,0:T(8,128)(2,1)} %copy-done.35, bf16[4,1024,512]{2,1,0:T(8,128)(2,1)} %collective-permute-done.26.other_ref, bf16[592,1024]{1,0:T(8,128)(2,1)} %copy-done.36, ...), custom_call_target="tpu_custom_call" | custom-call | flops 4294967296 | bytes 16777216 | tf_op jit(solution)/shard_map/pallas_call | solution.py:534
  300.6 3.4 shard_map.83.refs_0_
  304.1 8.9 %shard_map.84 = (bf16[4,1024,512]{2,1,0:T(8,128)(2,1)}, bf16[4,1024,512]{2,1,0:T(8,128)(2,1)}) custom-call(s32[3]{0:T(128)S(1)} %copy-done.18, bf16[1024,512]{1,0:T(8,128)(2,1)} %get-tuple-element.176.h_ref, bf16[336,1024]{1,0:T(8,128)(2,1)S(1)} %copy-done.13, bf16[336,1024]{1,0:T(8,128)(2,1)S(1)} %copy-done.21, ...), custom_call_target="tpu_custom_call" | custom-call | flops 4294967296 | bytes 16777216 | tf_op jit(solution)/shard_map/pallas_call | solution.py:496
  313.0 7.4 %collective-permute-done.27 = bf16[4,1024,512]{2,1,0:T(8,128)(2,1)S(1)} collective-permute-done((bf16[4,1024,512]{2,1,0:T(8,128)(2,1)}, bf16[4,1024,512]{2,1,0:T(8,128)(2,1)S(1)}, u32[]{:S(2)}, u32[]{:S(2)}) %collective-permute-start.27) | collective-permute-done | bytes 4194336 | tf_op jit(solution)/shard_map/ppermute | solution.py:693
  320.4 2.1 add_convert_fusion.3
  325.6 1.6 collective-permute-start.30
  327.2 1.7 collective-permute-start.31
  330.3 3.1 shard_map.85
  333.5 7.7 %collective-permute-done.30.refs_1_ = bf16[144,512]{1,0:T(8,128)(2,1)S(1)} collective-permute-done((bf16[144,512]{1,0:T(8,128)(2,1)S(1)}, bf16[144,512]{1,0:T(8,128)(2,1)S(1)}, u32[]{:S(2)}, u32[]{:S(2)}) %collective-permute-start.30) | collective-permute-done | bytes 147488 | tf_op jit(solution)/shard_map/ppermute | solution.py:689
  341.2 9.7 %collective-permute-done.31.refs_2_ = bf16[144,512]{1,0:T(8,128)(2,1)S(1)} collective-permute-done((bf16[144,512]{1,0:T(8,128)(2,1)S(1)}, bf16[144,512]{1,0:T(8,128)(2,1)S(1)}, u32[]{:S(2)}, u32[]{:S(2)}) %collective-permute-start.31) | collective-permute-done | bytes 147488 | tf_op jit(solution)/shard_map/ppermute | solution.py:689
  352.2 11.5 %collective-permute-done.33 = bf16[512,512]{1,0:T(8,128)(2,1)S(1)} collective-permute-done((bf16[512,512]{1,0:T(8,128)(2,1)S(1)}, bf16[512,512]{1,0:T(8,128)(2,1)S(1)}, u32[]{:S(2)}, u32[]{:S(2)}) %collective-permute-start.33) | collective-permute-done | bytes 524320 | tf_op jit(solution)/shard_map/ppermute | solution.py:693
  364.7 2.5 copy_bitcast_fusion
  367.2 18.2 %reduce-scatter.5.cloned.1.call-done.first_ref = bf16[1,584,1024]{2,1,0:T(8,128)(2,1)} async-done(((bf16[4,584,1024]{2,1,0:T(8,128)(2,1)}), bf16[1,584,1024]{2,1,0:T(8,128)(2,1)}) %reduce-scatter.5.cloned.1.call-update) | async-done | bytes 1196048 | tf_op jit(solution)/shard_map/reduce_scatter | solution.py:866
  386.6 3.0 shard_map.86
  (169 shorter events, 37.3 us)
Async XLA Ops:
  7.2 182.4 %all-gather.3.cloned.1.call-start = ((), (), s32[]{:S(2)}) async-start(), calls=%async_computation.4 | async-start | bytes 9437184 | tf_op jit(solution)/shard_map/all_gather | solution.py:813
  9.7 35.2 %collective-permute-start = (bf16[592,1024]{1,0:T(8,128)(2,1)S(1)}, bf16[592,1024]{1,0:T(8,128)(2,1)}, u32[]{:S(2)}, u32[]{:S(2)}) collective-permute-start(bf16[592,1024]{1,0:T(8,128)(2,1)S(1)} %maximum_maximum_fusion.own.refs_0_), channel_id=1, source_target_pairs={{0,8},{8,0},{16,24},{24,16},{1,9},{9,1},{17,25},{25,17},{2,10},{10... | collective-permute-start | bytes 3637256 | tf_op jit(solution)/shard_map/ppermute | solution.py:689
  12.8 32.1 %collective-permute-start.1 = (bf16[592,1024]{1,0:T(8,128)(2,1)S(1)}, bf16[592,1024]{1,0:T(8,128)(2,1)S(1)}, u32[]{:S(2)}, u32[]{:S(2)}) collective-permute-start(bf16[592,1024]{1,0:T(8,128)(2,1)S(1)} %maximum_maximum_fusion.own.refs_0_), channel_id=1, source_target_pairs={{8,16},{16,8},{9,17},{17,9},{10,18},{18,10},{11,19},{19,11},{12,20... | collective-permute-start | bytes 3637256 | tf_op jit(solution)/shard_map/ppermute | solution.py:689
  13.6 31.4 %collective-permute-start.2 = (bf16[144,512]{1,0:T(8,128)(2,1)S(1)}, bf16[144,512]{1,0:T(8,128)(2,1)S(1)}, u32[]{:S(2)}, u32[]{:S(2)}) collective-permute-start(bf16[144,512]{1,0:T(8,128)(2,1)S(1)} %slice_bitcast_fusion.12), channel_id=1, source_target_pairs={{0,24},{24,0},{1,25},{25,1},{2,26},{26,2},{3,27},{27,3},{4,28},{28... | collective-permute-start | bytes 442376 | tf_op jit(solution)/shard_map/ppermute | solution.py:689
  44.9 32.8 %copy-start.46 = (bf16[144,512]{1,0:T(8,128)(2,1)}, bf16[144,512]{1,0:T(8,128)(2,1)S(1)}, u32[]{:S(2)}) copy-start(bf16[144,512]{1,0:T(8,128)(2,1)S(1)} %collective-permute-done.2.far_ref) | copy-start | bytes 442372
  44.9 36.4 %copy-start.2 = (bf16[592,1024]{1,0:T(8,128)(2,1)}, bf16[592,1024]{1,0:T(8,128)(2,1)S(1)}, u32[]{:S(2)}) copy-start(bf16[592,1024]{1,0:T(8,128)(2,1)S(1)} %collective-permute-done.1.b.b_ref.refs_2_) | copy-start | bytes 3637252
  45.0 241.6 %reduce-scatter.3.cloned.1.call-start = ((), (), s32[]{:S(2)}) async-start(), calls=%async_computation.2 | async-start | bytes 5242880 | tf_op jit(solution)/shard_map/reduce_scatter | solution.py:851
  45.0 2.0 collective-permute-start.3
  45.8 31.9 %collective-permute-start.4 = (bf16[592,1024]{1,0:T(8,128)(2,1)S(1)}, bf16[592,1024]{1,0:T(8,128)(2,1)}, u32[]{:S(2)}, u32[]{:S(2)}) collective-permute-start(bf16[592,1024]{1,0:T(8,128)(2,1)S(1)} %collective-permute-done.1.b.b_ref.refs_2_), channel_id=1, source_target_pairs={{8,0},{16,24},{9,1},{17,25},{10,2},{18,26},{11,3},{19,27},{12,4},{... | collective-permute-start | bytes 3637256 | tf_op jit(solution)/shard_map/ppermute | solution.py:689
  47.1 34.2 %copy-start.37 = (bf16[592,1024]{1,0:T(8,128)(2,1)}, bf16[592,1024]{1,0:T(8,128)(2,1)S(1)}, u32[]{:S(2)}) copy-start(bf16[592,1024]{1,0:T(8,128)(2,1)S(1)} %collective-permute-done.3.c.refs_3_) | copy-start | bytes 3637252
  78.7 24.9 %collective-permute-start.5 = (bf16[512,1024]{1,0:T(8,128)(2,1)}, bf16[512,1024]{1,0:T(8,128)(2,1)S(1)}, u32[]{:S(2)}, u32[]{:S(2)}) collective-permute-start(bf16[512,1024]{1,0:T(8,128)(2,1)} %slice.162), channel_id=1, source_target_pairs={{8,0},{16,24},{9,1},{17,25},{10,2},{18,26},{11,3},{19,27},{12,4},{... | collective-permute-start | bytes 3145736 | tf_op jit(solution)/shard_map/ppermute | solution.py:689
  81.3 58.6 %copy-start.14 = (bf16[256,1024]{1,0:T(8,128)(2,1)}, bf16[256,1024]{1,0:T(8,128)(2,1)S(1)}, u32[]{:S(2)}) copy-start(bf16[256,1024]{1,0:T(8,128)(2,1)S(1)} %get-tuple-element.125.refs_6_) | copy-start | bytes 1572868
  81.4 26.2 %copy-start.12 = (bf16[336,1024]{1,0:T(8,128)(2,1)}, bf16[336,1024]{1,0:T(8,128)(2,1)S(1)}, u32[]{:S(2)}) copy-start(bf16[336,1024]{1,0:T(8,128)(2,1)S(1)} %maximum_maximum_fusion.1.refs_0_) | copy-start | bytes 2064388
  81.4 16.4 %collective-permute-start.6 = (bf16[336,1024]{1,0:T(8,128)(2,1)S(1)}, bf16[336,1024]{1,0:T(8,128)(2,1)}, u32[]{:S(2)}, u32[]{:S(2)}) collective-permute-start(bf16[336,1024]{1,0:T(8,128)(2,1)S(1)} %maximum_maximum_fusion.1.refs_0_), channel_id=1, source_target_pairs={{8,16},{16,8},{9,17},{17,9},{10,18},{18,10},{11,19},{19,11},{12,20... | collective-permute-start | bytes 2064392 | tf_op jit(solution)/shard_map/ppermute | solution.py:689
  83.6 14.1 %collective-permute-start.7 = (bf16[256,1024]{1,0:T(8,128)(2,1)S(1)}, bf16[256,1024]{1,0:T(8,128)(2,1)}, u32[]{:S(2)}, u32[]{:S(2)}) collective-permute-start(bf16[256,1024]{1,0:T(8,128)(2,1)S(1)} %get-tuple-element.125.refs_6_), channel_id=1, source_target_pairs={{8,16},{16,8},{9,17},{17,9},{10,18},{18,10},{11,19},{19,11},{12,20... | collective-permute-start | bytes 1572872 | tf_op jit(solution)/shard_map/ppermute | solution.py:689
  97.8 34.4 %copy-start.1 = (bf16[3,1024,512]{2,1,0:T(8,128)(2,1)S(1)}, bf16[3,1024,512]{2,1,0:T(8,128)(2,1)}, u32[]{:S(2)}) copy-start(bf16[3,1024,512]{2,1,0:T(8,128)(2,1)} %get-tuple-element.126.k_ref) | copy-start | bytes 9437188
  103.6 31.2 %copy-start.9 = (bf16[512,1024]{1,0:T(8,128)(2,1)}, bf16[512,1024]{1,0:T(8,128)(2,1)S(1)}, u32[]{:S(2)}) copy-start(bf16[512,1024]{1,0:T(8,128)(2,1)S(1)} %collective-permute-done.5.e_ref.refs_5_) | copy-start | bytes 3145732
  103.6 28.5 %collective-permute-start.9 = (bf16[3,1024,512]{2,1,0:T(8,128)(2,1)}, bf16[3,1024,512]{2,1,0:T(8,128)(2,1)S(1)}, u32[]{:S(2)}, u32[]{:S(2)}) collective-permute-start(bf16[3,1024,512]{2,1,0:T(8,128)(2,1)} %get-tuple-element.117), channel_id=1, source_target_pairs={{0,1},{1,0},{2,3},{3,2},{4,5},{5,4},{6,7},{7,6},{8,9},{9,8},{10,11... | collective-permute-start | bytes 9437192 | tf_op jit(solution)/shard_map/ppermute | solution.py:693
  107.4 24.7 %collective-permute-start.10 = (bf16[1,1024,512]{2,1,0:T(8,128)(2,1)S(1)}, bf16[1,1024,512]{2,1,0:T(8,128)(2,1)S(1)}, u32[]{:S(2)}, u32[]{:S(2)}) collective-permute-start(bf16[1,1024,512]{2,1,0:T(8,128)(2,1)S(1)} %get-tuple-element.121), channel_id=1, source_target_pairs={{0,1},{1,0},{2,3},{3,2},{4,5},{5,4},{6,7},{7,6},{8,9},{9,8},{10,11... | collective-permute-start | bytes 3145736 | tf_op jit(solution)/shard_map/ppermute | solution.py:693
  107.6 24.5 %collective-permute-start.8 = (bf16[336,1024]{1,0:T(8,128)(2,1)S(1)}, bf16[336,1024]{1,0:T(8,128)(2,1)S(1)}, u32[]{:S(2)}, u32[]{:S(2)}) collective-permute-start(bf16[336,1024]{1,0:T(8,128)(2,1)S(1)} %maximum_maximum_fusion.1.refs_0_), channel_id=1, source_target_pairs={{0,8},{8,0},{16,24},{24,16},{1,9},{9,1},{17,25},{25,17},{2,10},{10... | collective-permute-start | bytes 2064392 | tf_op jit(solution)/shard_map/ppermute | solution.py:689
  134.8 35.3 %copy-start.19 = (f32[1024,512]{1,0:T(8,128)}, f32[1024,512]{1,0:T(8,128)S(1)}, u32[]{:S(2)}) copy-start(f32[1024,512]{1,0:T(8,128)S(1)} %get-tuple-element.140.n_ref) | copy-start | bytes 6291460
  134.8 33.0 %collective-permute-start.14 = (bf16[2,512,512]{2,1,0:T(8,128)(2,1)S(1)}, bf16[2,512,512]{2,1,0:T(8,128)(2,1)S(1)}, u32[]{:S(2)}, u32[]{:S(2)}) collective-permute-start(bf16[2,512,512]{2,1,0:T(8,128)(2,1)S(1)} %get-tuple-element.130), channel_id=1, source_target_pairs={{0,2},{1,3},{2,0},{3,1},{4,6},{5,7},{6,4},{7,5},{8,10},{9,11},{10,... | collective-permute-start | bytes 3145736 | tf_op jit(solution)/shard_map/ppermute | solution.py:693
  136.3 31.5 %collective-permute-start.15 = (bf16[2,512,512]{2,1,0:T(8,128)(2,1)S(1)}, bf16[2,512,512]{2,1,0:T(8,128)(2,1)S(1)}, u32[]{:S(2)}, u32[]{:S(2)}) collective-permute-start(bf16[2,512,512]{2,1,0:T(8,128)(2,1)S(1)} %get-tuple-element.131), channel_id=1, source_target_pairs={{0,4},{1,5},{2,6},{3,7},{4,0},{5,1},{6,2},{7,3},{8,12},{9,13},{10,... | collective-permute-start | bytes 3145736 | tf_op jit(solution)/shard_map/ppermute | solution.py:693
  137.9 20.5 %collective-permute-start.12 = (bf16[336,1024]{1,0:T(8,128)(2,1)}, bf16[336,1024]{1,0:T(8,128)(2,1)S(1)}, u32[]{:S(2)}, u32[]{:S(2)}) collective-permute-start(bf16[336,1024]{1,0:T(8,128)(2,1)} %collective-permute-done.6.refs_2_), channel_id=1, source_target_pairs={{8,0},{16,24},{9,1},{17,25},{10,2},{18,26},{11,3},{19,27},{12,4},{... | collective-permute-start | bytes 2064392 | tf_op jit(solution)/shard_map/ppermute | solution.py:689
  139.2 28.6 %collective-permute-start.11 = (bf16[336,1024]{1,0:T(8,128)(2,1)S(1)}, bf16[336,1024]{1,0:T(8,128)(2,1)S(1)}, u32[]{:S(2)}, u32[]{:S(2)}) collective-permute-start(bf16[336,1024]{1,0:T(8,128)(2,1)S(1)} %collective-permute-done.8.refs_1_), channel_id=1, source_target_pairs={{8,16},{16,8},{9,17},{17,9},{10,18},{18,10},{11,19},{19,11},{12,20... | collective-permute-start | bytes 2064392 | tf_op jit(solution)/shard_map/ppermute | solution.py:689
  139.9 27.9 %collective-permute-start.13 = (bf16[256,1024]{1,0:T(8,128)(2,1)S(1)}, bf16[256,1024]{1,0:T(8,128)(2,1)S(1)}, u32[]{:S(2)}, u32[]{:S(2)}) collective-permute-start(bf16[256,1024]{1,0:T(8,128)(2,1)S(1)} %get-tuple-element.125.refs_6_), channel_id=1, source_target_pairs={{0,8},{8,0},{16,24},{24,16},{1,9},{9,1},{17,25},{25,17},{2,10},{10... | collective-permute-start | bytes 1572872 | tf_op jit(solution)/shard_map/ppermute | solution.py:689
  168.0 12.2 %collective-permute-start.16 = (bf16[512,512]{1,0:T(8,128)(2,1)S(1)}, bf16[512,512]{1,0:T(8,128)(2,1)S(1)}, u32[]{:S(2)}, u32[]{:S(2)}) collective-permute-start(bf16[512,512]{1,0:T(8,128)(2,1)S(1)} %fusion.1), channel_id=1, source_target_pairs={{0,4},{1,5},{2,6},{3,7},{4,0},{5,1},{6,2},{7,3},{8,12},{9,13},{10,... | collective-permute-start | bytes 1572872 | tf_op jit(solution)/shard_map/ppermute | solution.py:693
  168.6 17.3 %collective-permute-start.18 = (bf16[336,1024]{1,0:T(8,128)(2,1)S(1)}, bf16[336,1024]{1,0:T(8,128)(2,1)S(1)}, u32[]{:S(2)}, u32[]{:S(2)}) collective-permute-start(bf16[336,1024]{1,0:T(8,128)(2,1)S(1)} %collective-permute-done.11.refs_3_), channel_id=1, source_target_pairs={{8,0},{16,24},{9,1},{17,25},{10,2},{18,26},{11,3},{19,27},{12,4},{... | collective-permute-start | bytes 2064392 | tf_op jit(solution)/shard_map/ppermute | solution.py:689
  170.1 12.0 %collective-permute-start.17 = (bf16[512,512]{1,0:T(8,128)(2,1)S(1)}, bf16[512,512]{1,0:T(8,128)(2,1)S(1)}, u32[]{:S(2)}, u32[]{:S(2)}) collective-permute-start(bf16[512,512]{1,0:T(8,128)(2,1)S(1)} %fusion), channel_id=1, source_target_pairs={{0,2},{1,3},{2,0},{3,1},{4,6},{5,7},{6,4},{7,5},{8,10},{9,11},{10,... | collective-permute-start | bytes 1572872 | tf_op jit(solution)/shard_map/ppermute | solution.py:693
  170.7 11.4 %collective-permute-start.19 = (bf16[256,1024]{1,0:T(8,128)(2,1)S(1)}, bf16[256,1024]{1,0:T(8,128)(2,1)S(1)}, u32[]{:S(2)}, u32[]{:S(2)}) collective-permute-start(bf16[256,1024]{1,0:T(8,128)(2,1)S(1)} %collective-permute-done.13.refs_7_), channel_id=1, source_target_pairs={{8,16},{16,8},{9,17},{17,9},{10,18},{18,10},{11,19},{19,11},{12,20... | collective-permute-start | bytes 1572872 | tf_op jit(solution)/shard_map/ppermute | solution.py:689
  182.0 22.2 %copy-start.26 = (bf16[256,1024]{1,0:T(8,128)(2,1)}, bf16[256,1024]{1,0:T(8,128)(2,1)S(1)}, u32[]{:S(2)}) copy-start(bf16[256,1024]{1,0:T(8,128)(2,1)S(1)} %collective-permute-done.19.refs_9_) | copy-start | bytes 1572868
  186.7 17.5 %collective-permute-start.20 = (bf16[256,1024]{1,0:T(8,128)(2,1)}, bf16[256,1024]{1,0:T(8,128)(2,1)S(1)}, u32[]{:S(2)}, u32[]{:S(2)}) collective-permute-start(bf16[256,1024]{1,0:T(8,128)(2,1)} %collective-permute-done.7.refs_8_), channel_id=1, source_target_pairs={{8,0},{16,24},{9,1},{17,25},{10,2},{18,26},{11,3},{19,27},{12,4},{... | collective-permute-start | bytes 1572872 | tf_op jit(solution)/shard_map/ppermute | solution.py:689
  188.0 23.0 %collective-permute-start.21 = (bf16[256,1024]{1,0:T(8,128)(2,1)S(1)}, bf16[256,1024]{1,0:T(8,128)(2,1)S(1)}, u32[]{:S(2)}, u32[]{:S(2)}) collective-permute-start(bf16[256,1024]{1,0:T(8,128)(2,1)S(1)} %collective-permute-done.19.refs_9_), channel_id=1, source_target_pairs={{8,0},{16,24},{9,1},{17,25},{10,2},{18,26},{11,3},{19,27},{12,4},{... | collective-permute-start | bytes 1572872 | tf_op jit(solution)/shard_map/ppermute | solution.py:689
  211.8 173.5 %reduce-scatter.5.cloned.1.call-start = ((), (), s32[]{:S(2)}) async-start(), calls=%async_computation.3 | async-start | bytes 5980160 | tf_op jit(solution)/shard_map/reduce_scatter | solution.py:866
  229.3 9.8 %collective-permute-start.22 = (bf16[512,512]{1,0:T(8,128)(2,1)S(1)}, bf16[512,512]{1,0:T(8,128)(2,1)S(1)}, u32[]{:S(2)}, u32[]{:S(2)}) collective-permute-start(bf16[512,512]{1,0:T(8,128)(2,1)S(1)} %get-tuple-element.211), channel_id=1, source_target_pairs={{0,2},{1,3},{2,0},{3,1},{4,6},{5,7},{6,4},{7,5},{8,10},{9,11},{10,... | collective-permute-start | bytes 1572872 | tf_op jit(solution)/shard_map/ppermute | solution.py:693
  229.4 11.8 %collective-permute-start.23 = (bf16[512,512]{1,0:T(8,128)(2,1)S(1)}, bf16[512,512]{1,0:T(8,128)(2,1)S(1)}, u32[]{:S(2)}, u32[]{:S(2)}) collective-permute-start(bf16[512,512]{1,0:T(8,128)(2,1)S(1)} %get-tuple-element.210), channel_id=1, source_target_pairs={{0,4},{1,5},{2,6},{3,7},{4,0},{5,1},{6,2},{7,3},{8,12},{9,13},{10,... | collective-permute-start | bytes 1572872 | tf_op jit(solution)/shard_map/ppermute | solution.py:693
  241.4 20.6 %collective-permute-start.25 = (bf16[2,512,512]{2,1,0:T(8,128)(2,1)S(1)}, bf16[2,512,512]{2,1,0:T(8,128)(2,1)S(1)}, u32[]{:S(2)}, u32[]{:S(2)}) collective-permute-start(bf16[2,512,512]{2,1,0:T(8,128)(2,1)S(1)} %pad_maximum_fusion.2), channel_id=1, source_target_pairs={{0,4},{1,5},{2,6},{3,7},{4,0},{5,1},{6,2},{7,3},{8,12},{9,13},{10,... | collective-permute-start | bytes 3145736 | tf_op jit(solution)/shard_map/ppermute | solution.py:693
  243.1 19.1 %collective-permute-start.24 = (bf16[2,512,512]{2,1,0:T(8,128)(2,1)S(1)}, bf16[2,512,512]{2,1,0:T(8,128)(2,1)S(1)}, u32[]{:S(2)}, u32[]{:S(2)}) collective-permute-start(bf16[2,512,512]{2,1,0:T(8,128)(2,1)S(1)} %pad_maximum_fusion.1), channel_id=1, source_target_pairs={{0,2},{1,3},{2,0},{3,1},{4,6},{5,7},{6,4},{7,5},{8,10},{9,11},{10,... | collective-permute-start | bytes 3145736 | tf_op jit(solution)/shard_map/ppermute | solution.py:693
  263.0 7.4 %collective-permute-start.26 = (bf16[4,1024,512]{2,1,0:T(8,128)(2,1)S(1)}, bf16[4,1024,512]{2,1,0:T(8,128)(2,1)}, u32[]{:S(2)}, u32[]{:S(2)}) collective-permute-start(bf16[4,1024,512]{2,1,0:T(8,128)(2,1)S(1)} %pad_maximum_fusion.mine_ref), channel_id=1, source_target_pairs={{0,1},{1,0},{2,3},{3,2},{4,5},{5,4},{6,7},{7,6},{8,9},{9,8},{10,11... | collective-permute-start | bytes 12582920 | tf_op jit(solution)/shard_map/ppermute | solution.py:693
  313.0 7.4 %collective-permute-start.27 = (bf16[4,1024,512]{2,1,0:T(8,128)(2,1)}, bf16[4,1024,512]{2,1,0:T(8,128)(2,1)S(1)}, u32[]{:S(2)}, u32[]{:S(2)}) collective-permute-start(bf16[4,1024,512]{2,1,0:T(8,128)(2,1)} %get-tuple-element.178), channel_id=1, source_target_pairs={{0,1},{1,0},{2,3},{3,2},{4,5},{5,4},{6,7},{7,6},{8,9},{9,8},{10,11... | collective-permute-start | bytes 12582920 | tf_op jit(solution)/shard_map/ppermute | solution.py:693
  322.6 28.3 %collective-permute-start.28 = (bf16[2,512,512]{2,1,0:T(8,128)(2,1)S(1)}, bf16[2,512,512]{2,1,0:T(8,128)(2,1)S(1)}, u32[]{:S(2)}, u32[]{:S(2)}) collective-permute-start(bf16[2,512,512]{2,1,0:T(8,128)(2,1)S(1)} %pad_maximum_fusion.3), channel_id=1, source_target_pairs={{0,2},{1,3},{2,0},{3,1},{4,6},{5,7},{6,4},{7,5},{8,10},{9,11},{10,... | collective-permute-start | bytes 3145736 | tf_op jit(solution)/shard_map/ppermute | solution.py:693
  324.1 26.8 %collective-permute-start.29 = (bf16[2,512,512]{2,1,0:T(8,128)(2,1)S(1)}, bf16[2,512,512]{2,1,0:T(8,128)(2,1)S(1)}, u32[]{:S(2)}, u32[]{:S(2)}) collective-permute-start(bf16[2,512,512]{2,1,0:T(8,128)(2,1)S(1)} %pad_maximum_fusion.4), channel_id=1, source_target_pairs={{0,4},{1,5},{2,6},{3,7},{4,0},{5,1},{6,2},{7,3},{8,12},{9,13},{10,... | collective-permute-start | bytes 3145736 | tf_op jit(solution)/shard_map/ppermute | solution.py:693
  325.6 15.6 %collective-permute-start.30 = (bf16[144,512]{1,0:T(8,128)(2,1)S(1)}, bf16[144,512]{1,0:T(8,128)(2,1)S(1)}, u32[]{:S(2)}, u32[]{:S(2)}) collective-permute-start(bf16[144,512]{1,0:T(8,128)(2,1)S(1)} %get-tuple-element.214), channel_id=1, source_target_pairs={{0,8},{8,0},{16,24},{24,16},{1,9},{9,1},{17,25},{25,17},{2,10},{10... | collective-permute-start | bytes 442376 | tf_op jit(solution)/shard_map/ppermute | solution.py:689
  327.2 23.7 %collective-permute-start.31 = (bf16[144,512]{1,0:T(8,128)(2,1)S(1)}, bf16[144,512]{1,0:T(8,128)(2,1)S(1)}, u32[]{:S(2)}, u32[]{:S(2)}) collective-permute-start(bf16[144,512]{1,0:T(8,128)(2,1)S(1)} %get-tuple-element.213), channel_id=1, source_target_pairs={{0,16},{8,24},{16,0},{24,8},{1,17},{9,25},{17,1},{25,9},{2,18},{10... | collective-permute-start | bytes 442376 | tf_op jit(solution)/shard_map/ppermute | solution.py:689
  328.9 22.0 %collective-permute-start.32 = (bf16[144,512]{1,0:T(8,128)(2,1)S(1)}, bf16[144,512]{1,0:T(8,128)(2,1)S(1)}, u32[]{:S(2)}, u32[]{:S(2)}) collective-permute-start(bf16[144,512]{1,0:T(8,128)(2,1)S(1)} %get-tuple-element.212), channel_id=1, source_target_pairs={{0,24},{8,16},{16,8},{24,0},{1,25},{9,17},{17,9},{25,1},{2,26},{10... | collective-permute-start | bytes 442376 | tf_op jit(solution)/shard_map/ppermute | solution.py:689
  333.5 30.4 %copy-start.8 = (bf16[1024,512]{1,0:T(8,128)(2,1)S(1)}, bf16[1024,512]{1,0:T(8,128)(2,1)}, u32[]{:S(2)}) copy-start(bf16[1024,512]{1,0:T(8,128)(2,1)} %get-tuple-element.154.x_ref) | copy-start | bytes 3145732
  351.4 12.3 %collective-permute-start.33 = (bf16[512,512]{1,0:T(8,128)(2,1)S(1)}, bf16[512,512]{1,0:T(8,128)(2,1)S(1)}, u32[]{:S(2)}, u32[]{:S(2)}) collective-permute-start(bf16[512,512]{1,0:T(8,128)(2,1)S(1)} %get-tuple-element.196), channel_id=1, source_target_pairs={{0,4},{1,5},{2,6},{3,7},{4,0},{5,1},{6,2},{7,3},{8,12},{9,13},{10,... | collective-permute-start | bytes 1572872 | tf_op jit(solution)/shard_map/ppermute | solution.py:693
  351.6 12.3 %collective-permute-start.34 = (bf16[512,512]{1,0:T(8,128)(2,1)S(1)}, bf16[512,512]{1,0:T(8,128)(2,1)S(1)}, u32[]{:S(2)}, u32[]{:S(2)}) collective-permute-start(bf16[512,512]{1,0:T(8,128)(2,1)S(1)} %get-tuple-element.197), channel_id=1, source_target_pairs={{0,2},{1,3},{2,0},{3,1},{4,6},{5,7},{6,4},{7,5},{8,10},{9,11},{10,... | collective-permute-start | bytes 1572872 | tf_op jit(solution)/shard_map/ppermute | solution.py:693
  (37 other events, 271.2 us)
Sparse Core Ops, SparseCore 0:
  45.1 55.6 all-gather.2
  211.2 75.3 reduce-scatter.2
  289.0 96.2 reduce-scatter.4
